TPU v7x, 32 devices: a whole 2x2x4 slice. The times are simulated.
32 devices in a mesh: dp: 16 (over z, y, core), centre: 2 (over x).
Axes of the slice: x: 2, y: 2, z: 4, core: 2. Of those that a mesh axis runs over, the one named last changes fastest.
Arguments:
- samples: float32 [8192, 512], P('dp'), may hold values from -4 to 4
- targets: float32 [8192, 64], P('dp'), may hold values from -6 to 6
- centres: float32 [4096, 512], P('centre'), may hold values from -4 to 4
- coefficients: float32 [4096, 64], P('centre'), may hold values from -0.9 to 0.9
Outputs:
- residual: float32 [8192, 64], P('dp')
- new_coefficients: float32 [4096, 64], P(('centre', 'dp'))
All inputs are finite; a program needn't handle non-finite values.
Results may differ from a plain program's by a relative error of at most 0.0001.
Values sent between devices are 32-bit elements; how exact they have to be, the bound alone decides.
No kernel may reach another device: no remote copies, remote signals or barrier semaphores. Data moves between devices by JAX's collectives and lax.ppermute only.
A program may use at most 128 MiB of HBM per device.

v0:
```python
import jax
import jax.numpy as jnp
from jax import lax
from jax.sharding import PartitionSpec as P

softening = 0.01
kernel_scale = 0.2
learning_rate = 4.0


def kernel_block(left, right):
    cross = lax.dot_general(
        left,
        right,
        (((1,), (1,)), ((), ())),
        precision=lax.Precision.HIGHEST,
        preferred_element_type=jnp.float32,
    )
    left_sq = jnp.sum(left * left, axis=1)
    right_sq = jnp.sum(right * right, axis=1)
    dist_sq = jnp.maximum(left_sq[:, None] + right_sq[None, :] - 2.0 * cross, 0.0)
    return jnp.exp(-jnp.sqrt(dist_sq + softening) / kernel_scale)


def matmul(left, right):
    return jnp.dot(left, right, precision=lax.Precision.HIGHEST, preferred_element_type=jnp.float32)


def spread(theta_own):
    return lax.all_gather(theta_own, "dp", axis=0, tiled=True)


def body(samples, targets, centres, coefficients):
    dp_count = lax.axis_size("dp")
    dp_index = lax.axis_index("dp")
    share_rows = centres.shape[0] // dp_count
    data_tile = kernel_block(samples, centres)
    partial_pred = matmul(data_tile, coefficients)
    predictions = lax.psum(partial_pred, "centre")
    residual = predictions - targets
    partial_grad = lax.dot_general(
        data_tile,
        residual,
        (((0,), (0,)), ((), ())),
        precision=lax.Precision.HIGHEST,
        preferred_element_type=jnp.float32,
    )
    grad_own = lax.psum_scatter(partial_grad, "dp", scatter_dimension=0, tiled=True)
    start_full = spread(grad_own)
    own_centres = lax.dynamic_slice_in_dim(centres, dp_index * share_rows, share_rows, 0)
    row_centres = lax.all_gather(own_centres, "centre", axis=0, tiled=True)
    square = kernel_block(row_centres, centres)
    row_part = jnp.sum(square, axis=1)

    def project(gathered):
        return lax.psum_scatter(matmul(square, gathered), "centre", scatter_dimension=0, tiled=True)

    row_sums = lax.psum(row_part, "centre")
    largest = lax.pmax(jnp.max(row_sums), "dp")
    step_size = 1.0 / largest
    image = project(step_size * start_full)
    theta = step_size * grad_own
    theta = theta + step_size * (grad_own - image)
    image = project(spread(theta))
    theta = theta + step_size * (grad_own - image)
    own_coeffs = lax.dynamic_slice_in_dim(coefficients, dp_index * share_rows, share_rows, 0)
    return (residual, own_coeffs - learning_rate * theta)


def solution(mesh):
    return jax.shard_map(
        body,
        mesh=mesh,
        in_specs=(P("dp", None), P("dp", None), P("centre", None), P("centre", None)),
        out_specs=(P("dp", None), P(("centre", "dp"), None)),
        check_vma=False,
    )
```

profile of v0, /device:TPU:0, one launch (start us, length us, event | category | flops | bytes accessed | tf_op | source)
XLA Modules:
  0.0 185.3 jit_solution(13473866344640113006)
XLA Ops:
  7.2 2.7 %multiply_reduce_fusion = f32[2048]{0:T(1024)S(1)} fusion(f32[2048,512]{1,0:T(8,128)} %param.6), kind=kLoop, calls=%fused_computation.1 | loop fusion | flops 2095104 | bytes 4202496 | tf_op jit(solution)/shard_map/reduce_sum | solution.py:20
  9.9 0.1 multiply_reduce_fusion.1
  10.1 0.9 copy-done
  11.0 8.5 %multiply_exponential_fusion = f32[512,2048]{1,0:T(8,128)S(1)} fusion(f32[512,512]{1,0:T(8,128)S(1)} %copy-done.2, f32[2048,512]{1,0:T(8,128)S(1)} %copy-done, f32[2048]{0:T(1024)S(1)} %multiply_reduce_fusion, f32[512]{0:T(512)S(1)} %multiply_reduce_fusion.1), kind=kOutput, calls=%fused_computation | convolution fusion | flops 6449790976 | bytes 9447424 | tf_op jit(solution)/shard_map/dot_general | solution.py:12
  19.5 1.9 %copy-done.1 = f32[512,2048]{1,0:T(8,128)} copy-done((f32[512,2048]{1,0:T(8,128)}, f32[512,2048]{1,0:T(8,128)S(1)}, u32[]{:S(2)}) %copy-start.1) | copy-done | bytes 4194328
  21.4 5.0 %fusion.12 = f32[512,64]{0,1:T(8,128)} fusion(f32[512,2048]{1,0:T(8,128)S(1)} %multiply_exponential_fusion, f32[2048,64]{0,1:T(8,128)S(1)} %copy-done.3), kind=kOutput, calls=%fused_computation.20 | convolution fusion | flops 805306368 | bytes 4849664 | tf_op jit(solution)/shard_map/dot_general | solution.py:26
  26.5 24.2 %all-reduce.2.cloned.1.call-done = f32[512,64]{0,1:T(8,128)} async-done(((f32[512,64]{0,1:T(8,128)}), f32[512,64]{0,1:T(8,128)}) %all-reduce.2.cloned.1.call-update) | async-done | bytes 131088 | tf_op jit(solution)/shard_map/psum | solution.py:39
  50.7 0.9 sub.19
  51.7 5.8 %fusion.13 = f32[2048,64]{0,1:T(8,128)} fusion(f32[512,2048]{1,0:T(8,128)} %copy-done.1, f32[512,64]{0,1:T(8,128)S(1)} %sub.19), kind=kOutput, calls=%fused_computation.21 | convolution fusion | flops 805306368 | bytes 4849664 | tf_op jit(solution)/shard_map/dot_general | solution.py:41
  57.6 1.0 constant_dynamic-slice_fusion
  58.5 8.3 %all_gather.9 = f32[256,512]{1,0:T(8,128)S(1)} all-gather(f32[128,512]{1,0:T(8,128)S(1)} %constant_dynamic-slice_fusion), channel_id=1, replica_groups=mesh['dp'=16,'centre'=2] {'centre'}, dimensions={0}, use_global_device_ids=true | all-gather | bytes 786432 | tf_op jit(solution)/shard_map/all_gather | solution.py:51
  66.9 6.4 %fusion.11 = (f32[256]{0:T(256)S(1)}, f32[256,2048]{1,0:T(8,128)S(1)}) fusion(f32[256,512]{1,0:T(8,128)S(1)} %all_gather.9, f32[2048,512]{1,0:T(8,128)} %param.6, f32[2048]{0:T(1024)S(1)} %multiply_reduce_fusion, f32[256]{0:T(256)S(1)} %multiply_reduce_fusion.2), kind=kOutput, calls=%fused_computation.19 | convolution fusion | flops 3225419520 | bytes 6825984 | tf_op jit(solution)/shard_map/dot_general | solution.py:12
  73.4 4.9 %psum.15 = f32[256]{0:T(256)S(1)} all-reduce(f32[256]{0:T(256)S(1)} %get-tuple-element.2), channel_id=1, replica_groups=mesh['dp'=16,'centre'=2] {'centre'}, use_global_device_ids=true, to_apply=%region_5.0 | all-reduce | flops 256 | bytes 2048 | tf_op jit(solution)/shard_map/psum | solution.py:58
  78.3 0.6 reduce_max.9
  78.9 31.3 %pmax.7 = f32[]{:T(128)} all-reduce(f32[]{:T(128)} %reduce_max.9), channel_id=1, replica_groups=mesh['dp'=16,'centre'=2] {'dp'}, use_global_device_ids=true, to_apply=%region_7.0 | all-reduce | flops 1 | bytes 8 | tf_op jit(solution)/shard_map/pmax | solution.py:59
  110.9 2.5 %reduce-scatter.4.cloned.1.call-done = f32[128,64]{0,1:T(8,128)} async-done(((f32[2048,64]{0,1:T(8,128)}), f32[128,64]{0,1:T(8,128)}) %reduce-scatter.4.cloned.1.call-update) | async-done | bytes 32784 | tf_op jit(solution)/shard_map/reduce_scatter | solution.py:48
  113.4 21.2 %all_gather.10 = f32[2048,64]{0,1:T(8,128)S(1)} all-gather(f32[128,64]{0,1:T(8,128)} %reduce-scatter.4.cloned.1.call-done), channel_id=1, replica_groups=mesh['dp'=16,'centre'=2] {'dp'}, dimensions={0}, use_global_device_ids=true | all-gather | bytes 557056 | tf_op jit(solution)/shard_map/all_gather | solution.py:30
  134.7 2.6 %fusion.7 = f32[256,64]{0,1:T(8,128)} fusion(f32[256,2048]{1,0:T(8,128)S(1)} %get-tuple-element.3, f32[2048,64]{0,1:T(8,128)S(1)} %all_gather.10, f32[]{:T(128)S(6)} %div.19), kind=kOutput, calls=%fused_computation.11 | convolution fusion | flops 402784256 | bytes 2686980 | tf_op jit(solution)/shard_map/dot_general | solution.py:26
  137.4 7.2 %reduce-scatter.6.cloned.1.call-done = f32[128,64]{0,1:T(8,128)} async-done(((f32[256,64]{0,1:T(8,128)}), f32[128,64]{0,1:T(8,128)}) %reduce-scatter.6.cloned.1.call-update) | async-done | bytes 32784 | tf_op jit(solution)/shard_map/reduce_scatter | solution.py:56
  144.6 0.8 fusion.10
  145.4 22.9 %all_gather.11 = f32[2048,64]{0,1:T(8,128)S(1)} all-gather(f32[128,64]{0,1:T(8,128)S(1)} %fusion.10), channel_id=1, replica_groups=mesh['dp'=16,'centre'=2] {'dp'}, dimensions={0}, use_global_device_ids=true | all-gather | bytes 557056 | tf_op jit(solution)/shard_map/all_gather | solution.py:30
  168.3 2.6 %fusion.14 = f32[256,64]{0,1:T(8,128)} fusion(f32[256,2048]{1,0:T(8,128)S(1)} %get-tuple-element.3, f32[2048,64]{0,1:T(8,128)S(1)} %all_gather.11), kind=kOutput, calls=%fused_computation.22 | convolution fusion | flops 402653184 | bytes 2686976 | tf_op jit(solution)/shard_map/dot_general | solution.py:26
  171.0 6.4 %reduce-scatter.8.cloned.1.call-done = f32[128,64]{0,1:T(8,128)} async-done(((f32[256,64]{0,1:T(8,128)}), f32[128,64]{0,1:T(8,128)}) %reduce-scatter.8.cloned.1.call-update) | async-done | bytes 32784 | tf_op jit(solution)/shard_map/reduce_scatter | solution.py:56
  177.4 1.4 multiply_subtract_fusion
  (21 shorter events, 0.4 us)
Async XLA Ops:
  7.2 2.8 %copy-start.2 = (f32[512,512]{1,0:T(8,128)S(1)}, f32[512,512]{1,0:T(8,128)}, u32[]{:S(2)}) copy-start(f32[512,512]{1,0:T(8,128)} %param.4) | copy-start | bytes 3145732
  7.2 43.6 %all-reduce.2.cloned.1.call-start = ((), (), s32[]{:S(2)}) async-start(), calls=%async_computation.3 | async-start | bytes 262144 | tf_op jit(solution)/shard_map/psum | solution.py:39
  7.2 3.7 %copy-start = (f32[2048,512]{1,0:T(8,128)S(1)}, f32[2048,512]{1,0:T(8,128)}, u32[]{:S(2)}) copy-start(f32[2048,512]{1,0:T(8,128)} %param.6) | copy-start | bytes 12582916
  11.0 10.5 %copy-start.3 = (f32[2048,64]{0,1:T(8,128)S(1)}, f32[2048,64]{0,1:T(8,128)}, u32[]{:S(2)}) copy-start(f32[2048,64]{0,1:T(8,128)} %param.7) | copy-start | bytes 1572868
  19.5 1.9 %copy-start.1 = (f32[512,2048]{1,0:T(8,128)}, f32[512,2048]{1,0:T(8,128)S(1)}, u32[]{:S(2)}) copy-start(f32[512,2048]{1,0:T(8,128)S(1)} %multiply_exponential_fusion) | copy-start | bytes 12582916
  21.4 29.3 %copy-start.6 = (f32[512,64]{0,1:T(8,128)S(1)}, f32[512,64]{0,1:T(8,128)}, u32[]{:S(2)}) copy-start(f32[512,64]{0,1:T(8,128)} %param.5) | copy-start | bytes 393220
  26.5 87.0 %reduce-scatter.4.cloned.1.call-start = ((), (), s32[]{:S(2)}) async-start(), calls=%async_computation.4 | async-start | bytes 557056 | tf_op jit(solution)/shard_map/reduce_scatter | solution.py:48
  51.7 21.7 %copy-start.4 = (f32[512,64]{0,1:T(8,128)}, f32[512,64]{0,1:T(8,128)S(1)}, u32[]{:S(2)}) copy-start(f32[512,64]{0,1:T(8,128)S(1)} %sub.19) | copy-start | bytes 393220
  57.5 87.1 %reduce-scatter.6.cloned.1.call-start = ((), (), s32[]{:S(2)}) async-start(), calls=%async_computation.5 | async-start | bytes 98304 | tf_op jit(solution)/shard_map/reduce_scatter | solution.py:56
  113.4 63.9 %copy-start.5 = (f32[128,64]{0,1:T(8,128)S(1)}, f32[128,64]{0,1:T(8,128)}, u32[]{:S(2)}) copy-start(f32[128,64]{0,1:T(8,128)} %reduce-scatter.4.cloned.1.call-done) | copy-start | bytes 98308
  137.3 40.0 %reduce-scatter.8.cloned.1.call-start = ((), (), s32[]{:S(2)}) async-start(), calls=%async_computation.6 | async-start | bytes 98304 | tf_op jit(solution)/shard_map/reduce_scatter | solution.py:56
Sparse Core Ops, SparseCore 0:
  26.6 24.1 all-reduce.1
  57.6 55.7 reduce-scatter.3
  137.5 7.1 reduce-scatter.5
  171.1 6.2 reduce-scatter.7
where the time goes:
time: 186 us; the launch traced here: 185 us
  blocking collectives  88.6 us (48%)
  waiting for transfers between devices  40.4 us (22%)
  matrix products  31.1 us (17%)
  between operations  14.5 us (8%)
  other arithmetic  6.66 us (4%)
  local copies, waits for them, and re-layouts  3.79 us (2%)
    all_gather x2, blocking collectives, spread(): return lax.all_gather(theta_own, 'dp', axis=0, tiled=True)  44.1 us
    pmax x1, blocking collectives, body(): largest = lax.pmax(jnp.max(row_sums), 'dp')  31.3 us
    psum x1, waiting for transfers between devices, body(): predictions = lax.psum(partial_pred, 'centre')  24.2 us
    dot_general x2, matrix products, kernel_block(): lax.dot_general(left, right, (((1,), (1,)), ((), ())), precision=lax.Prec...  15 us
    reduce_scatter x2, waiting for transfers between devices, project(): lax.psum_scatter(matmul(square, gathered), 'centre', scatter_dimension=0,...  13.6 us
    dot_general x3, matrix products, matmul(): jnp.dot(left, right, precision=lax.Precision.HIGHEST, preferred_element_t...  10.3 us
    all_gather x1, blocking collectives, body(): row_centres = lax.all_gather(own_centres, 'centre', axis=0, tiled=True)  8.28 us
    dot_general x1, matrix products, body(): lax.dot_general(data_tile, residual, (((0,), (0,)), ((), ())), precision=...  5.81 us
  transfers between devices with their start and end apart: 4, of which 4 were waited for; matrix products, arithmetic and copies ran while one was open for 4% of the time, Pallas kernels for 0%

commit v1 on v0

v1 whole, which is shorter than its diff:
```python
import functools
import jax
import jax.numpy as jnp
from jax import lax
from jax.experimental import pallas as pl
from jax.experimental.pallas import tpu as pltpu
from jax.sharding import PartitionSpec as P

softening = 0.01
kernel_scale = 0.2
learning_rate = 4.0
f32, bf16 = jnp.float32, jnp.bfloat16


def split(x):
    high = x.astype(bf16)
    return high, (x - high.astype(f32)).astype(bf16)


def dot(left, right):
    return jnp.dot(left, right, preferred_element_type=f32)


def add(ref, value, step):
    ref[...] = jnp.where(step == 0, value, ref[...] + value)


def call(kernel, name, info, ins, outs, grid=(1,), scratch=(), flops=0, size=0, room=16):
    def spec(pair):
        array, block = pair
        if block is None:
            rank = len(array.shape)
            return pl.BlockSpec(array.shape, lambda i, s, rank=rank: (0,) * rank)
        return pl.BlockSpec(*block)

    result = pl.pallas_call(
        kernel,
        name=name,
        grid_spec=pltpu.PrefetchScalarGridSpec(
            num_scalar_prefetch=1,
            grid=grid,
            in_specs=[spec(pair) for pair in ins],
            out_specs=[spec(pair) for pair in outs],
            scratch_shapes=list(scratch),
        ),
        out_shape=[jax.ShapeDtypeStruct(a.shape, a.dtype) for a, _ in outs],
        compiler_params=pltpu.CompilerParams(vmem_limit_bytes=room * 1024 * 1024),
        cost_estimate=pl.CostEstimate(flops=flops, bytes_accessed=size, transcendentals=0),
    )(info, *[array for array, _ in ins])
    return result


def like(*shape, dtype=f32):
    return jax.ShapeDtypeStruct(shape, dtype)


def points_in(x, at, high_ref, low_ref, square_ref):
    xt = x.T
    high, low = split(xt)
    wide, rest = high.astype(f32), low.astype(f32)
    where = pl.ds(at, x.shape[0])
    square_ref[:, where] = jnp.sum(wide * wide + 2.0 * (wide * rest), axis=0, keepdims=True)
    high_ref[:, where] = (-2.0 * wide).astype(bf16)
    low_ref[:, where] = (-2.0 * rest).astype(bf16)


def entries(high, low, square, xh, xl, xsq):
    cross = dot(high, xh) + dot(low, xh) + dot(high, xl)
    dist = jnp.maximum(cross + (square + xsq), 0.0) + softening
    return jnp.exp(jnp.sqrt(dist) * (-1.0 / kernel_scale))


def data_kernel(info, x_ref, c_ref, w_ref, *refs):
    near_ref, away_ref, kh_ref, kl_ref, ch_ref, cl_ref, sq_ref, pred_ref, rows_ref, xh, xl, xsq, acc = refs
    step = pl.program_id(0)

    @pl.when(step == 0)
    def _():
        points_in(x_ref[...], 0, xh, xl, xsq)
        share = near_ref.shape[0]
        rows_ref[:share, :] = near_ref[...]
        rows_ref[share:, :] = away_ref[...]

    high, low = split(c_ref[...])
    wide, rest = high.astype(f32), low.astype(f32)
    square = jnp.sum(wide * wide + 2.0 * (wide * rest), axis=1, keepdims=True)
    ch_ref[...] = high
    cl_ref[...] = low
    sq_ref[...] = square
    tile = entries(high, low, square, xh[...], xl[...], xsq[...])
    kh, kl = split(tile)
    kh_ref[...] = kh
    kl_ref[...] = kl
    weights = jnp.concatenate(split(w_ref[...]), axis=0)
    add(acc, dot(weights, kh) + dot(weights, kl), step)
    outs = pred_ref.shape[0]

    @pl.when(step == pl.num_programs(0) - 1)
    def _():
        pred_ref[...] = acc[:outs, :] + acc[outs:, :]


def centre_kernel(info, *refs):
    x_refs = refs[:-9]
    ch_ref, cl_ref, sq_ref, kh_ref, kl_ref, sum_ref, xh, xl, xsq = refs[-9:]
    step = pl.program_id(0)

    @pl.when(step == 0)
    def _():
        at = 0
        for x_ref in x_refs:
            points_in(x_ref[...], at, xh, xl, xsq)
            at += x_ref.shape[0]

    tile = entries(ch_ref[...], cl_ref[...], sq_ref[...], xh[...], xl[...], xsq[...])
    kh, kl = split(tile)
    kh_ref[...] = kh
    kl_ref[...] = kl
    add(sum_ref, jnp.sum(tile.reshape(-1, 8, tile.shape[1]), axis=0), step)


def back(parts, right, out_ref):
    points = sum(ref.shape[-1] for ref in parts[0])
    high, low = [
        jnp.concatenate([ref[...].reshape(-1, ref.shape[-1]) for ref in refs], axis=1) for refs in parts
    ]
    outs = right.shape[1] // 2
    product = (dot(high, right) + dot(low, right)).T
    out_ref[:outs, :] = product[:outs] + product[outs:]


def grad_kernel(others, info, *refs):
    p_refs = refs[: 1 + others]
    t_ref, high_ref, low_ref, out_ref, res_ref, right_ref = refs[1 + others :]

    @pl.when(pl.program_id(0) == 0)
    def _():
        total = p_refs[0][...]
        for ref in p_refs[1:]:
            total = total + ref[...]
        residual = total - t_ref[...]
        res_ref[...] = residual
        right_ref[...] = jnp.concatenate(split(residual.T), axis=1)

    back(([high_ref], [low_ref]), right_ref[...], out_ref)


def keep_kernel(info, right_ref, *refs):
    count = len(refs) // 2
    back((refs[:count], refs[count:-1]), right_ref[...], refs[-1])


def image_kernel(shards, info, *refs):
    near_refs, away_refs = refs[:shards], refs[shards : 2 * shards]
    high_refs, low_refs = refs[2 * shards : 3 * shards], refs[3 * shards : 4 * shards]
    out_ref, right_ref, own_ref, max_ref, image_ref = refs[4 * shards :]
    outs, share = own_ref.shape

    @pl.when(pl.program_id(0) == 0)
    def _():
        total = near_refs[0][...]
        for ref in near_refs[1:]:
            total = total + ref[...]
        image = total[:outs]
        for ref in away_refs:
            image = image + ref[...]
        largest = jnp.max(total[outs : outs + 2], keepdims=True)
        max_ref[...] = jnp.broadcast_to(largest, max_ref.shape)
        image_ref[...] = image
        for j in range(shards):
            part = image_ref[:, pl.ds(place(info, j, shards, share), share)]
            right_ref[j * share : (j + 1) * share, :] = jnp.concatenate(split(part.T), axis=1)
            if j == 0:
                own_ref[...] = part

    back((high_refs, low_refs), right_ref[...], out_ref)
    out_ref[outs:, :] = jnp.broadcast_to(max_ref[:, :1], (8, out_ref.shape[1]))


def place(info, j, shards, share):
    return pl.multiple_of(lax.rem(info[3] + j, shards) * share, share)


def product_kernel(mids, shards, info, *refs):
    pieces = refs[: 2 * mids]
    oh, ol, fh, fl, osum, fsum, near_ref, away_ref, left, own, far = refs[2 * mids :]
    outs = pieces[0].shape[0]
    share = pieces[0].shape[1] // 2
    step = pl.program_id(0)

    @pl.when(step == 0)
    def _():
        core, mid = info[0], info[1]
        for m in range(mids):
            for k in range(2):
                high, low = split(pieces[2 * m + k][...])
                for top in range(2):
                    block = top * 2 * mids + 2 * (mid ^ m) + (core ^ k)
                    where = pl.ds(pl.multiple_of(block * share, share), share)
                    left[:outs, where] = high[:, top * share : (top + 1) * share]
                    left[outs:, where] = low[:, top * share : (top + 1) * share]

    rows = oh.shape[0]
    part = left[:, pl.ds(pl.multiple_of(step * rows, rows), rows)]
    add(own, dot(part, oh[...]) + dot(part, ol[...]), step)
    add(far, dot(part, fh[...]) + dot(part, fl[...]), step)

    @pl.when(step == pl.num_programs(0) - 1)
    def _():
        row = lax.broadcasted_iota(jnp.int32, (8, share), 0)
        for j in range(shards):
            source, sums, at = (own, osum, 0) if j == 0 else (far, fsum, 2 * share * (j - 1))
            where = pl.ds(place(info, j, shards, share), share)
            first, last = slice(at, at + share), slice(at + share, at + 2 * share)
            near_ref[:outs, where] = source[:outs, first] + source[outs:, first]
            away_ref[:, where] = source[:outs, last] + source[outs:, last]
            near_sum = jnp.sum(sums[:, first], axis=0, keepdims=True)
            away_sum = jnp.sum(sums[:, last], axis=0, keepdims=True)
            near_ref[outs:, where] = jnp.where(row == 0, near_sum, away_sum)


def join_kernel(mids, share, info, keep_ref, got_ref, *refs):
    outs = keep_ref.shape[0]
    piece_refs = refs[-mids:]
    for m in range(mids):
        for top in range(2):
            at = pl.ds(pl.multiple_of((top * mids + (info[1] ^ m)) * share, share), share)
            to = slice(top * share, (top + 1) * share)
            piece_refs[m][:outs, to] = keep_ref[:, at] + got_ref[:outs, at]
    if len(refs) > mids:
        largest = jnp.maximum(refs[0][...], got_ref[outs:, : refs[0].shape[1]])
        for m in range(mids):
            piece_refs[m][outs:, :] = jnp.broadcast_to(largest[:, :1], (8, 2 * share))


def sum_kernel(info, *refs):
    total = refs[0][...]
    for ref in refs[1:-1]:
        total = total + ref[...]
    refs[-1][...] = total


def theta_kernel(mids, share, info, part_ref, own_ref, *refs):
    pieces = refs[:mids]
    keep_ref, give_ref = refs[mids:]
    outs = part_ref.shape[0]
    second = pieces[0][:outs, :]
    largest = pieces[0][outs:, :]
    for ref in pieces[1:]:
        second = second + ref[:outs, :]
        largest = jnp.maximum(largest, ref[outs:, :])
    step = 1.0 / largest[:1, :1]
    theta = (3.0 * step) * part_ref[...] + (step * step * step) * second
    first, last = theta[:, :share], theta[:, share:]
    upper = info[2] == 1
    keep_ref[...] = jnp.where(upper, last, first) - (3.0 * step * step) * own_ref[...]
    give_ref[...] = jnp.where(upper, first, last)


def final_kernel(info, keep_ref, got_ref, coeff_ref, out_ref):
    out_ref[...] = coeff_ref[...] - learning_rate * (keep_ref[...] + got_ref[...])


def send_xor(array, mask):
    count = lax.axis_size("dp")
    return lax.ppermute(array, "dp", [(i, i ^ mask) for i in range(count)])


def send_far(array, mask, shift):
    dp, centre = lax.axis_size("dp"), lax.axis_size("centre")
    pairs = [
        (d * centre + c, (d ^ mask) * centre + (c + shift) % centre)
        for d in range(dp)
        for c in range(centre)
    ]
    return lax.ppermute(array, ("dp", "centre"), pairs)


def after(value, *others):
    return lax.optimization_barrier((value, *others))[0]


def body(samples, targets, centres, coefficients):
    count = lax.axis_size("dp")
    shards = lax.axis_size("centre")
    index = lax.axis_index("dp")
    rows, width = centres.shape
    share = rows // count
    points, outs = targets.shape
    half = count // 2
    mids = half // 2
    core, mid, top = index % 2, (index // 2) % mids, index // half
    info = jnp.stack([core, mid, top, lax.axis_index("centre"), index, index ^ half]).astype(jnp.int32)
    weights = coefficients.T

    near = (centres, ((share, width), lambda i, s: (s[4], 0)))
    away = (centres, ((share, width), lambda i, s: (s[5], 0)))
    block = min(512, rows)
    steps = rows // block
    rowed = lambda array, wide: (array, ((block, wide), lambda i, s: (i, 0)))
    kh, kl, ch, cl, square, pred, pair = call(
        data_kernel, "data", info,
        [(samples, None), rowed(centres, width), (weights, ((outs, block), lambda i, s: (0, i))), near, away],
        [
            rowed(like(rows, points, dtype=bf16), points),
            rowed(like(rows, points, dtype=bf16), points),
            rowed(like(rows, width, dtype=bf16), width),
            rowed(like(rows, width, dtype=bf16), width),
            rowed(like(rows, 1), 1),
            (like(outs, points), None),
            (like(2 * share, width), None),
        ],
        (steps,),
        [
            pltpu.VMEM((width, points), bf16),
            pltpu.VMEM((width, points), bf16),
            pltpu.VMEM((1, points), f32),
            pltpu.VMEM((2 * outs, points), f32),
        ],
        flops=6 * rows * points * width, size=12 * rows * width,
    )
    got = [send_far(pred, 0, shift) for shift in range(1, shards)]

    def centre_tile(blocks, columns, name):
        return call(
            centre_kernel, name, info,
            blocks + [rowed(ch, width), rowed(cl, width), rowed(square, 1)],
            [
                rowed(like(rows, columns, dtype=bf16), columns),
                rowed(like(rows, columns, dtype=bf16), columns),
                (like(8, columns), None),
            ],
            (steps,),
            [
                pltpu.VMEM((width, columns), bf16),
                pltpu.VMEM((width, columns), bf16),
                pltpu.VMEM((1, columns), f32),
            ],
            flops=6 * rows * columns * width, size=8 * rows * width,
            room=12 + columns // 64,
        )

    own_high, own_low, own_sums = centre_tile([near, away], 2 * share, "own_tile")
    far = [send_far(after(pair, own_high), 0, -shift) for shift in range(1, shards)]
    got[0] = after(got[0], own_high)

    pairs = count // 2
    group = min(4, pairs)

    def halves(array, flip, wide, at=0):
        return (
            array.reshape(pairs, 2, share, array.shape[1]),
            ((group, None, share, wide), lambda i, s: (i, s[0] ^ flip, 0, at)),
        )

    def columns(height):
        return (like(height, pairs * share), ((height, group * share), lambda i, s: (0, i)))

    backs = (pairs // group,)
    give, residual, right = call(
        functools.partial(grad_kernel, len(got)), "grad_give", info,
        [(pred, None)]
        + [(g, None) for g in got]
        + [(targets.T, None), halves(kh, 1, points), halves(kl, 1, points)],
        [columns(outs), (like(outs, points), None), (like(points, 2 * outs, dtype=bf16), None)],
        backs,
    )
    received = send_xor(give, 1)
    (keep,) = call(
        keep_kernel, "grad_keep", info,
        [(right, None), halves(kh, 0, points), halves(kl, 0, points)],
        [columns(outs)], backs,
    )

    def join(keep, received, extra, height):
        return call(
            functools.partial(join_kernel, mids, share), "join", info,
            [(keep, None), (received, None)] + [(e, None) for e in extra],
            [(like(height, 2 * share), None)] * mids,
        )

    pieces = join(keep, received, [], outs)
    pieces = [pieces[0]] + [send_xor(pieces[m], 2 * m) for m in range(1, mids)]
    (part,) = call(
        sum_kernel, "sum", info, [(p, None) for p in pieces], [(like(outs, 2 * share), None)]
    )
    gathered = [part] + [send_xor(part, 2 * m) for m in range(1, mids)]
    parts = []
    for piece in gathered:
        parts += [piece, send_xor(piece, 1)]
    wide = 2 * share * (shards - 1)
    far_high, far_low, far_sums = centre_tile([(after(f, part), None) for f in far], wide, "far_tile")

    near_part, away_part = call(
        functools.partial(product_kernel, mids, shards), "product", info,
        [(p, None) for p in parts]
        + [rowed(own_high, 2 * share), rowed(own_low, 2 * share), rowed(far_high, wide), rowed(far_low, wide)]
        + [(own_sums, None), (far_sums, None)],
        [(like(outs + 8, shards * share), None), (like(outs, shards * share), None)],
        (steps,),
        [
            pltpu.VMEM((2 * outs, rows), bf16),
            pltpu.VMEM((2 * outs, 2 * share), f32),
            pltpu.VMEM((2 * outs, wide), f32),
        ],
        room=12 + wide // 64,
    )
    nears = [near_part] + [send_far(near_part, 0, shift) for shift in range(1, shards)]
    aways = [send_far(away_part, half, shift) for shift in range(shards)]

    def near_halves(own, far, flip):
        return [halves(own, flip, share)] + [halves(far, flip, share, 2 * j) for j in range(shards - 1)]

    give, right, own, largest = call(
        functools.partial(image_kernel, shards), "image_give", info,
        [(a, None) for a in nears + aways]
        + near_halves(own_high, far_high, 1)
        + near_halves(own_low, far_low, 1),
        [
            columns(outs + 8),
            (like(shards * share, 2 * outs, dtype=bf16), None),
            (like(outs, share), None),
            (like(8, share), None),
        ],
        backs, [pltpu.VMEM((outs, shards * share), f32)],
    )
    received = send_xor(give, 1)
    (keep,) = call(
        keep_kernel, "image_keep", info,
        [(right, None)] + near_halves(own_high, far_high, 0) + near_halves(own_low, far_low, 0),
        [columns(outs)], backs,
    )
    pieces = join(keep, received, [largest], outs + 8)
    pieces = [pieces[0]] + [send_xor(pieces[m], 2 * m) for m in range(1, mids)]
    keep, give = call(
        functools.partial(theta_kernel, mids, share), "theta", info,
        [(part, None), (own, None)] + [(p, None) for p in pieces],
        [(like(outs, share), None)] * 2,
    )
    (new_coefficients,) = call(
        final_kernel, "final", info,
        [
            (keep, None),
            (send_xor(give, half), None),
            (weights, ((outs, share), lambda i, s: (0, s[4]))),
        ],
        [(like(outs, share), None)],
    )
    return (residual.T, new_coefficients.T)


def solution(mesh):
    return jax.shard_map(
        body,
        mesh=mesh,
        in_specs=(P("dp", None), P("dp", None), P("centre", None), P("centre", None)),
        out_specs=(P("dp", None), P(("centre", "dp"), None)),
        check_vma=False,
    )
```

time: 186 us -> 77.2 us (0.42)
  blocking collectives: 88.6 us -> 0 us
  matrix products: 31.1 us -> 0 us
  Pallas kernels: 0 us -> 29.9 us
  starting transfers between devices: 0.16 us -> 21.1 us
  waiting for transfers between devices: 40.4 us -> 20.5 us
  between operations: 14.5 us -> 0.84 us
  other arithmetic: 6.66 us -> 0 us
    all_gather x3 -> x0, blocking collectives: 52.4 us -> none  [the longest x2 44.1 us: spread(): return lax.all_gather(theta_own, 'dp', axis=0, tiled=True)]
    pmax x1 -> x0, blocking collectives: 31.3 us -> none  [body(): largest = lax.pmax(jnp.max(row_sums), 'dp')]
    dot_general x6 -> x0, matrix products: 31.1 us -> none  [the longest x2 15 us: kernel_block(): lax.dot_general(left, right, (((1,), (1,)), ((), ())), precision=lax.Prec...]
    pallas_call x0 -> x13, Pallas kernels: none -> 29.9 us  [call(): pl.pallas_call(kernel, name=name, grid_spec=pltpu.PrefetchScalarGridSpec(...]
    psum x1 -> x0, waiting for transfers between devices: 24.2 us -> none  [body(): predictions = lax.psum(partial_pred, 'centre')]
    ppermute x0 -> x21, starting transfers between devices: none -> 21.1 us  [the longest x16 13.5 us: send_xor(): return lax.ppermute(array, 'dp', [(i, i ^ mask) for i in range(count)])]
    ppermute x0 -> x21, waiting for transfers between devices: none -> 20.5 us  [the longest x16 14 us: send_xor(): return lax.ppermute(array, 'dp', [(i, i ^ mask) for i in range(count)])]
    reduce_scatter x3 -> x0, waiting for transfers between devices: 16.1 us -> none  [the longest x2 13.6 us: project(): lax.psum_scatter(matmul(square, gathered), 'centre', scatter_dimension=0,...]
  transfers between devices with their start and end apart: 4 -> 21, of which waited for: 4 -> 12; matrix products, arithmetic and copies ran while one was open for 4% -> 0% of each run, Pallas kernels for 0% -> 20%
where the time goes in v1:
time: 77.2 us; the launch traced here: 76.9 us
  Pallas kernels  29.9 us (39%)
  starting transfers between devices  21.1 us (27%)
  waiting for transfers between devices  20.5 us (27%)
  local copies, waits for them, and re-layouts  4.55 us (6%)
  between operations  0.84 us (1%)
    pallas_call x13, Pallas kernels, call(): pl.pallas_call(kernel, name=name, grid_spec=pltpu.PrefetchScalarGridSpec(...  29.9 us
    ppermute x16, waiting for transfers between devices, send_xor(): return lax.ppermute(array, 'dp', [(i, i ^ mask) for i in range(count)])  14 us
    ppermute x16, starting transfers between devices, send_xor(): return lax.ppermute(array, 'dp', [(i, i ^ mask) for i in range(count)])  13.5 us
    ppermute x5, starting transfers between devices, send_far(): return lax.ppermute(array, ('dp', 'centre'), pairs)  7.55 us
    ppermute x5, waiting for transfers between devices, send_far(): return lax.ppermute(array, ('dp', 'centre'), pairs)  6.46 us
    unnamed x12, local copies, waits for them, and re-layouts  4.47 us
  transfers between devices with their start and end apart: 21, of which 12 were waited for; matrix products, arithmetic and copies ran while one was open for 0% of the time, Pallas kernels for 20%

profile of v1, /device:TPU:0, one launch (start us, length us, event | category | flops | bytes accessed | tf_op | source)
XLA Modules:
  0.0 76.9 jit_solution(616981221377584615)
XLA Ops:
  0.8 2.2 %copy-done = f32[2048,512]{1,0:T(8,128)S(1)} copy-done((f32[2048,512]{1,0:T(8,128)S(1)}, f32[2048,512]{1,0:T(8,128)}, u32[]{:S(2)}) %copy-start) | copy-done | bytes 4194328
  5.2 8.3 %data.1 = (bf16[2048,512]{1,0:T(8,128)(2,1)S(1)}, bf16[2048,512]{1,0:T(8,128)(2,1)S(1)}, bf16[2048,512]{1,0:T(8,128)(2,1)S(1)}, bf16[2048,512]{1,0:T(8,128)(2,1)...) custom-call(s32[6]{0:T(128)S(1)} %stack.27.info, f32[512,512]{1,0:T(8,128)S(1)} %copy-done.4, ...), custom_call_target="tpu_custom_call" | custom-call | flops 3221225472 | bytes 12582912 | tf_op jit(solution)/shard_map/data/pallas_call | solution.py:36
  13.5 3.0 %collective-permute-start = (f32[64,512]{1,0:T(8,128)S(1)}, f32[64,512]{1,0:T(8,128)S(1)}, u32[]{:S(2)}, u32[]{:S(2)}) collective-permute-start(f32[64,512]{1,0:T(8,128)S(1)} %get-tuple-element.37.refs_0_), channel_id=1, source_target_pairs={{0,1},{1,0},{2,3},{3,2},{4,5},{5,4},{6,7},{7,6},{8,9},{9,8},{10,11... | collective-permute-start | bytes 393224 | tf_op jit(solution)/shard_map/ppermute | solution.py:276
  16.5 4.0 %own_tile.1 = (bf16[2048,256]{1,0:T(8,128)(2,1)S(1)}, bf16[2048,256]{1,0:T(8,128)(2,1)S(1)}, f32[8,256]{1,0:T(8,128)S(1)}) custom-call(s32[6]{0:T(128)S(1)} %stack.27.info, f32[2048,512]{1,0:T(8,128)S(1)} %copy-done.1, f32[2048,512]{1,0:T(8,128)S(1)} %copy-done.1, bf16[2048,512]{1,0:T(8,128)(2,1)S(1)} %get-tuple-element.38.refs_2_.refs_1_, ...), custom_call_target="tpu_custom_call" | custom-call | flops 1610612736 | bytes 8388608 | tf_op jit(solution)/shard_map/own_tile/pallas_call | solution.py:36
  20.7 2.7 %grad_give.1 = (f32[64,1024]{1,0:T(8,128)S(1)}, f32[64,512]{1,0:T(8,128)}, bf16[512,128]{1,0:T(8,128)(2,1)S(1)}) custom-call(s32[6]{0:T(128)S(1)} %stack.27.info, f32[64,512]{1,0:T(8,128)S(1)} %get-tuple-element.37.refs_0_, f32[64,512]{1,0:T(8,128)S(1)} %collective-permute-done.refs_1_, f32[64,512]{1,0:T(8,128)S(1)} %bitcast.30, ...), custom_call_target="tpu_custom_call" | custom-call | tf_op jit(solution)/shard_map/grad_give/pallas_call | solution.py:36
  23.4 1.8 %grad_keep.1.keep_ref = f32[64,1024]{1,0:T(8,128)S(1)} custom-call(s32[6]{0:T(128)S(1)} %stack.27.info, bf16[512,128]{1,0:T(8,128)(2,1)S(1)} %get-tuple-element.46.right_ref, bf16[8,2,128,512]{3,2,1,0:T(8,128)(2,1)S(1)} %bitcast.25, bf16[8,2,128,512]{3,2,1,0:T(8,128)(2,1)S(1)} %bitcast.27), custom_call_target="tpu_custom_call" | custom-call | tf_op jit(solution)/shard_map/grad_keep/pallas_call | solution.py:36
  25.8 2.1 %collective-permute-start.2 = (f32[64,256]{1,0:T(8,128)S(1)}, f32[64,256]{1,0:T(8,128)S(1)}, u32[]{:S(2)}, u32[]{:S(2)}) collective-permute-start(f32[64,256]{1,0:T(8,128)S(1)} %get-tuple-element.49), channel_id=1, source_target_pairs={{0,4},{2,6},{4,0},{6,2},{8,12},{10,14},{12,8},{14,10},{16,20},{18,... | collective-permute-start | bytes 196616 | tf_op jit(solution)/shard_map/ppermute | solution.py:266
  27.9 1.6 %collective-permute-start.3 = (f32[64,256]{1,0:T(8,128)S(1)}, f32[64,256]{1,0:T(8,128)S(1)}, u32[]{:S(2)}, u32[]{:S(2)}) collective-permute-start(f32[64,256]{1,0:T(8,128)S(1)} %get-tuple-element.50), channel_id=1, source_target_pairs={{0,8},{2,10},{4,12},{6,14},{8,0},{10,2},{12,4},{14,6},{16,24},{18,... | collective-permute-start | bytes 196616 | tf_op jit(solution)/shard_map/ppermute | solution.py:266
  30.7 1.8 %collective-permute-done.3.refs_2_ = f32[64,256]{1,0:T(8,128)S(1)} collective-permute-done((f32[64,256]{1,0:T(8,128)S(1)}, f32[64,256]{1,0:T(8,128)S(1)}, u32[]{:S(2)}, u32[]{:S(2)}) %collective-permute-start.3) | collective-permute-done | bytes 65568 | tf_op jit(solution)/shard_map/ppermute | solution.py:266
  32.5 2.2 %collective-permute-done.4.refs_3_ = f32[64,256]{1,0:T(8,128)S(1)} collective-permute-done((f32[64,256]{1,0:T(8,128)S(1)}, f32[64,256]{1,0:T(8,128)S(1)}, u32[]{:S(2)}, u32[]{:S(2)}) %collective-permute-start.4) | collective-permute-done | bytes 65568 | tf_op jit(solution)/shard_map/ppermute | solution.py:266
  37.3 1.5 %collective-permute-start.6 = (f32[64,256]{1,0:T(8,128)S(1)}, f32[64,256]{1,0:T(8,128)S(1)}, u32[]{:S(2)}, u32[]{:S(2)}) collective-permute-start(f32[64,256]{1,0:T(8,128)S(1)} %sum.1.refs_0_.part_ref), channel_id=1, source_target_pairs={{0,4},{2,6},{4,0},{6,2},{8,12},{10,14},{12,8},{14,10},{16,20},{18,... | collective-permute-start | bytes 196616 | tf_op jit(solution)/shard_map/ppermute | solution.py:266
  38.8 1.7 %collective-permute-done.10.refs_6_ = f32[64,256]{1,0:T(8,128)S(1)} collective-permute-done((f32[64,256]{1,0:T(8,128)S(1)}, f32[64,256]{1,0:T(8,128)S(1)}, u32[]{:S(2)}, u32[]{:S(2)}) %collective-permute-start.10) | collective-permute-done | bytes 65568 | tf_op jit(solution)/shard_map/ppermute | solution.py:266
  41.5 4.0 %far_tile.1 = (bf16[2048,256]{1,0:T(8,128)(2,1)S(1)}, bf16[2048,256]{1,0:T(8,128)(2,1)S(1)}, f32[8,256]{1,0:T(8,128)S(1)}) custom-call(s32[6]{0:T(128)S(1)} %stack.27.info, f32[256,512]{1,0:T(8,128)S(1)} %collective-permute-done.12.refs_0_, bf16[2048,512]{1,0:T(8,128)(2,1)S(1)} %get-tuple-element.38.refs_2_.refs_1_, ...), custom_call_target="tpu_custom_call" | custom-call | flops 1610612736 | bytes 8388608 | tf_op jit(solution)/shard_map/far_tile/pallas_call | solution.py:36
  45.6 2.0 %product.1 = (f32[72,256]{1,0:T(8,128)S(1)}, f32[64,256]{1,0:T(8,128)S(1)}) custom-call(s32[6]{0:T(128)S(1)} %stack.27.info, f32[64,256]{1,0:T(8,128)S(1)} %sum.1.refs_0_.part_ref, f32[64,256]{1,0:T(8,128)S(1)} %collective-permute-done.5.refs_1_, f32[64,256]{1,0:T(8,128)S(1)} %collective-permute-done.6.refs_2_, ...), custom_call_target="tpu_custom_call" | custom-call | tf_op jit(solution)/shard_map/product/pallas_call | solution.py:36
  47.6 1.6 %collective-permute-start.13 = (f32[72,256]{1,0:T(8,128)S(1)}, f32[72,256]{1,0:T(8,128)S(1)}, u32[]{:S(2)}, u32[]{:S(2)}) collective-permute-start(f32[72,256]{1,0:T(8,128)S(1)} %get-tuple-element.60.refs_0_), channel_id=1, source_target_pairs={{0,1},{1,0},{2,3},{3,2},{4,5},{5,4},{6,7},{7,6},{8,9},{9,8},{10,11... | collective-permute-start | bytes 221192 | tf_op jit(solution)/shard_map/ppermute | solution.py:276
  49.2 2.6 %collective-permute-start.15 = (f32[64,256]{1,0:T(8,128)S(1)}, f32[64,256]{1,0:T(8,128)S(1)}, u32[]{:S(2)}, u32[]{:S(2)}) collective-permute-start(f32[64,256]{1,0:T(8,128)S(1)} %get-tuple-element.61), channel_id=1, source_target_pairs={{0,17},{1,16},{2,19},{3,18},{4,21},{5,20},{6,23},{7,22},{8,25},{9,... | collective-permute-start | bytes 196616 | tf_op jit(solution)/shard_map/ppermute | solution.py:276
  52.1 5.8 %collective-permute-done.15.refs_3_ = f32[64,256]{1,0:T(8,128)S(1)} collective-permute-done((f32[64,256]{1,0:T(8,128)S(1)}, f32[64,256]{1,0:T(8,128)S(1)}, u32[]{:S(2)}, u32[]{:S(2)}) %collective-permute-start.15) | collective-permute-done | bytes 65568 | tf_op jit(solution)/shard_map/ppermute | solution.py:276
  58.5 1.9 %image_give.1 = (f32[72,1024]{1,0:T(8,128)S(1)}, bf16[256,128]{1,0:T(8,128)(2,1)S(1)}, f32[64,128]{1,0:T(8,128)S(1)}, f32[8,128]{1,0:T(8,128)S(1)}) custom-call(s32[6]{0:T(128)S(1)} %stack.27.info, f32[72,256]{1,0:T(8,128)S(1)} %get-tuple-element.60.refs_0_, f32[72,256]{1,0:T(8,128)S(1)} %collective-permute-done.13.refs_1_, ...), custom_call_target="tpu_custom_call" | custom-call | tf_op jit(solution)/shard_map/image_give/pallas_call | solution.py:36
  60.5 1.6 %image_keep.1.keep_ref = f32[64,1024]{1,0:T(8,128)S(1)} custom-call(s32[6]{0:T(128)S(1)} %stack.27.info, bf16[256,128]{1,0:T(8,128)(2,1)S(1)} %get-tuple-element.63.right_ref, bf16[8,2,128,256]{3,2,1,0:T(8,128)(2,1)S(1)} %bitcast.17, bf16[8,2,128,256]{3,2,1,0:T(8,128)(2,1)S(1)} %bitcast.21, bf16[8,2,128,256]{3,2,1,0:T(8,128)(2,1)S(1)} %bitcast.19, ...), custom_call_target="tpu_custom_call" | custom-call | tf_op jit(solution)/shard_map/image_keep/pallas_call | solution.py:36
  62.8 1.4 %collective-permute-start.17 = (f32[72,256]{1,0:T(8,128)S(1)}, f32[72,256]{1,0:T(8,128)S(1)}, u32[]{:S(2)}, u32[]{:S(2)}) collective-permute-start(f32[72,256]{1,0:T(8,128)S(1)} %get-tuple-element.67), channel_id=1, source_target_pairs={{0,4},{2,6},{4,0},{6,2},{8,12},{10,14},{12,8},{14,10},{16,20},{18,... | collective-permute-start | bytes 221192 | tf_op jit(solution)/shard_map/ppermute | solution.py:266
  64.2 2.1 %collective-permute-start.19 = (f32[72,256]{1,0:T(8,128)S(1)}, f32[72,256]{1,0:T(8,128)S(1)}, u32[]{:S(2)}, u32[]{:S(2)}) collective-permute-start(f32[72,256]{1,0:T(8,128)S(1)} %get-tuple-element.69), channel_id=1, source_target_pairs={{0,12},{2,14},{4,8},{6,10},{8,4},{10,6},{12,0},{14,2},{16,28},{18,... | collective-permute-start | bytes 221192 | tf_op jit(solution)/shard_map/ppermute | solution.py:266
  67.5 1.8 %collective-permute-done.18.refs_2_ = f32[72,256]{1,0:T(8,128)S(1)} collective-permute-done((f32[72,256]{1,0:T(8,128)S(1)}, f32[72,256]{1,0:T(8,128)S(1)}, u32[]{:S(2)}, u32[]{:S(2)}) %collective-permute-start.18) | collective-permute-done | bytes 73760 | tf_op jit(solution)/shard_map/ppermute | solution.py:266
  70.9 2.6 %collective-permute-start.20 = (f32[64,128]{1,0:T(8,128)S(1)}, f32[64,128]{1,0:T(8,128)S(1)}, u32[]{:S(2)}, u32[]{:S(2)}) collective-permute-start(f32[64,128]{1,0:T(8,128)S(1)} %get-tuple-element.71), channel_id=1, source_target_pairs={{0,16},{2,18},{4,20},{6,22},{8,24},{10,26},{12,28},{14,30},{16,0},... | collective-permute-start | bytes 98312 | tf_op jit(solution)/shard_map/ppermute | solution.py:266
  73.5 2.2 %collective-permute-done.20.got_ref = f32[64,128]{1,0:T(8,128)S(1)} collective-permute-done((f32[64,128]{1,0:T(8,128)S(1)}, f32[64,128]{1,0:T(8,128)S(1)}, u32[]{:S(2)}, u32[]{:S(2)}) %collective-permute-start.20) | collective-permute-done | bytes 32800 | tf_op jit(solution)/shard_map/ppermute | solution.py:266
  (44 shorter events, 13.6 us)
Async XLA Ops:
  5.2 11.3 %copy-start.1 = (f32[2048,512]{1,0:T(8,128)S(1)}, f32[2048,512]{1,0:T(8,128)}, u32[]{:S(2)}) copy-start(f32[2048,512]{1,0:T(8,128)} %refs_1_.3) | copy-start | bytes 12582916
  13.5 7.1 %collective-permute-start = (f32[64,512]{1,0:T(8,128)S(1)}, f32[64,512]{1,0:T(8,128)S(1)}, u32[]{:S(2)}, u32[]{:S(2)}) collective-permute-start(f32[64,512]{1,0:T(8,128)S(1)} %get-tuple-element.37.refs_0_), channel_id=1, source_target_pairs={{0,1},{1,0},{2,3},{3,2},{4,5},{5,4},{6,7},{7,6},{8,9},{9,8},{10,11... | collective-permute-start | bytes 393224 | tf_op jit(solution)/shard_map/ppermute | solution.py:276
  16.5 4.1 %copy-start.5 = (f32[512,64]{0,1:T(8,128)S(1)}, f32[512,64]{0,1:T(8,128)}, u32[]{:S(2)}) copy-start(f32[512,64]{0,1:T(8,128)} %param.5) | copy-start | bytes 393220
  20.6 21.0 %collective-permute-start.12 = (f32[256,512]{1,0:T(8,128)S(1)}, f32[256,512]{1,0:T(8,128)S(1)}, u32[]{:S(2)}, u32[]{:S(2)}) collective-permute-start(f32[256,512]{1,0:T(8,128)S(1)} %get-tuple-element.54), channel_id=1, source_target_pairs={{0,1},{1,0},{2,3},{3,2},{4,5},{5,4},{6,7},{7,6},{8,9},{9,8},{10,11... | collective-permute-start | bytes 1572872 | tf_op jit(solution)/shard_map/ppermute | solution.py:276
  23.4 1.8 %collective-permute-start.1 = (f32[64,1024]{1,0:T(8,128)S(1)}, f32[64,1024]{1,0:T(8,128)S(1)}, u32[]{:S(2)}, u32[]{:S(2)}) collective-permute-start(f32[64,1024]{1,0:T(8,128)S(1)} %get-tuple-element.47), channel_id=1, source_target_pairs={{0,2},{2,0},{4,6},{6,4},{8,10},{10,8},{12,14},{14,12},{16,18},{18,... | collective-permute-start | bytes 786440 | tf_op jit(solution)/shard_map/ppermute | solution.py:266
  25.8 4.9 %collective-permute-start.2 = (f32[64,256]{1,0:T(8,128)S(1)}, f32[64,256]{1,0:T(8,128)S(1)}, u32[]{:S(2)}, u32[]{:S(2)}) collective-permute-start(f32[64,256]{1,0:T(8,128)S(1)} %get-tuple-element.49), channel_id=1, source_target_pairs={{0,4},{2,6},{4,0},{6,2},{8,12},{10,14},{12,8},{14,10},{16,20},{18,... | collective-permute-start | bytes 196616 | tf_op jit(solution)/shard_map/ppermute | solution.py:266
  27.9 4.5 %collective-permute-start.3 = (f32[64,256]{1,0:T(8,128)S(1)}, f32[64,256]{1,0:T(8,128)S(1)}, u32[]{:S(2)}, u32[]{:S(2)}) collective-permute-start(f32[64,256]{1,0:T(8,128)S(1)} %get-tuple-element.50), channel_id=1, source_target_pairs={{0,8},{2,10},{4,12},{6,14},{8,0},{10,2},{12,4},{14,6},{16,24},{18,... | collective-permute-start | bytes 196616 | tf_op jit(solution)/shard_map/ppermute | solution.py:266
  29.5 5.2 %collective-permute-start.4 = (f32[64,256]{1,0:T(8,128)S(1)}, f32[64,256]{1,0:T(8,128)S(1)}, u32[]{:S(2)}, u32[]{:S(2)}) collective-permute-start(f32[64,256]{1,0:T(8,128)S(1)} %get-tuple-element.51), channel_id=1, source_target_pairs={{0,12},{2,14},{4,8},{6,10},{8,4},{10,6},{12,0},{14,2},{16,28},{18,... | collective-permute-start | bytes 196616 | tf_op jit(solution)/shard_map/ppermute | solution.py:266
  35.2 5.2 %collective-permute-start.10 = (f32[64,256]{1,0:T(8,128)S(1)}, f32[64,256]{1,0:T(8,128)S(1)}, u32[]{:S(2)}, u32[]{:S(2)}) collective-permute-start(f32[64,256]{1,0:T(8,128)S(1)} %sum.1.refs_0_.part_ref), channel_id=1, source_target_pairs={{0,12},{2,14},{4,8},{6,10},{8,4},{10,6},{12,0},{14,2},{16,28},{18,... | collective-permute-start | bytes 196616 | tf_op jit(solution)/shard_map/ppermute | solution.py:266
  36.7 4.3 %collective-permute-start.8 = (f32[64,256]{1,0:T(8,128)S(1)}, f32[64,256]{1,0:T(8,128)S(1)}, u32[]{:S(2)}, u32[]{:S(2)}) collective-permute-start(f32[64,256]{1,0:T(8,128)S(1)} %sum.1.refs_0_.part_ref), channel_id=1, source_target_pairs={{0,8},{2,10},{4,12},{6,14},{8,0},{10,2},{12,4},{14,6},{16,24},{18,... | collective-permute-start | bytes 196616 | tf_op jit(solution)/shard_map/ppermute | solution.py:266
  37.3 4.3 %collective-permute-start.6 = (f32[64,256]{1,0:T(8,128)S(1)}, f32[64,256]{1,0:T(8,128)S(1)}, u32[]{:S(2)}, u32[]{:S(2)}) collective-permute-start(f32[64,256]{1,0:T(8,128)S(1)} %sum.1.refs_0_.part_ref), channel_id=1, source_target_pairs={{0,4},{2,6},{4,0},{6,2},{8,12},{10,14},{12,8},{14,10},{16,20},{18,... | collective-permute-start | bytes 196616 | tf_op jit(solution)/shard_map/ppermute | solution.py:266
  38.8 6.8 %collective-permute-start.5 = (f32[64,256]{1,0:T(8,128)S(1)}, f32[64,256]{1,0:T(8,128)S(1)}, u32[]{:S(2)}, u32[]{:S(2)}) collective-permute-start(f32[64,256]{1,0:T(8,128)S(1)} %sum.1.refs_0_.part_ref), channel_id=1, source_target_pairs={{0,2},{2,0},{4,6},{6,4},{8,10},{10,8},{12,14},{14,12},{16,18},{18,... | collective-permute-start | bytes 196616 | tf_op jit(solution)/shard_map/ppermute | solution.py:266
  40.5 5.1 %collective-permute-start.11 = (f32[64,256]{1,0:T(8,128)S(1)}, f32[64,256]{1,0:T(8,128)S(1)}, u32[]{:S(2)}, u32[]{:S(2)}) collective-permute-start(f32[64,256]{1,0:T(8,128)S(1)} %collective-permute-done.10.refs_6_), channel_id=1, source_target_pairs={{0,2},{2,0},{4,6},{6,4},{8,10},{10,8},{12,14},{14,12},{16,18},{18,... | collective-permute-start | bytes 196616 | tf_op jit(solution)/shard_map/ppermute | solution.py:266
  40.9 4.6 %collective-permute-start.9 = (f32[64,256]{1,0:T(8,128)S(1)}, f32[64,256]{1,0:T(8,128)S(1)}, u32[]{:S(2)}, u32[]{:S(2)}) collective-permute-start(f32[64,256]{1,0:T(8,128)S(1)} %collective-permute-done.8.refs_4_), channel_id=1, source_target_pairs={{0,2},{2,0},{4,6},{6,4},{8,10},{10,8},{12,14},{14,12},{16,18},{18,... | collective-permute-start | bytes 196616 | tf_op jit(solution)/shard_map/ppermute | solution.py:266
  41.5 4.0 %collective-permute-start.7 = (f32[64,256]{1,0:T(8,128)S(1)}, f32[64,256]{1,0:T(8,128)S(1)}, u32[]{:S(2)}, u32[]{:S(2)}) collective-permute-start(f32[64,256]{1,0:T(8,128)S(1)} %collective-permute-done.6.refs_2_), channel_id=1, source_target_pairs={{0,2},{2,0},{4,6},{6,4},{8,10},{10,8},{12,14},{14,12},{16,18},{18,... | collective-permute-start | bytes 196616 | tf_op jit(solution)/shard_map/ppermute | solution.py:266
  47.6 10.9 %collective-permute-start.13 = (f32[72,256]{1,0:T(8,128)S(1)}, f32[72,256]{1,0:T(8,128)S(1)}, u32[]{:S(2)}, u32[]{:S(2)}) collective-permute-start(f32[72,256]{1,0:T(8,128)S(1)} %get-tuple-element.60.refs_0_), channel_id=1, source_target_pairs={{0,1},{1,0},{2,3},{3,2},{4,5},{5,4},{6,7},{7,6},{8,9},{9,8},{10,11... | collective-permute-start | bytes 221192 | tf_op jit(solution)/shard_map/ppermute | solution.py:276
  49.2 8.7 %collective-permute-start.15 = (f32[64,256]{1,0:T(8,128)S(1)}, f32[64,256]{1,0:T(8,128)S(1)}, u32[]{:S(2)}, u32[]{:S(2)}) collective-permute-start(f32[64,256]{1,0:T(8,128)S(1)} %get-tuple-element.61), channel_id=1, source_target_pairs={{0,17},{1,16},{2,19},{3,18},{4,21},{5,20},{6,23},{7,22},{8,25},{9,... | collective-permute-start | bytes 196616 | tf_op jit(solution)/shard_map/ppermute | solution.py:276
  51.8 6.8 %collective-permute-start.14 = (f32[64,256]{1,0:T(8,128)S(1)}, f32[64,256]{1,0:T(8,128)S(1)}, u32[]{:S(2)}, u32[]{:S(2)}) collective-permute-start(f32[64,256]{1,0:T(8,128)S(1)} %get-tuple-element.61), channel_id=1, source_target_pairs={{0,16},{1,17},{2,18},{3,19},{4,20},{5,21},{6,22},{7,23},{8,24},{9,... | collective-permute-start | bytes 196616 | tf_op jit(solution)/shard_map/ppermute | solution.py:276
  60.4 1.7 %collective-permute-start.16 = (f32[72,1024]{1,0:T(8,128)S(1)}, f32[72,1024]{1,0:T(8,128)S(1)}, u32[]{:S(2)}, u32[]{:S(2)}) collective-permute-start(f32[72,1024]{1,0:T(8,128)S(1)} %get-tuple-element.64), channel_id=1, source_target_pairs={{0,2},{2,0},{4,6},{6,4},{8,10},{10,8},{12,14},{14,12},{16,18},{18,... | collective-permute-start | bytes 884744 | tf_op jit(solution)/shard_map/ppermute | solution.py:266
  60.5 15.3 %copy-start.3 = (f32[2048,64]{0,1:T(8,128)S(1)}, f32[2048,64]{0,1:T(8,128)}, u32[]{:S(2)}) copy-start(f32[2048,64]{0,1:T(8,128)} %param.7) | copy-start | bytes 1572868
  62.8 4.7 %collective-permute-start.17 = (f32[72,256]{1,0:T(8,128)S(1)}, f32[72,256]{1,0:T(8,128)S(1)}, u32[]{:S(2)}, u32[]{:S(2)}) collective-permute-start(f32[72,256]{1,0:T(8,128)S(1)} %get-tuple-element.67), channel_id=1, source_target_pairs={{0,4},{2,6},{4,0},{6,2},{8,12},{10,14},{12,8},{14,10},{16,20},{18,... | collective-permute-start | bytes 221192 | tf_op jit(solution)/shard_map/ppermute | solution.py:266
  64.2 5.1 %collective-permute-start.18 = (f32[72,256]{1,0:T(8,128)S(1)}, f32[72,256]{1,0:T(8,128)S(1)}, u32[]{:S(2)}, u32[]{:S(2)}) collective-permute-start(f32[72,256]{1,0:T(8,128)S(1)} %get-tuple-element.68), channel_id=1, source_target_pairs={{0,8},{2,10},{4,12},{6,14},{8,0},{10,2},{12,4},{14,6},{16,24},{18,... | collective-permute-start | bytes 221192 | tf_op jit(solution)/shard_map/ppermute | solution.py:266
  64.2 6.1 %collective-permute-start.19 = (f32[72,256]{1,0:T(8,128)S(1)}, f32[72,256]{1,0:T(8,128)S(1)}, u32[]{:S(2)}, u32[]{:S(2)}) collective-permute-start(f32[72,256]{1,0:T(8,128)S(1)} %get-tuple-element.69), channel_id=1, source_target_pairs={{0,12},{2,14},{4,8},{6,10},{8,4},{10,6},{12,0},{14,2},{16,28},{18,... | collective-permute-start | bytes 221192 | tf_op jit(solution)/shard_map/ppermute | solution.py:266
  70.9 4.9 %collective-permute-start.20 = (f32[64,128]{1,0:T(8,128)S(1)}, f32[64,128]{1,0:T(8,128)S(1)}, u32[]{:S(2)}, u32[]{:S(2)}) collective-permute-start(f32[64,128]{1,0:T(8,128)S(1)} %get-tuple-element.71), channel_id=1, source_target_pairs={{0,16},{2,18},{4,20},{6,22},{8,24},{10,26},{12,28},{14,30},{16,0},... | collective-permute-start | bytes 98312 | tf_op jit(solution)/shard_map/ppermute | solution.py:266
  (3 other events, 4.5 us)

commit v2 on v0

v2 whole, which is shorter than its diff:
```python
import functools
import jax
import jax.numpy as jnp
from jax import lax
from jax.experimental import pallas as pl
from jax.experimental.pallas import tpu as pltpu
from jax.sharding import PartitionSpec as P

softening = 0.01
kernel_scale = 0.2
learning_rate = 4.0
f32, bf16 = jnp.float32, jnp.bfloat16
mega = 1024 * 1024


def split(x):
    high = x.astype(bf16)
    return high, (x - high.astype(f32)).astype(bf16)


def dot(left, right):
    return jnp.dot(left, right, preferred_element_type=f32)


def place():
    index, count = lax.axis_index("dp"), lax.axis_size("dp")
    return index, lax.rem(index, 2), lax.rem(index // 2, count // 4), index // (count // 2)


def like(*shape, dtype=f32):
    return jax.ShapeDtypeStruct(shape, dtype)


def call(kernel, name, ins, outs, scratch=(), room=8 * mega, flops=0, space=pltpu.VMEM):
    return pl.pallas_call(
        kernel,
        name=name,
        in_specs=[pl.BlockSpec(memory_space=space)] * len(ins),
        out_specs=[pl.BlockSpec(memory_space=pltpu.VMEM)] * len(outs),
        out_shape=list(outs),
        scratch_shapes=list(scratch),
        compiler_params=pltpu.CompilerParams(vmem_limit_bytes=room),
        cost_estimate=pl.CostEstimate(flops=flops, bytes_accessed=0, transcendentals=0),
    )(*ins)


def points_in(x):
    high, low = split(x.T)
    wide, rest = high.astype(f32), low.astype(f32)
    square = jnp.sum(wide * wide + 2.0 * (wide * rest), axis=0, keepdims=True)
    return (-2.0 * wide).astype(bf16), (-2.0 * rest).astype(bf16), square


def entries(high, low, square, xh, xl, xsq):
    cross = dot(high, xh) + dot(low, xh) + dot(high, xl)
    dist = jnp.maximum(cross + (square + xsq), 0.0) + softening
    return jnp.exp(dist * lax.rsqrt(dist) * (-1.0 / kernel_scale))


def load_kernel(c_hbm, ch_ref, cl_ref, sq_ref, pair_ref, c_ref, sems):
    rows, share = c_ref.shape[0], pair_ref.shape[0] // 2
    index, half = place()[0], lax.axis_size("dp") // 2
    loads = sems.shape[0]
    load = rows // loads
    copies = [
        pltpu.make_async_copy(c_hbm.at[pl.ds(i * load, load)], c_ref.at[pl.ds(i * load, load)], sems.at[i])
        for i in range(loads)
    ]
    for copy in copies:
        copy.start()
    for i, copy in enumerate(copies):
        copy.wait()
        where = slice(i * load, (i + 1) * load)
        high, low = split(c_ref[where, :])
        wide, rest = high.astype(f32), low.astype(f32)
        ch_ref[where, :] = high
        cl_ref[where, :] = low
        sq_ref[where, :] = jnp.sum(wide * wide + 2.0 * (wide * rest), axis=1, keepdims=True)
    for t, at in enumerate((index, lax.rem(index + half, 2 * half))):
        pair_ref[t * share : (t + 1) * share, :] = c_ref[pl.ds(pl.multiple_of(at * share, share), share), :]


def data_kernel(block, x_ref, w_ref, ch_ref, cl_ref, sq_ref, kh_ref, kl_ref, pred_ref, xh_ref, xl_ref):
    rows, outs = ch_ref.shape[0], pred_ref.shape[0]
    xh, xl, xsq = points_in(x_ref[...])
    xh_ref[...] = xh
    xl_ref[...] = xl
    pred = None
    for i in range(rows // block):
        where = slice(i * block, (i + 1) * block)
        tile = entries(ch_ref[where, :], cl_ref[where, :], sq_ref[where, :], xh_ref[...], xl_ref[...], xsq)
        kh, kl = split(tile)
        kh_ref[where, :] = kh
        kl_ref[where, :] = kl
        weights = jnp.concatenate(split(w_ref[:, where]), axis=0)
        part = dot(weights, kh) + dot(weights, kl)
        pred = part if pred is None else pred + part
    pred_ref[...] = pred[:outs, :] + pred[outs:, :]


def centre_kernel(block, *refs):
    x_refs = refs[:-8]
    ch_ref, cl_ref, sq_ref, kh_ref, kl_ref, sum_ref, xh_ref, xl_ref = refs[-8:]
    rows = ch_ref.shape[0]
    at = 0
    for x_ref in x_refs:
        span = slice(at, at + x_ref.shape[0])
        at = span.stop
        xh, xl, xsq = points_in(x_ref[...])
        xh_ref[...] = xh
        xl_ref[...] = xl
        total = None
        for i in range(rows // block):
            where = slice(i * block, (i + 1) * block)
            tile = entries(ch_ref[where, :], cl_ref[where, :], sq_ref[where, :], xh_ref[...], xl_ref[...], xsq)
            kh, kl = split(tile)
            kh_ref[where, span] = kh
            kl_ref[where, span] = kl
            part = jnp.sum(tile.reshape(-1, 8, tile.shape[1]), axis=0)
            total = part if total is None else total + part
        sum_ref[:, span] = total


def share_rows(mids, share, flip):
    _, core, mid, _ = place()
    for m in range(mids):
        for top in range(2):
            block = top * 2 * mids + 2 * (mid ^ m) + (core ^ flip)
            yield pl.ds(pl.multiple_of(block * share, share), share)


def take(ref, where, columns=slice(None)):
    return jnp.concatenate([ref[rows, columns] for rows in where], axis=0)


def back(mids, share, flip, parts, right):
    where = list(share_rows(mids, share, flip))
    product, at = 0.0, 0
    for high, low, columns in parts:
        size = columns.stop - columns.start
        values = right[at : at + size]
        at += size
        product = product + (dot(take(high, where, columns), values) + dot(take(low, where, columns), values))
    product = product.T
    outs = right.shape[1] // 2
    return product[:outs] + product[outs:]


def grad_kernel(mids, share, *refs):
    t_ref, high_ref, low_ref, out_ref, res_ref, right_ref = refs[-6:]
    total = refs[0][...]
    for ref in refs[1:-6]:
        total = total + ref[...]
    residual = total - t_ref[...]
    res_ref[...] = residual
    right = jnp.concatenate(split(residual.T), axis=1)
    right_ref[...] = right
    out_ref[...] = back(mids, share, 1, [(high_ref, low_ref, slice(0, right.shape[0]))], right)


def grad_keep_kernel(mids, share, right_ref, high_ref, low_ref, out_ref):
    right = right_ref[...]
    out_ref[...] = back(mids, share, 0, [(high_ref, low_ref, slice(0, right.shape[0]))], right)


def near_parts(share, own_high, own_low, far_high, far_low):
    parts = [(own_high, own_low, slice(0, share))]
    for at in range(0, far_high.shape[1], 2 * share):
        parts.append((far_high, far_low, slice(at, at + share)))
    return parts


def image_kernel(mids, shards, *refs):
    near_refs, away_refs = refs[:shards], refs[shards : 2 * shards]
    kernels = refs[2 * shards : 2 * shards + 4]
    out_ref, right_ref, own_ref, max_ref, image_ref = refs[2 * shards + 4 :]
    outs, share = own_ref.shape
    total = near_refs[0][...]
    for ref in near_refs[1:]:
        total = total + ref[...]
    image = total[:outs]
    for ref in away_refs:
        image = image + ref[...]
    largest = jnp.max(total[outs : outs + 2], keepdims=True)
    max_ref[...] = jnp.broadcast_to(largest, max_ref.shape)
    out_ref[outs:, :] = jnp.broadcast_to(largest, (8, out_ref.shape[1]))
    image_ref[...] = image
    for j in range(shards):
        part = image_ref[:, pl.ds(shard_at(j, shards, share), share)]
        right_ref[j * share : (j + 1) * share, :] = jnp.concatenate(split(part.T), axis=1)
        if j == 0:
            own_ref[...] = part
    out_ref[:outs, :] = back(mids, share, 1, near_parts(share, *kernels), right_ref[...])


def image_keep_kernel(mids, share, right_ref, *refs):
    refs[-1][...] = back(mids, share, 0, near_parts(share, *refs[:4]), right_ref[...])


def shard_at(j, shards, share):
    return pl.multiple_of(lax.rem(lax.axis_index("centre") + j, shards) * share, share)


def product(mids, share, flip, pieces, kernels):
    where = list(share_rows(mids, share, flip))
    high, low = split(jnp.concatenate([ref[...] for ref in pieces], axis=1))
    left = jnp.concatenate([high, low], axis=0)
    outs = high.shape[0]
    for kh, kl in (kernels[:2], kernels[2:]):
        result = dot(left, take(kh, where)) + dot(left, take(kl, where))
        yield result[:outs] + result[outs:]


def first_kernel(mids, share, *refs):
    own_ref, far_ref = refs[-2:]
    own, far = product(mids, share, 0, refs[:mids], refs[mids : mids + 4])
    own_ref[...] = own
    far_ref[...] = far


def second_kernel(mids, shards, *refs):
    own_ref, far_ref, osum, fsum, near_ref, away_ref = refs[mids + 4 :]
    outs = away_ref.shape[0]
    share = away_ref.shape[1] // shards
    own, far = product(mids, share, 1, refs[:mids], refs[mids : mids + 4])
    own, far = own + own_ref[...], far + far_ref[...]
    row = lax.broadcasted_iota(jnp.int32, (8, share), 0)
    for j in range(shards):
        source, sums, at = (own, osum, 0) if j == 0 else (far, fsum, 2 * share * (j - 1))
        where = pl.ds(shard_at(j, shards, share), share)
        first, last = slice(at, at + share), slice(at + share, at + 2 * share)
        near_ref[:outs, where] = source[:, first]
        away_ref[:, where] = source[:, last]
        near_sum = jnp.sum(sums[:, first], axis=0, keepdims=True)
        away_sum = jnp.sum(sums[:, last], axis=0, keepdims=True)
        near_ref[outs:, where] = jnp.where(row == 0, near_sum, away_sum)


def join_kernel(mids, keep_ref, got_ref, *refs):
    outs = keep_ref.shape[0]
    piece_refs = refs[-mids:]
    wide = piece_refs[0].shape[1]
    for m in range(mids):
        columns = slice(m * wide, (m + 1) * wide)
        piece_refs[m][:outs, :] = keep_ref[:, columns] + got_ref[:outs, columns]
    if len(refs) > mids:
        largest = jnp.maximum(refs[0][...], got_ref[outs:, : refs[0].shape[1]])
        for m in range(mids):
            piece_refs[m][outs:, :] = jnp.broadcast_to(largest[:, :1], (8, wide))


def sum_kernel(*refs):
    total = refs[0][...]
    for ref in refs[1:-1]:
        total = total + ref[...]
    refs[-1][...] = total


def theta_kernel(mids, share, part_ref, own_ref, *refs):
    pieces = refs[:mids]
    keep_ref, give_ref = refs[mids:]
    outs = part_ref.shape[0]
    second = pieces[0][:outs, :]
    largest = pieces[0][outs:, :]
    for ref in pieces[1:]:
        second = second + ref[:outs, :]
        largest = jnp.maximum(largest, ref[outs:, :])
    step = 1.0 / largest[:1, :1]
    theta = (3.0 * step) * part_ref[...] + (step * step * step) * second
    first, last = theta[:, :share], theta[:, share:]
    upper = place()[3] == 1
    keep_ref[...] = jnp.where(upper, last, first) - (3.0 * step * step) * own_ref[...]
    give_ref[...] = jnp.where(upper, first, last)


def final_kernel(keep_ref, got_ref, coeff_ref, out_ref):
    share = out_ref.shape[1]
    coefficients = coeff_ref[:, pl.ds(pl.multiple_of(place()[0] * share, share), share)]
    out_ref[...] = coefficients - learning_rate * (keep_ref[...] + got_ref[...])


def send_xor(array, mask):
    count = lax.axis_size("dp")
    return lax.ppermute(array, "dp", [(i, i ^ mask) for i in range(count)])


def send_far(array, mask, shift):
    dp, centre = lax.axis_size("dp"), lax.axis_size("centre")
    pairs = [
        (d * centre + c, (d ^ mask) * centre + (c + shift) % centre)
        for d in range(dp)
        for c in range(centre)
    ]
    return lax.ppermute(array, ("dp", "centre"), pairs)


def after(value, *others):
    return lax.optimization_barrier((value, *others))[0]


def body(samples, targets, centres, coefficients):
    count = lax.axis_size("dp")
    shards = lax.axis_size("centre")
    rows, width = centres.shape
    share = rows // count
    points, outs = targets.shape
    half = count // 2
    mids = half // 2
    weights = coefficients.T
    block = min(256, rows)

    loads = min(8, count)
    kept = 4 * rows * width + 512 * rows + 8 * share * width
    ch, cl, square, pair = call(
        load_kernel, "load", [centres],
        [
            like(rows, width, dtype=bf16),
            like(rows, width, dtype=bf16),
            like(rows, 1),
            like(2 * share, width),
        ],
        [pltpu.VMEM((rows, width), f32), pltpu.SemaphoreType.DMA((loads,))],
        room=103 * mega // 2 - kept, space=pltpu.HBM,
    )
    kh, kl, pred = call(
        functools.partial(data_kernel, block), "data", [samples, weights, ch, cl, square],
        [like(rows, points, dtype=bf16), like(rows, points, dtype=bf16), like(outs, points)],
        [pltpu.VMEM((width, points), bf16), pltpu.VMEM((width, points), bf16)],
    )
    got = [send_far(pred, 0, shift) for shift in range(1, shards)]

    def centre_tile(blocks, name):
        size = blocks[0].shape[0]
        columns = size * len(blocks)
        return call(
            functools.partial(centre_kernel, block), name, blocks + [ch, cl, square],
            [like(rows, columns, dtype=bf16), like(rows, columns, dtype=bf16), like(8, columns)],
            [pltpu.VMEM((width, size), bf16), pltpu.VMEM((width, size), bf16)],
            flops=6 * rows * columns * width,
        )

    own_high, own_low, own_sums = centre_tile([after(pair, pred)], "own_tile")
    got[0] = after(got[0], own_high)

    give, residual, right = call(
        functools.partial(grad_kernel, mids, share), "grad_give",
        [pred] + got + [targets.T, kh, kl],
        [like(outs, half * share), like(outs, points), like(points, 2 * outs, dtype=bf16)],
    )
    received = send_xor(give, 1)
    far = [send_far(after(pair, give), 0, -shift) for shift in range(1, shards)]
    (keep,) = call(
        functools.partial(grad_keep_kernel, mids, share), "grad_keep",
        [right, kh, kl], [like(outs, half * share)],
    )

    def join(keep, received, extra, height):
        return call(
            functools.partial(join_kernel, mids), "join",
            [keep, received] + extra, [like(height, 2 * share)] * mids,
        )

    pieces = join(keep, received, [], outs)
    pieces = [pieces[0]] + [send_xor(pieces[m], 2 * m) for m in range(mids - 1, 0, -1)]
    (part,) = call(sum_kernel, "sum", pieces, [like(outs, 2 * share)])
    gathered = [part] + [send_xor(part, 2 * m) for m in range(1, mids)]
    far_high, far_low, far_sums = centre_tile([after(f, part) for f in far], "far_tile")
    kernels = [own_high, own_low, far_high, far_low]
    crossed = [send_xor(after(piece, far_sums), 1) for piece in gathered]
    wide = 2 * share * (shards - 1)
    firsts = call(
        functools.partial(first_kernel, mids, share), "product_first",
        gathered + kernels, [like(outs, 2 * share), like(outs, wide)],
    )
    near_part, away_part = call(
        functools.partial(second_kernel, mids, shards), "product_second",
        crossed + kernels + list(firsts) + [own_sums, far_sums],
        [like(outs + 8, shards * share), like(outs, shards * share)],
    )
    aways = [send_far(away_part, half, shift) for shift in range(shards - 1, -1, -1)]
    nears = [near_part] + [send_far(near_part, 0, shift) for shift in range(1, shards)]

    give, right, own, largest = call(
        functools.partial(image_kernel, mids, shards), "image_give",
        nears + aways + kernels,
        [
            like(outs + 8, half * share),
            like(shards * share, 2 * outs, dtype=bf16),
            like(outs, share),
            like(8, share),
        ],
        [pltpu.VMEM((outs, shards * share), f32)],
    )
    received = send_xor(give, 1)
    (keep,) = call(
        functools.partial(image_keep_kernel, mids, share), "image_keep",
        [right] + kernels, [like(outs, half * share)],
    )
    pieces = join(keep, received, [largest], outs + 8)
    pieces = [pieces[0]] + [send_xor(pieces[m], 2 * m) for m in range(mids - 1, 0, -1)]
    keep, give = call(
        functools.partial(theta_kernel, mids, share), "theta",
        [part, own] + pieces, [like(outs, share)] * 2,
    )
    (new_coefficients,) = call(
        final_kernel, "final", [keep, send_xor(give, half), weights], [like(outs, share)]
    )
    return (residual.T, new_coefficients.T)


def solution(mesh):
    return jax.shard_map(
        body,
        mesh=mesh,
        in_specs=(P("dp", None), P("dp", None), P("centre", None), P("centre", None)),
        out_specs=(P("dp", None), P(("centre", "dp"), None)),
        check_vma=False,
    )
```

time: 186 us -> 64.1 us (0.34)
  blocking collectives: 88.6 us -> 0 us
  matrix products: 31.1 us -> 0 us
  starting transfers between devices: 0.16 us -> 22.8 us
  Pallas kernels: 0 us -> 20 us
  waiting for transfers between devices: 40.4 us -> 20.4 us
  between operations: 14.5 us -> 0.8 us
  other arithmetic: 6.66 us -> 0 us
  local copies, waits for them, and re-layouts: 3.79 us -> 0.01 us
    all_gather x3 -> x0, blocking collectives: 52.4 us -> none  [the longest x2 44.1 us: spread(): return lax.all_gather(theta_own, 'dp', axis=0, tiled=True)]
    pmax x1 -> x0, blocking collectives: 31.3 us -> none  [body(): largest = lax.pmax(jnp.max(row_sums), 'dp')]
    dot_general x6 -> x0, matrix products: 31.1 us -> none  [the longest x2 15 us: kernel_block(): lax.dot_general(left, right, (((1,), (1,)), ((), ())), precision=lax.Prec...]
    psum x1 -> x0, waiting for transfers between devices: 24.2 us -> none  [body(): predictions = lax.psum(partial_pred, 'centre')]
    ppermute x0 -> x21, starting transfers between devices: none -> 22.8 us  [the longest x16 13.6 us: send_xor(): return lax.ppermute(array, 'dp', [(i, i ^ mask) for i in range(count)])]
    ppermute x0 -> x21, waiting for transfers between devices: none -> 20.4 us  [the longest x16 12.9 us: send_xor(): return lax.ppermute(array, 'dp', [(i, i ^ mask) for i in range(count)])]
    pallas_call x0 -> x15, Pallas kernels: none -> 20 us  [call(): pl.pallas_call(kernel, name=name, in_specs=[pl.BlockSpec(memory_space=spa...]
    reduce_scatter x3 -> x0, waiting for transfers between devices: 16.1 us -> none  [the longest x2 13.6 us: project(): lax.psum_scatter(matmul(square, gathered), 'centre', scatter_dimension=0,...]
  transfers between devices with their start and end apart: 4 -> 21, of which waited for: 4 -> 15; matrix products, arithmetic and copies ran while one was open for 4% -> 0% of each run, Pallas kernels for 0% -> 11%
where the time goes in v2:
time: 64.1 us; the launch traced here: 64 us
  starting transfers between devices  22.8 us (36%)
  waiting for transfers between devices  20.4 us (32%)
  Pallas kernels  20 us (31%)
  between operations  0.8 us (1%)
    pallas_call x15, Pallas kernels, call(): pl.pallas_call(kernel, name=name, in_specs=[pl.BlockSpec(memory_space=spa...  20 us
    ppermute x16, starting transfers between devices, send_xor(): return lax.ppermute(array, 'dp', [(i, i ^ mask) for i in range(count)])  13.6 us
    ppermute x16, waiting for transfers between devices, send_xor(): return lax.ppermute(array, 'dp', [(i, i ^ mask) for i in range(count)])  12.9 us
    ppermute x5, starting transfers between devices, send_far(): return lax.ppermute(array, ('dp', 'centre'), pairs)  9.2 us
    ppermute x5, waiting for transfers between devices, send_far(): return lax.ppermute(array, ('dp', 'centre'), pairs)  7.49 us
  transfers between devices with their start and end apart: 21, of which 15 were waited for; matrix products, arithmetic and copies ran while one was open for 0% of the time, Pallas kernels for 11%

profile of v2, /device:TPU:0, one launch (start us, length us, event | category | flops | bytes accessed | tf_op | source)
XLA Modules:
  0.0 64.0 jit_solution(7922008913511836677)
XLA Ops:
  0.6 3.2 %load.1 = (bf16[2048,512]{1,0:T(8,128)(2,1)S(1)}, bf16[2048,512]{1,0:T(8,128)(2,1)S(1)}, f32[2048,1]{1,0:T(8,128)S(1)}, f32[256,512]{1,0:T(8,128)S(1)}) custom-call(f32[2048,512]{1,0:T(8,128)} %c_hbm.1), custom_call_target="tpu_custom_call" | custom-call | tf_op jit(solution)/shard_map/load/pallas_call | solution.py:35
  3.9 6.6 %data.1 = (bf16[2048,512]{1,0:T(8,128)(2,1)S(1)}, bf16[2048,512]{1,0:T(8,128)(2,1)S(1)}, f32[64,512]{1,0:T(8,128)S(1)}) custom-call(f32[512,512]{1,0:T(8,128)S(1)} %copy-done.1, f32[64,2048]{1,0:T(8,128)S(1)} %bitcast.4, bf16[2048,512]{1,0:T(8,128)(2,1)S(1)} %get-tuple-element.44.ch_ref.refs_1_, bf16[2048,512]{1,0:T(8,128)(2,1)S(1)} %get-tuple-element.45.cl_ref.refs_2_, ...), custom_call_target="tpu_custom_call" | custom-call | tf_op jit(solution)/shard_map/data/pallas_call | solution.py:35
  10.5 3.0 %collective-permute-start = (f32[64,512]{1,0:T(8,128)S(1)}, f32[64,512]{1,0:T(8,128)S(1)}, u32[]{:S(2)}, u32[]{:S(2)}) collective-permute-start(f32[64,512]{1,0:T(8,128)S(1)} %get-tuple-element.47.refs_0_), channel_id=1, source_target_pairs={{0,1},{1,0},{2,3},{3,2},{4,5},{5,4},{6,7},{7,6},{8,9},{9,8},{10,11... | collective-permute-start | bytes 393224 | tf_op jit(solution)/shard_map/ppermute | solution.py:294
  13.5 2.5 %own_tile.1 = (bf16[2048,256]{1,0:T(8,128)(2,1)S(1)}, bf16[2048,256]{1,0:T(8,128)(2,1)S(1)}, f32[8,256]{1,0:T(8,128)S(1)}) custom-call(f32[256,512]{1,0:T(8,128)S(1)} %get-tuple-element.61.refs_0_, bf16[2048,512]{1,0:T(8,128)(2,1)S(1)} %get-tuple-element.44.ch_ref.refs_1_, bf16[2048,512]{1,0:T(8,128)(2,1)S(1)} %get-tuple-element.45.cl_ref.refs_2_, ...), custom_call_target="tpu_custom_call" | custom-call | flops 1610612736 | tf_op jit(solution)/shard_map/own_tile/pallas_call | solution.py:35
  16.0 1.0 %collective-permute-done.refs_1_ = f32[64,512]{1,0:T(8,128)S(1)} collective-permute-done((f32[64,512]{1,0:T(8,128)S(1)}, f32[64,512]{1,0:T(8,128)S(1)}, u32[]{:S(2)}, u32[]{:S(2)}) %collective-permute-start) | collective-permute-done | bytes 131104 | tf_op jit(solution)/shard_map/ppermute | solution.py:294
  17.0 1.3 %grad_give.1 = (f32[64,1024]{1,0:T(8,128)S(1)}, f32[64,512]{1,0:T(8,128)}, bf16[512,128]{1,0:T(8,128)(2,1)S(1)}) custom-call(f32[64,512]{1,0:T(8,128)S(1)} %get-tuple-element.47.refs_0_, f32[64,512]{1,0:T(8,128)S(1)} %collective-permute-done.refs_1_, f32[64,512]{1,0:T(8,128)S(1)} %bitcast.6, bf16[2048,512]{1,0:T(8,128)(2,1)S(1)} %get-tuple-element.52.refs_3_.high_ref, ...), custom_call_target="tpu_custom_call" | custom-call | tf_op jit(solution)/shard_map/grad_give/pallas_call | solution.py:35
  18.3 1.7 %collective-permute-start.5 = (f32[256,512]{1,0:T(8,128)S(1)}, f32[256,512]{1,0:T(8,128)S(1)}, u32[]{:S(2)}, u32[]{:S(2)}) collective-permute-start(f32[256,512]{1,0:T(8,128)S(1)} %get-tuple-element.61.refs_0_), channel_id=1, source_target_pairs={{0,1},{1,0},{2,3},{3,2},{4,5},{5,4},{6,7},{7,6},{8,9},{9,8},{10,11... | collective-permute-start | bytes 1572872 | tf_op jit(solution)/shard_map/ppermute | solution.py:294
  20.1 0.8 %grad_keep.1.keep_ref = f32[64,1024]{1,0:T(8,128)S(1)} custom-call(bf16[512,128]{1,0:T(8,128)(2,1)S(1)} %get-tuple-element.55.right_ref, bf16[2048,512]{1,0:T(8,128)(2,1)S(1)} %get-tuple-element.52.refs_3_.high_ref, bf16[2048,512]{1,0:T(8,128)(2,1)S(1)} %get-tuple-element.53.refs_4_.low_ref), custom_call_target="tpu_custom_call" | custom-call | tf_op jit(solution)/shard_map/grad_keep/pallas_call | solution.py:35
  20.9 0.8 %collective-permute-done.1.got_ref = f32[64,1024]{1,0:T(8,128)S(1)} collective-permute-done((f32[64,1024]{1,0:T(8,128)S(1)}, f32[64,1024]{1,0:T(8,128)S(1)}, u32[]{:S(2)}, u32[]{:S(2)}) %collective-permute-start.1) | collective-permute-done | bytes 262176 | tf_op jit(solution)/shard_map/ppermute | solution.py:284
  21.7 2.6 %collective-permute-start.2 = (f32[64,256]{1,0:T(8,128)S(1)}, f32[64,256]{1,0:T(8,128)S(1)}, u32[]{:S(2)}, u32[]{:S(2)}) collective-permute-start(f32[64,256]{1,0:T(8,128)S(1)} %get-tuple-element.58), channel_id=1, source_target_pairs={{0,12},{2,14},{4,8},{6,10},{8,4},{10,6},{12,0},{14,2},{16,28},{18,... | collective-permute-start | bytes 196616 | tf_op jit(solution)/shard_map/ppermute | solution.py:284
  25.2 2.0 %collective-permute-done.2.refs_1_ = f32[64,256]{1,0:T(8,128)S(1)} collective-permute-done((f32[64,256]{1,0:T(8,128)S(1)}, f32[64,256]{1,0:T(8,128)S(1)}, u32[]{:S(2)}, u32[]{:S(2)}) %collective-permute-start.2) | collective-permute-done | bytes 65568 | tf_op jit(solution)/shard_map/ppermute | solution.py:284
  27.2 1.3 %collective-permute-done.3.refs_2_ = f32[64,256]{1,0:T(8,128)S(1)} collective-permute-done((f32[64,256]{1,0:T(8,128)S(1)}, f32[64,256]{1,0:T(8,128)S(1)}, u32[]{:S(2)}, u32[]{:S(2)}) %collective-permute-start.3) | collective-permute-done | bytes 65568 | tf_op jit(solution)/shard_map/ppermute | solution.py:284
  29.0 1.8 %collective-permute-start.11 = (f32[64,256]{1,0:T(8,128)S(1)}, f32[64,256]{1,0:T(8,128)S(1)}, u32[]{:S(2)}, u32[]{:S(2)}) collective-permute-start(f32[64,256]{1,0:T(8,128)S(1)} %sum.1.refs_0_.part_ref), channel_id=1, source_target_pairs={{0,12},{2,14},{4,8},{6,10},{8,4},{10,6},{12,0},{14,2},{16,28},{18,... | collective-permute-start | bytes 196616 | tf_op jit(solution)/shard_map/ppermute | solution.py:284
  31.2 1.3 %collective-permute-start.7 = (f32[64,256]{1,0:T(8,128)S(1)}, f32[64,256]{1,0:T(8,128)S(1)}, u32[]{:S(2)}, u32[]{:S(2)}) collective-permute-start(f32[64,256]{1,0:T(8,128)S(1)} %sum.1.refs_0_.part_ref), channel_id=1, source_target_pairs={{0,4},{2,6},{4,0},{6,2},{8,12},{10,14},{12,8},{14,10},{16,20},{18,... | collective-permute-start | bytes 196616 | tf_op jit(solution)/shard_map/ppermute | solution.py:284
  32.5 2.6 %far_tile.1 = (bf16[2048,256]{1,0:T(8,128)(2,1)S(1)}, bf16[2048,256]{1,0:T(8,128)(2,1)S(1)}, f32[8,256]{1,0:T(8,128)S(1)}) custom-call(f32[256,512]{1,0:T(8,128)S(1)} %collective-permute-done.5.refs_0_, bf16[2048,512]{1,0:T(8,128)(2,1)S(1)} %get-tuple-element.44.ch_ref.refs_1_, bf16[2048,512]{1,0:T(8,128)(2,1)S(1)} %get-tuple-element.45.cl_ref.refs_2_, ...), custom_call_target="tpu_custom_call" | custom-call | flops 1610612736 | tf_op jit(solution)/shard_map/far_tile/pallas_call | solution.py:35
  38.5 2.6 %collective-permute-start.15 = (f32[64,256]{1,0:T(8,128)S(1)}, f32[64,256]{1,0:T(8,128)S(1)}, u32[]{:S(2)}, u32[]{:S(2)}) collective-permute-start(f32[64,256]{1,0:T(8,128)S(1)} %get-tuple-element.75), channel_id=1, source_target_pairs={{0,16},{1,17},{2,18},{3,19},{4,20},{5,21},{6,22},{7,23},{8,24},{9,... | collective-permute-start | bytes 196616 | tf_op jit(solution)/shard_map/ppermute | solution.py:294
  41.1 1.3 %collective-permute-start.14 = (f32[64,256]{1,0:T(8,128)S(1)}, f32[64,256]{1,0:T(8,128)S(1)}, u32[]{:S(2)}, u32[]{:S(2)}) collective-permute-start(f32[64,256]{1,0:T(8,128)S(1)} %get-tuple-element.75), channel_id=1, source_target_pairs={{0,17},{1,16},{2,19},{3,18},{4,21},{5,20},{6,23},{7,22},{8,25},{9,... | collective-permute-start | bytes 196616 | tf_op jit(solution)/shard_map/ppermute | solution.py:294
  42.4 2.7 %collective-permute-done.15.refs_3_ = f32[64,256]{1,0:T(8,128)S(1)} collective-permute-done((f32[64,256]{1,0:T(8,128)S(1)}, f32[64,256]{1,0:T(8,128)S(1)}, u32[]{:S(2)}, u32[]{:S(2)}) %collective-permute-start.15) | collective-permute-done | bytes 65568 | tf_op jit(solution)/shard_map/ppermute | solution.py:294
  45.1 3.7 %collective-permute-done.14.refs_2_ = f32[64,256]{1,0:T(8,128)S(1)} collective-permute-done((f32[64,256]{1,0:T(8,128)S(1)}, f32[64,256]{1,0:T(8,128)S(1)}, u32[]{:S(2)}, u32[]{:S(2)}) %collective-permute-start.14) | collective-permute-done | bytes 65568 | tf_op jit(solution)/shard_map/ppermute | solution.py:294
  50.1 1.1 %collective-permute-done.16.got_ref = f32[72,1024]{1,0:T(8,128)S(1)} collective-permute-done((f32[72,1024]{1,0:T(8,128)S(1)}, f32[72,1024]{1,0:T(8,128)S(1)}, u32[]{:S(2)}, u32[]{:S(2)}) %collective-permute-start.16) | collective-permute-done | bytes 294944 | tf_op jit(solution)/shard_map/ppermute | solution.py:284
  51.9 2.1 %collective-permute-start.18 = (f32[72,256]{1,0:T(8,128)S(1)}, f32[72,256]{1,0:T(8,128)S(1)}, u32[]{:S(2)}, u32[]{:S(2)}) collective-permute-start(f32[72,256]{1,0:T(8,128)S(1)} %get-tuple-element.82), channel_id=1, source_target_pairs={{0,8},{2,10},{4,12},{6,14},{8,0},{10,2},{12,4},{14,6},{16,24},{18,... | collective-permute-start | bytes 221192 | tf_op jit(solution)/shard_map/ppermute | solution.py:284
  54.8 2.6 %collective-permute-done.17.refs_1_ = f32[72,256]{1,0:T(8,128)S(1)} collective-permute-done((f32[72,256]{1,0:T(8,128)S(1)}, f32[72,256]{1,0:T(8,128)S(1)}, u32[]{:S(2)}, u32[]{:S(2)}) %collective-permute-start.17) | collective-permute-done | bytes 73760 | tf_op jit(solution)/shard_map/ppermute | solution.py:284
  58.5 1.9 %collective-permute-start.20 = (f32[64,128]{1,0:T(8,128)S(1)}, f32[64,128]{1,0:T(8,128)S(1)}, u32[]{:S(2)}, u32[]{:S(2)}) collective-permute-start(f32[64,128]{1,0:T(8,128)S(1)} %get-tuple-element.85), channel_id=1, source_target_pairs={{0,16},{2,18},{4,20},{6,22},{8,24},{10,26},{12,28},{14,30},{16,0},... | collective-permute-start | bytes 98312 | tf_op jit(solution)/shard_map/ppermute | solution.py:284
  60.4 3.0 %collective-permute-done.20.got_ref = f32[64,128]{1,0:T(8,128)S(1)} collective-permute-done((f32[64,128]{1,0:T(8,128)S(1)}, f32[64,128]{1,0:T(8,128)S(1)}, u32[]{:S(2)}, u32[]{:S(2)}) %collective-permute-start.20) | collective-permute-done | bytes 32800 | tf_op jit(solution)/shard_map/ppermute | solution.py:284
  (39 shorter events, 9.7 us)
Async XLA Ops:
  0.6 3.3 %copy-start = (f32[2048,64]{0,1:T(8,128)S(1)}, f32[2048,64]{0,1:T(8,128)}, u32[]{:S(2)}) copy-start(f32[2048,64]{0,1:T(8,128)} %param.7) | copy-start | bytes 1572868
  0.6 3.3 %copy-start.1 = (f32[512,512]{1,0:T(8,128)S(1)}, f32[512,512]{1,0:T(8,128)}, u32[]{:S(2)}) copy-start(f32[512,512]{1,0:T(8,128)} %x_ref.1) | copy-start | bytes 3145732
  10.5 6.5 %collective-permute-start = (f32[64,512]{1,0:T(8,128)S(1)}, f32[64,512]{1,0:T(8,128)S(1)}, u32[]{:S(2)}, u32[]{:S(2)}) collective-permute-start(f32[64,512]{1,0:T(8,128)S(1)} %get-tuple-element.47.refs_0_), channel_id=1, source_target_pairs={{0,1},{1,0},{2,3},{3,2},{4,5},{5,4},{6,7},{7,6},{8,9},{9,8},{10,11... | collective-permute-start | bytes 393224 | tf_op jit(solution)/shard_map/ppermute | solution.py:294
  13.5 3.5 %copy-start.2 = (f32[512,64]{0,1:T(8,128)S(1)}, f32[512,64]{0,1:T(8,128)}, u32[]{:S(2)}) copy-start(f32[512,64]{0,1:T(8,128)} %param.5) | copy-start | bytes 393220
  18.3 14.2 %collective-permute-start.5 = (f32[256,512]{1,0:T(8,128)S(1)}, f32[256,512]{1,0:T(8,128)S(1)}, u32[]{:S(2)}, u32[]{:S(2)}) collective-permute-start(f32[256,512]{1,0:T(8,128)S(1)} %get-tuple-element.61.refs_0_), channel_id=1, source_target_pairs={{0,1},{1,0},{2,3},{3,2},{4,5},{5,4},{6,7},{7,6},{8,9},{9,8},{10,11... | collective-permute-start | bytes 1572872 | tf_op jit(solution)/shard_map/ppermute | solution.py:294
  20.1 1.5 %collective-permute-start.1 = (f32[64,1024]{1,0:T(8,128)S(1)}, f32[64,1024]{1,0:T(8,128)S(1)}, u32[]{:S(2)}, u32[]{:S(2)}) collective-permute-start(f32[64,1024]{1,0:T(8,128)S(1)} %get-tuple-element.56), channel_id=1, source_target_pairs={{0,2},{2,0},{4,6},{6,4},{8,10},{10,8},{12,14},{14,12},{16,18},{18,... | collective-permute-start | bytes 786440 | tf_op jit(solution)/shard_map/ppermute | solution.py:284
  21.7 5.5 %collective-permute-start.2 = (f32[64,256]{1,0:T(8,128)S(1)}, f32[64,256]{1,0:T(8,128)S(1)}, u32[]{:S(2)}, u32[]{:S(2)}) collective-permute-start(f32[64,256]{1,0:T(8,128)S(1)} %get-tuple-element.58), channel_id=1, source_target_pairs={{0,12},{2,14},{4,8},{6,10},{8,4},{10,6},{12,0},{14,2},{16,28},{18,... | collective-permute-start | bytes 196616 | tf_op jit(solution)/shard_map/ppermute | solution.py:284
  24.3 4.3 %collective-permute-start.3 = (f32[64,256]{1,0:T(8,128)S(1)}, f32[64,256]{1,0:T(8,128)S(1)}, u32[]{:S(2)}, u32[]{:S(2)}) collective-permute-start(f32[64,256]{1,0:T(8,128)S(1)} %get-tuple-element.59), channel_id=1, source_target_pairs={{0,8},{2,10},{4,12},{6,14},{8,0},{10,2},{12,4},{14,6},{16,24},{18,... | collective-permute-start | bytes 196616 | tf_op jit(solution)/shard_map/ppermute | solution.py:284
  24.7 4.3 %collective-permute-start.4 = (f32[64,256]{1,0:T(8,128)S(1)}, f32[64,256]{1,0:T(8,128)S(1)}, u32[]{:S(2)}, u32[]{:S(2)}) collective-permute-start(f32[64,256]{1,0:T(8,128)S(1)} %get-tuple-element.60), channel_id=1, source_target_pairs={{0,4},{2,6},{4,0},{6,2},{8,12},{10,14},{12,8},{14,10},{16,20},{18,... | collective-permute-start | bytes 196616 | tf_op jit(solution)/shard_map/ppermute | solution.py:284
  29.0 6.2 %collective-permute-start.11 = (f32[64,256]{1,0:T(8,128)S(1)}, f32[64,256]{1,0:T(8,128)S(1)}, u32[]{:S(2)}, u32[]{:S(2)}) collective-permute-start(f32[64,256]{1,0:T(8,128)S(1)} %sum.1.refs_0_.part_ref), channel_id=1, source_target_pairs={{0,12},{2,14},{4,8},{6,10},{8,4},{10,6},{12,0},{14,2},{16,28},{18,... | collective-permute-start | bytes 196616 | tf_op jit(solution)/shard_map/ppermute | solution.py:284
  30.8 4.4 %collective-permute-start.9 = (f32[64,256]{1,0:T(8,128)S(1)}, f32[64,256]{1,0:T(8,128)S(1)}, u32[]{:S(2)}, u32[]{:S(2)}) collective-permute-start(f32[64,256]{1,0:T(8,128)S(1)} %sum.1.refs_0_.part_ref), channel_id=1, source_target_pairs={{0,8},{2,10},{4,12},{6,14},{8,0},{10,2},{12,4},{14,6},{16,24},{18,... | collective-permute-start | bytes 196616 | tf_op jit(solution)/shard_map/ppermute | solution.py:284
  31.2 4.3 %collective-permute-start.7 = (f32[64,256]{1,0:T(8,128)S(1)}, f32[64,256]{1,0:T(8,128)S(1)}, u32[]{:S(2)}, u32[]{:S(2)}) collective-permute-start(f32[64,256]{1,0:T(8,128)S(1)} %sum.1.refs_0_.part_ref), channel_id=1, source_target_pairs={{0,4},{2,6},{4,0},{6,2},{8,12},{10,14},{12,8},{14,10},{16,20},{18,... | collective-permute-start | bytes 196616 | tf_op jit(solution)/shard_map/ppermute | solution.py:284
  35.5 1.5 %collective-permute-start.6 = (f32[64,256]{1,0:T(8,128)S(1)}, f32[64,256]{1,0:T(8,128)S(1)}, u32[]{:S(2)}, u32[]{:S(2)}) collective-permute-start(f32[64,256]{1,0:T(8,128)S(1)} %sum.1.refs_0_.part_ref), channel_id=1, source_target_pairs={{0,2},{2,0},{4,6},{6,4},{8,10},{10,8},{12,14},{14,12},{16,18},{18,... | collective-permute-start | bytes 196616 | tf_op jit(solution)/shard_map/ppermute | solution.py:284
  35.5 1.5 %collective-permute-start.8 = (f32[64,256]{1,0:T(8,128)S(1)}, f32[64,256]{1,0:T(8,128)S(1)}, u32[]{:S(2)}, u32[]{:S(2)}) collective-permute-start(f32[64,256]{1,0:T(8,128)S(1)} %collective-permute-done.7.refs_1_), channel_id=1, source_target_pairs={{0,2},{2,0},{4,6},{6,4},{8,10},{10,8},{12,14},{14,12},{16,18},{18,... | collective-permute-start | bytes 196616 | tf_op jit(solution)/shard_map/ppermute | solution.py:284
  36.0 1.3 %collective-permute-start.10 = (f32[64,256]{1,0:T(8,128)S(1)}, f32[64,256]{1,0:T(8,128)S(1)}, u32[]{:S(2)}, u32[]{:S(2)}) collective-permute-start(f32[64,256]{1,0:T(8,128)S(1)} %collective-permute-done.9.refs_2_), channel_id=1, source_target_pairs={{0,2},{2,0},{4,6},{6,4},{8,10},{10,8},{12,14},{14,12},{16,18},{18,... | collective-permute-start | bytes 196616 | tf_op jit(solution)/shard_map/ppermute | solution.py:284
  36.0 1.4 %collective-permute-start.12 = (f32[64,256]{1,0:T(8,128)S(1)}, f32[64,256]{1,0:T(8,128)S(1)}, u32[]{:S(2)}, u32[]{:S(2)}) collective-permute-start(f32[64,256]{1,0:T(8,128)S(1)} %collective-permute-done.11.refs_3_), channel_id=1, source_target_pairs={{0,2},{2,0},{4,6},{6,4},{8,10},{10,8},{12,14},{14,12},{16,18},{18,... | collective-permute-start | bytes 196616 | tf_op jit(solution)/shard_map/ppermute | solution.py:284
  37.9 10.9 %collective-permute-start.13 = (f32[72,256]{1,0:T(8,128)S(1)}, f32[72,256]{1,0:T(8,128)S(1)}, u32[]{:S(2)}, u32[]{:S(2)}) collective-permute-start(f32[72,256]{1,0:T(8,128)S(1)} %get-tuple-element.74.refs_0_), channel_id=1, source_target_pairs={{0,1},{1,0},{2,3},{3,2},{4,5},{5,4},{6,7},{7,6},{8,9},{9,8},{10,11... | collective-permute-start | bytes 221192 | tf_op jit(solution)/shard_map/ppermute | solution.py:294
  38.5 6.6 %collective-permute-start.15 = (f32[64,256]{1,0:T(8,128)S(1)}, f32[64,256]{1,0:T(8,128)S(1)}, u32[]{:S(2)}, u32[]{:S(2)}) collective-permute-start(f32[64,256]{1,0:T(8,128)S(1)} %get-tuple-element.75), channel_id=1, source_target_pairs={{0,16},{1,17},{2,18},{3,19},{4,20},{5,21},{6,22},{7,23},{8,24},{9,... | collective-permute-start | bytes 196616 | tf_op jit(solution)/shard_map/ppermute | solution.py:294
  41.1 7.7 %collective-permute-start.14 = (f32[64,256]{1,0:T(8,128)S(1)}, f32[64,256]{1,0:T(8,128)S(1)}, u32[]{:S(2)}, u32[]{:S(2)}) collective-permute-start(f32[64,256]{1,0:T(8,128)S(1)} %get-tuple-element.75), channel_id=1, source_target_pairs={{0,17},{1,16},{2,19},{3,18},{4,21},{5,20},{6,23},{7,22},{8,25},{9,... | collective-permute-start | bytes 196616 | tf_op jit(solution)/shard_map/ppermute | solution.py:294
  49.5 1.6 %collective-permute-start.16 = (f32[72,1024]{1,0:T(8,128)S(1)}, f32[72,1024]{1,0:T(8,128)S(1)}, u32[]{:S(2)}, u32[]{:S(2)}) collective-permute-start(f32[72,1024]{1,0:T(8,128)S(1)} %get-tuple-element.78), channel_id=1, source_target_pairs={{0,2},{2,0},{4,6},{6,4},{8,10},{10,8},{12,14},{14,12},{16,18},{18,... | collective-permute-start | bytes 884744 | tf_op jit(solution)/shard_map/ppermute | solution.py:284
  51.2 6.1 %collective-permute-start.17 = (f32[72,256]{1,0:T(8,128)S(1)}, f32[72,256]{1,0:T(8,128)S(1)}, u32[]{:S(2)}, u32[]{:S(2)}) collective-permute-start(f32[72,256]{1,0:T(8,128)S(1)} %get-tuple-element.81), channel_id=1, source_target_pairs={{0,12},{2,14},{4,8},{6,10},{8,4},{10,6},{12,0},{14,2},{16,28},{18,... | collective-permute-start | bytes 221192 | tf_op jit(solution)/shard_map/ppermute | solution.py:284
  51.9 6.0 %collective-permute-start.18 = (f32[72,256]{1,0:T(8,128)S(1)}, f32[72,256]{1,0:T(8,128)S(1)}, u32[]{:S(2)}, u32[]{:S(2)}) collective-permute-start(f32[72,256]{1,0:T(8,128)S(1)} %get-tuple-element.82), channel_id=1, source_target_pairs={{0,8},{2,10},{4,12},{6,14},{8,0},{10,2},{12,4},{14,6},{16,24},{18,... | collective-permute-start | bytes 221192 | tf_op jit(solution)/shard_map/ppermute | solution.py:284
  54.1 4.4 %collective-permute-start.19 = (f32[72,256]{1,0:T(8,128)S(1)}, f32[72,256]{1,0:T(8,128)S(1)}, u32[]{:S(2)}, u32[]{:S(2)}) collective-permute-start(f32[72,256]{1,0:T(8,128)S(1)} %get-tuple-element.83), channel_id=1, source_target_pairs={{0,4},{2,6},{4,0},{6,2},{8,12},{10,14},{12,8},{14,10},{16,20},{18,... | collective-permute-start | bytes 221192 | tf_op jit(solution)/shard_map/ppermute | solution.py:284
  58.5 4.9 %collective-permute-start.20 = (f32[64,128]{1,0:T(8,128)S(1)}, f32[64,128]{1,0:T(8,128)S(1)}, u32[]{:S(2)}, u32[]{:S(2)}) collective-permute-start(f32[64,128]{1,0:T(8,128)S(1)} %get-tuple-element.85), channel_id=1, source_target_pairs={{0,16},{2,18},{4,20},{6,22},{8,24},{10,26},{12,28},{14,30},{16,0},... | collective-permute-start | bytes 98312 | tf_op jit(solution)/shard_map/ppermute | solution.py:284

commit v3 on v2

--- a/solution.py
+++ b/solution.py
@@ -121,26 +121,25 @@
         sum_ref[:, span] = total
 
 
-def share_rows(mids, share, flip):
+def share_rows(mids, share, flip, tops=(0, 1)):
     _, core, mid, _ = place()
     for m in range(mids):
-        for top in range(2):
+        for top in tops:
             block = top * 2 * mids + 2 * (mid ^ m) + (core ^ flip)
             yield pl.ds(pl.multiple_of(block * share, share), share)
 
 
-def take(ref, where, columns=slice(None)):
-    return jnp.concatenate([ref[rows, columns] for rows in where], axis=0)
-
-
-def back(mids, share, flip, parts, right):
-    where = list(share_rows(mids, share, flip))
+def take(ref, where):
+    return jnp.concatenate([ref[rows, :] for rows in where], axis=0)
+
+
+def back(where, parts, right):
+    where = list(where)
     product, at = 0.0, 0
-    for high, low, columns in parts:
-        size = columns.stop - columns.start
-        values = right[at : at + size]
-        at += size
-        product = product + (dot(take(high, where, columns), values) + dot(take(low, where, columns), values))
+    for high, low in parts:
+        values = right[at : at + high.shape[1]]
+        at += high.shape[1]
+        product = product + (dot(take(high, where), values) + dot(take(low, where), values))
     product = product.T
     outs = right.shape[1] // 2
     return product[:outs] + product[outs:]
@@ -155,46 +154,37 @@
     res_ref[...] = residual
     right = jnp.concatenate(split(residual.T), axis=1)
     right_ref[...] = right
-    out_ref[...] = back(mids, share, 1, [(high_ref, low_ref, slice(0, right.shape[0]))], right)
+    out_ref[...] = back(share_rows(mids, share, 1), [(high_ref, low_ref)], right)
 
 
 def grad_keep_kernel(mids, share, right_ref, high_ref, low_ref, out_ref):
     right = right_ref[...]
-    out_ref[...] = back(mids, share, 0, [(high_ref, low_ref, slice(0, right.shape[0]))], right)
-
-
-def near_parts(share, own_high, own_low, far_high, far_low):
-    parts = [(own_high, own_low, slice(0, share))]
-    for at in range(0, far_high.shape[1], 2 * share):
-        parts.append((far_high, far_low, slice(at, at + share)))
-    return parts
-
-
-def image_kernel(mids, shards, *refs):
-    near_refs, away_refs = refs[:shards], refs[shards : 2 * shards]
-    kernels = refs[2 * shards : 2 * shards + 4]
-    out_ref, right_ref, own_ref, max_ref, image_ref = refs[2 * shards + 4 :]
-    outs, share = own_ref.shape
-    total = near_refs[0][...]
-    for ref in near_refs[1:]:
+    out_ref[...] = back(share_rows(mids, share, 0), [(high_ref, low_ref)], right)
+
+
+def image_kernel(mids, share, shards, *refs):
+    kernels = refs[shards : shards + 4]
+    out_ref, right_ref, own_ref, max_ref, image_ref = refs[shards + 4 :]
+    outs, size = own_ref.shape[0], 2 * share
+    total = refs[0][...]
+    for ref in refs[1:shards]:
         total = total + ref[...]
-    image = total[:outs]
-    for ref in away_refs:
-        image = image + ref[...]
-    largest = jnp.max(total[outs : outs + 2], keepdims=True)
+    largest = jnp.max(total[outs : outs + 1], keepdims=True)
     max_ref[...] = jnp.broadcast_to(largest, max_ref.shape)
     out_ref[outs:, :] = jnp.broadcast_to(largest, (8, out_ref.shape[1]))
-    image_ref[...] = image
+    image_ref[...] = total[:outs]
     for j in range(shards):
-        part = image_ref[:, pl.ds(shard_at(j, shards, share), share)]
-        right_ref[j * share : (j + 1) * share, :] = jnp.concatenate(split(part.T), axis=1)
+        part = image_ref[:, pl.ds(shard_at(j, shards, size), size)]
+        right_ref[j * size : (j + 1) * size, :] = jnp.concatenate(split(part.T), axis=1)
         if j == 0:
-            own_ref[...] = part
-    out_ref[:outs, :] = back(mids, share, 1, near_parts(share, *kernels), right_ref[...])
+            own_ref[...] = part[:, :share]
+    where = share_rows(mids, share, 1, [place()[3]])
+    out_ref[:outs, :] = back(where, [kernels[:2], kernels[2:]], right_ref[...])
 
 
 def image_keep_kernel(mids, share, right_ref, *refs):
-    refs[-1][...] = back(mids, share, 0, near_parts(share, *refs[:4]), right_ref[...])
+    where = share_rows(mids, share, 0, [place()[3]])
+    refs[-1][...] = back(where, [refs[:2], refs[2:4]], right_ref[...])
 
 
 def shard_at(j, shards, share):
@@ -218,22 +208,21 @@
     far_ref[...] = far
 
 
-def second_kernel(mids, shards, *refs):
-    own_ref, far_ref, osum, fsum, near_ref, away_ref = refs[mids + 4 :]
-    outs = away_ref.shape[0]
-    share = away_ref.shape[1] // shards
-    own, far = product(mids, share, 1, refs[:mids], refs[mids : mids + 4])
+def second_kernel(mids, share, shards, *refs):
+    own_ref, far_ref, osum, fsum, out_ref = refs[-5:]
+    outs, size = own_ref.shape[0], 2 * share
+    own, far = product(mids, share, 1, refs[:-9], refs[-9:-5])
     own, far = own + own_ref[...], far + far_ref[...]
-    row = lax.broadcasted_iota(jnp.int32, (8, share), 0)
     for j in range(shards):
-        source, sums, at = (own, osum, 0) if j == 0 else (far, fsum, 2 * share * (j - 1))
-        where = pl.ds(shard_at(j, shards, share), share)
-        first, last = slice(at, at + share), slice(at + share, at + 2 * share)
-        near_ref[:outs, where] = source[:, first]
-        away_ref[:, where] = source[:, last]
-        near_sum = jnp.sum(sums[:, first], axis=0, keepdims=True)
-        away_sum = jnp.sum(sums[:, last], axis=0, keepdims=True)
-        near_ref[outs:, where] = jnp.where(row == 0, near_sum, away_sum)
+        source, sums, at = (own, osum, 0) if j == 0 else (far, fsum, size * (j - 1))
+        where = pl.ds(shard_at(j, shards, size), size)
+        out_ref[:outs, where] = source[:, at : at + size]
+        row_sums = jnp.sum(sums[:, at : at + size], axis=0, keepdims=True)
+        out_ref[outs:, where] = jnp.broadcast_to(row_sums, (8, size))
+
+
+def pack_kernel(*refs):
+    refs[-1][...] = jnp.concatenate([ref[...] for ref in refs[:-1]], axis=1)
 
 
 def join_kernel(mids, keep_ref, got_ref, *refs):
@@ -256,27 +245,20 @@
     refs[-1][...] = total
 
 
-def theta_kernel(mids, share, part_ref, own_ref, *refs):
-    pieces = refs[:mids]
-    keep_ref, give_ref = refs[mids:]
-    outs = part_ref.shape[0]
+def final_kernel(mids, whole_ref, own_ref, coeff_ref, *refs):
+    pieces, out_ref = refs[:mids], refs[mids]
+    outs, share = out_ref.shape
     second = pieces[0][:outs, :]
     largest = pieces[0][outs:, :]
     for ref in pieces[1:]:
         second = second + ref[:outs, :]
         largest = jnp.maximum(largest, ref[outs:, :])
     step = 1.0 / largest[:1, :1]
-    theta = (3.0 * step) * part_ref[...] + (step * step * step) * second
-    first, last = theta[:, :share], theta[:, share:]
-    upper = place()[3] == 1
-    keep_ref[...] = jnp.where(upper, last, first) - (3.0 * step * step) * own_ref[...]
-    give_ref[...] = jnp.where(upper, first, last)
-
-
-def final_kernel(keep_ref, got_ref, coeff_ref, out_ref):
-    share = out_ref.shape[1]
-    coefficients = coeff_ref[:, pl.ds(pl.multiple_of(place()[0] * share, share), share)]
-    out_ref[...] = coefficients - learning_rate * (keep_ref[...] + got_ref[...])
+    index, _, _, top = place()
+    gradient = jnp.where(top == 1, whole_ref[:, share:], whole_ref[:, :share])
+    theta = 3.0 * step * (gradient - step * own_ref[...]) + (step * step * step) * second
+    coefficients = coeff_ref[:, pl.ds(pl.multiple_of(index * share, share), share)]
+    out_ref[...] = coefficients - learning_rate * theta
 
 
 def send_xor(array, mask):
@@ -348,7 +330,6 @@
         [like(outs, half * share), like(outs, points), like(points, 2 * outs, dtype=bf16)],
     )
     received = send_xor(give, 1)
-    far = [send_far(after(pair, give), 0, -shift) for shift in range(1, shards)]
     (keep,) = call(
         functools.partial(grad_keep_kernel, mids, share), "grad_keep",
         [right, kh, kl], [like(outs, half * share)],
@@ -357,53 +338,57 @@
     def join(keep, received, extra, height):
         return call(
             functools.partial(join_kernel, mids), "join",
-            [keep, received] + extra, [like(height, 2 * share)] * mids,
+            [keep, received] + extra, [like(height, keep.shape[1] // mids)] * mids,
         )
 
-    pieces = join(keep, received, [], outs)
-    pieces = [pieces[0]] + [send_xor(pieces[m], 2 * m) for m in range(mids - 1, 0, -1)]
-    (part,) = call(sum_kernel, "sum", pieces, [like(outs, 2 * share)])
-    gathered = [part] + [send_xor(part, 2 * m) for m in range(1, mids)]
-    far_high, far_low, far_sums = centre_tile([after(f, part) for f in far], "far_tile")
+    def total(arrays):
+        return call(sum_kernel, "sum", arrays, [like(*arrays[0].shape)])[0]
+
+    def spread(pieces):
+        sent = [send_xor(pieces[m], 2 * m) for m in range(mids - 1, 0, -1)]
+        return [pieces[0]] + sent[::-1]
+
+    pieces = spread(join(keep, received, [], outs))
+    far = [send_far(after(pair, received, keep), 0, -shift) for shift in range(1, shards)]
+    part = total(pieces)
+    whole = total([part, send_xor(part, half)])
+    gathered = spread([whole] * mids)
+    far_high, far_low, far_sums = centre_tile([after(f, whole) for f in far], "far_tile")
     kernels = [own_high, own_low, far_high, far_low]
-    crossed = [send_xor(after(piece, far_sums), 1) for piece in gathered]
     wide = 2 * share * (shards - 1)
+    packed = call(
+        pack_kernel, "pack", [after(whole, far_sums)] + gathered[1:], [like(outs, 2 * share * mids)]
+    )[0]
+    crossed = [send_xor(packed, 1)]
     firsts = call(
         functools.partial(first_kernel, mids, share), "product_first",
         gathered + kernels, [like(outs, 2 * share), like(outs, wide)],
     )
-    near_part, away_part = call(
-        functools.partial(second_kernel, mids, shards), "product_second",
+    (image,) = call(
+        functools.partial(second_kernel, mids, share, shards), "product_second",
         crossed + kernels + list(firsts) + [own_sums, far_sums],
-        [like(outs + 8, shards * share), like(outs, shards * share)],
-    )
-    aways = [send_far(away_part, half, shift) for shift in range(shards - 1, -1, -1)]
-    nears = [near_part] + [send_far(near_part, 0, shift) for shift in range(1, shards)]
-
+        [like(outs + 8, 2 * share * shards)],
+    )
+    images = [image] + [send_far(image, 0, shift) for shift in range(1, shards)]
     give, right, own, largest = call(
-        functools.partial(image_kernel, mids, shards), "image_give",
-        nears + aways + kernels,
+        functools.partial(image_kernel, mids, share, shards), "image_give",
+        images + kernels,
         [
-            like(outs + 8, half * share),
-            like(shards * share, 2 * outs, dtype=bf16),
+            like(outs + 8, mids * share),
+            like(2 * share * shards, 2 * outs, dtype=bf16),
             like(outs, share),
             like(8, share),
         ],
-        [pltpu.VMEM((outs, shards * share), f32)],
+        [pltpu.VMEM((outs, 2 * share * shards), f32)],
     )
     received = send_xor(give, 1)
     (keep,) = call(
         functools.partial(image_keep_kernel, mids, share), "image_keep",
-        [right] + kernels, [like(outs, half * share)],
-    )
-    pieces = join(keep, received, [largest], outs + 8)
-    pieces = [pieces[0]] + [send_xor(pieces[m], 2 * m) for m in range(mids - 1, 0, -1)]
-    keep, give = call(
-        functools.partial(theta_kernel, mids, share), "theta",
-        [part, own] + pieces, [like(outs, share)] * 2,
-    )
+        [right] + kernels, [like(outs, mids * share)],
+    )
+    pieces = spread(join(keep, received, [largest], outs + 8))
     (new_coefficients,) = call(
-        final_kernel, "final", [keep, send_xor(give, half), weights], [like(outs, share)]
+        functools.partial(final_kernel, mids), "final", [whole, own, weights] + pieces, [like(outs, share)]
     )
     return (residual.T, new_coefficients.T)
 

time: 64.1 us -> 59.7 us (0.931)
  starting transfers between devices: 22.8 us -> 18.7 us
    ppermute x5 -> x3, starting transfers between devices: 9.2 us -> 5.32 us  [send_far(): return lax.ppermute(array, ('dp', 'centre'), pairs)]
    ppermute x5 -> x3, waiting for transfers between devices: 7.49 us -> 6.41 us  [send_far(): return lax.ppermute(array, ('dp', 'centre'), pairs)]
    ppermute x16 -> x13, waiting for transfers between devices: 12.9 us -> 13.5 us  [send_xor(): return lax.ppermute(array, 'dp', [(i, i ^ mask) for i in range(count)])]
    ppermute x16 -> x13, starting transfers between devices: 13.6 us -> 13.4 us  [send_xor(): return lax.ppermute(array, 'dp', [(i, i ^ mask) for i in range(count)])]
    pallas_call x15 -> x16, Pallas kernels: 20 us -> 20 us  [call(): pl.pallas_call(kernel, name=name, in_specs=[pl.BlockSpec(memory_space=spa...]
  transfers between devices with their start and end apart: 21 -> 16, of which waited for: 15 -> 13; matrix products, arithmetic and copies ran while one was open for 0% -> 0% of each run, Pallas kernels for 11% -> 12%
where the time goes in v3:
time: 59.7 us; the launch traced here: 59.5 us
  Pallas kernels  20 us (34%)
  waiting for transfers between devices  19.9 us (33%)
  starting transfers between devices  18.7 us (31%)
  between operations  0.79 us (1%)
    pallas_call x16, Pallas kernels, call(): pl.pallas_call(kernel, name=name, in_specs=[pl.BlockSpec(memory_space=spa...  20 us
    ppermute x13, waiting for transfers between devices, send_xor(): return lax.ppermute(array, 'dp', [(i, i ^ mask) for i in range(count)])  13.5 us
    ppermute x13, starting transfers between devices, send_xor(): return lax.ppermute(array, 'dp', [(i, i ^ mask) for i in range(count)])  13.4 us
    ppermute x3, waiting for transfers between devices, send_far(): return lax.ppermute(array, ('dp', 'centre'), pairs)  6.41 us
    ppermute x3, starting transfers between devices, send_far(): return lax.ppermute(array, ('dp', 'centre'), pairs)  5.32 us
  transfers between devices with their start and end apart: 16, of which 13 were waited for; matrix products, arithmetic and copies ran while one was open for 0% of the time, Pallas kernels for 12%

profile of v3, /device:TPU:0, one launch (start us, length us, event | category | flops | bytes accessed | tf_op | source)
XLA Modules:
  0.0 59.5 jit_solution(4810708310630018062)
XLA Ops:
  0.6 3.2 %load.1 = (bf16[2048,512]{1,0:T(8,128)(2,1)S(1)}, bf16[2048,512]{1,0:T(8,128)(2,1)S(1)}, f32[2048,1]{1,0:T(8,128)S(1)}, f32[256,512]{1,0:T(8,128)S(1)}) custom-call(f32[2048,512]{1,0:T(8,128)} %c_hbm.1), custom_call_target="tpu_custom_call" | custom-call | tf_op jit(solution)/shard_map/load/pallas_call | solution.py:35
  3.9 6.6 %data.1 = (bf16[2048,512]{1,0:T(8,128)(2,1)S(1)}, bf16[2048,512]{1,0:T(8,128)(2,1)S(1)}, f32[64,512]{1,0:T(8,128)S(1)}) custom-call(f32[512,512]{1,0:T(8,128)S(1)} %copy-done.1, f32[64,2048]{1,0:T(8,128)S(1)} %bitcast.4, bf16[2048,512]{1,0:T(8,128)(2,1)S(1)} %get-tuple-element.37.ch_ref.refs_1_, bf16[2048,512]{1,0:T(8,128)(2,1)S(1)} %get-tuple-element.38.cl_ref.refs_2_, ...), custom_call_target="tpu_custom_call" | custom-call | tf_op jit(solution)/shard_map/data/pallas_call | solution.py:35
  10.5 3.0 %collective-permute-start = (f32[64,512]{1,0:T(8,128)S(1)}, f32[64,512]{1,0:T(8,128)S(1)}, u32[]{:S(2)}, u32[]{:S(2)}) collective-permute-start(f32[64,512]{1,0:T(8,128)S(1)} %get-tuple-element.40.refs_0_), channel_id=1, source_target_pairs={{0,1},{1,0},{2,3},{3,2},{4,5},{5,4},{6,7},{7,6},{8,9},{9,8},{10,11... | collective-permute-start | bytes 393224 | tf_op jit(solution)/shard_map/ppermute | solution.py:276
  13.5 2.5 %own_tile.1 = (bf16[2048,256]{1,0:T(8,128)(2,1)S(1)}, bf16[2048,256]{1,0:T(8,128)(2,1)S(1)}, f32[8,256]{1,0:T(8,128)S(1)}) custom-call(f32[256,512]{1,0:T(8,128)S(1)} %get-tuple-element.54.refs_0_, bf16[2048,512]{1,0:T(8,128)(2,1)S(1)} %get-tuple-element.37.ch_ref.refs_1_, bf16[2048,512]{1,0:T(8,128)(2,1)S(1)} %get-tuple-element.38.cl_ref.refs_2_, ...), custom_call_target="tpu_custom_call" | custom-call | flops 1610612736 | tf_op jit(solution)/shard_map/own_tile/pallas_call | solution.py:35
  16.0 1.0 %collective-permute-done.refs_1_ = f32[64,512]{1,0:T(8,128)S(1)} collective-permute-done((f32[64,512]{1,0:T(8,128)S(1)}, f32[64,512]{1,0:T(8,128)S(1)}, u32[]{:S(2)}, u32[]{:S(2)}) %collective-permute-start) | collective-permute-done | bytes 131104 | tf_op jit(solution)/shard_map/ppermute | solution.py:276
  17.0 1.3 %grad_give.1 = (f32[64,1024]{1,0:T(8,128)S(1)}, f32[64,512]{1,0:T(8,128)}, bf16[512,128]{1,0:T(8,128)(2,1)S(1)}) custom-call(f32[64,512]{1,0:T(8,128)S(1)} %get-tuple-element.40.refs_0_, f32[64,512]{1,0:T(8,128)S(1)} %collective-permute-done.refs_1_, f32[64,512]{1,0:T(8,128)S(1)} %bitcast.6, bf16[2048,512]{1,0:T(8,128)(2,1)S(1)} %get-tuple-element.45.refs_3_.high_ref, ...), custom_call_target="tpu_custom_call" | custom-call | tf_op jit(solution)/shard_map/grad_give/pallas_call | solution.py:35
  19.9 1.7 %collective-permute-start.6 = (f32[256,512]{1,0:T(8,128)S(1)}, f32[256,512]{1,0:T(8,128)S(1)}, u32[]{:S(2)}, u32[]{:S(2)}) collective-permute-start(f32[256,512]{1,0:T(8,128)S(1)} %get-tuple-element.54.refs_0_), channel_id=1, source_target_pairs={{0,1},{1,0},{2,3},{3,2},{4,5},{5,4},{6,7},{7,6},{8,9},{9,8},{10,11... | collective-permute-start | bytes 1572872 | tf_op jit(solution)/shard_map/ppermute | solution.py:276
  21.7 1.6 %collective-permute-start.2 = (f32[64,256]{1,0:T(8,128)S(1)}, f32[64,256]{1,0:T(8,128)S(1)}, u32[]{:S(2)}, u32[]{:S(2)}) collective-permute-start(f32[64,256]{1,0:T(8,128)S(1)} %get-tuple-element.51), channel_id=1, source_target_pairs={{0,4},{2,6},{4,0},{6,2},{8,12},{10,14},{12,8},{14,10},{16,20},{18,... | collective-permute-start | bytes 196616 | tf_op jit(solution)/shard_map/ppermute | solution.py:266
  23.2 1.6 %collective-permute-start.3 = (f32[64,256]{1,0:T(8,128)S(1)}, f32[64,256]{1,0:T(8,128)S(1)}, u32[]{:S(2)}, u32[]{:S(2)}) collective-permute-start(f32[64,256]{1,0:T(8,128)S(1)} %get-tuple-element.52), channel_id=1, source_target_pairs={{0,8},{2,10},{4,12},{6,14},{8,0},{10,2},{12,4},{14,6},{16,24},{18,... | collective-permute-start | bytes 196616 | tf_op jit(solution)/shard_map/ppermute | solution.py:266
  25.2 0.8 %collective-permute-done.2.refs_1_ = f32[64,256]{1,0:T(8,128)S(1)} collective-permute-done((f32[64,256]{1,0:T(8,128)S(1)}, f32[64,256]{1,0:T(8,128)S(1)}, u32[]{:S(2)}, u32[]{:S(2)}) %collective-permute-start.2) | collective-permute-done | bytes 65568 | tf_op jit(solution)/shard_map/ppermute | solution.py:266
  26.0 2.1 %collective-permute-done.3.refs_2_ = f32[64,256]{1,0:T(8,128)S(1)} collective-permute-done((f32[64,256]{1,0:T(8,128)S(1)}, f32[64,256]{1,0:T(8,128)S(1)}, u32[]{:S(2)}, u32[]{:S(2)}) %collective-permute-start.3) | collective-permute-done | bytes 65568 | tf_op jit(solution)/shard_map/ppermute | solution.py:266
  28.1 1.9 %collective-permute-done.4.refs_3_ = f32[64,256]{1,0:T(8,128)S(1)} collective-permute-done((f32[64,256]{1,0:T(8,128)S(1)}, f32[64,256]{1,0:T(8,128)S(1)}, u32[]{:S(2)}, u32[]{:S(2)}) %collective-permute-start.4) | collective-permute-done | bytes 65568 | tf_op jit(solution)/shard_map/ppermute | solution.py:266
  30.0 2.6 %collective-permute-start.5 = (f32[64,256]{1,0:T(8,128)S(1)}, f32[64,256]{1,0:T(8,128)S(1)}, u32[]{:S(2)}, u32[]{:S(2)}) collective-permute-start(f32[64,256]{1,0:T(8,128)S(1)} %sum.2.refs_0_), channel_id=1, source_target_pairs={{0,16},{2,18},{4,20},{6,22},{8,24},{10,26},{12,28},{14,30},{16,0},... | collective-permute-start | bytes 196616 | tf_op jit(solution)/shard_map/ppermute | solution.py:266
  32.7 3.2 %collective-permute-done.5.refs_1_ = f32[64,256]{1,0:T(8,128)S(1)} collective-permute-done((f32[64,256]{1,0:T(8,128)S(1)}, f32[64,256]{1,0:T(8,128)S(1)}, u32[]{:S(2)}, u32[]{:S(2)}) %collective-permute-start.5) | collective-permute-done | bytes 65568 | tf_op jit(solution)/shard_map/ppermute | solution.py:266
  36.1 1.9 %collective-permute-start.8 = (f32[64,256]{1,0:T(8,128)S(1)}, f32[64,256]{1,0:T(8,128)S(1)}, u32[]{:S(2)}, u32[]{:S(2)}) collective-permute-start(f32[64,256]{1,0:T(8,128)S(1)} %sum.3.refs_0_.whole_ref), channel_id=1, source_target_pairs={{0,8},{2,10},{4,12},{6,14},{8,0},{10,2},{12,4},{14,6},{16,24},{18,... | collective-permute-start | bytes 196616 | tf_op jit(solution)/shard_map/ppermute | solution.py:266
  38.0 1.4 %collective-permute-start.7 = (f32[64,256]{1,0:T(8,128)S(1)}, f32[64,256]{1,0:T(8,128)S(1)}, u32[]{:S(2)}, u32[]{:S(2)}) collective-permute-start(f32[64,256]{1,0:T(8,128)S(1)} %sum.3.refs_0_.whole_ref), channel_id=1, source_target_pairs={{0,4},{2,6},{4,0},{6,2},{8,12},{10,14},{12,8},{14,10},{16,20},{18,... | collective-permute-start | bytes 196616 | tf_op jit(solution)/shard_map/ppermute | solution.py:266
  39.4 2.6 %far_tile.1 = (bf16[2048,256]{1,0:T(8,128)(2,1)S(1)}, bf16[2048,256]{1,0:T(8,128)(2,1)S(1)}, f32[8,256]{1,0:T(8,128)S(1)}) custom-call(f32[256,512]{1,0:T(8,128)S(1)} %collective-permute-done.6.refs_0_, bf16[2048,512]{1,0:T(8,128)(2,1)S(1)} %get-tuple-element.37.ch_ref.refs_1_, bf16[2048,512]{1,0:T(8,128)(2,1)S(1)} %get-tuple-element.38.cl_ref.refs_2_, ...), custom_call_target="tpu_custom_call" | custom-call | flops 1610612736 | tf_op jit(solution)/shard_map/far_tile/pallas_call | solution.py:35
  42.8 1.0 %collective-permute-done.10.refs_0_ = f32[64,1024]{1,0:T(8,128)S(1)} collective-permute-done((f32[64,1024]{1,0:T(8,128)S(1)}, f32[64,1024]{1,0:T(8,128)S(1)}, u32[]{:S(2)}, u32[]{:S(2)}) %collective-permute-start.10) | collective-permute-done | bytes 262176 | tf_op jit(solution)/shard_map/ppermute | solution.py:266
  44.9 5.4 %collective-permute-done.11.refs_1_ = f32[72,512]{1,0:T(8,128)S(1)} collective-permute-done((f32[72,512]{1,0:T(8,128)S(1)}, f32[72,512]{1,0:T(8,128)S(1)}, u32[]{:S(2)}, u32[]{:S(2)}) %collective-permute-start.11) | collective-permute-done | bytes 147488 | tf_op jit(solution)/shard_map/ppermute | solution.py:276
  51.7 0.8 %collective-permute-done.12.got_ref = f32[72,512]{1,0:T(8,128)S(1)} collective-permute-done((f32[72,512]{1,0:T(8,128)S(1)}, f32[72,512]{1,0:T(8,128)S(1)}, u32[]{:S(2)}, u32[]{:S(2)}) %collective-permute-start.12) | collective-permute-done | bytes 147488 | tf_op jit(solution)/shard_map/ppermute | solution.py:266
  52.6 1.4 %collective-permute-start.13 = (f32[72,128]{1,0:T(8,128)S(1)}, f32[72,128]{1,0:T(8,128)S(1)}, u32[]{:S(2)}, u32[]{:S(2)}) collective-permute-start(f32[72,128]{1,0:T(8,128)S(1)} %get-tuple-element.69), channel_id=1, source_target_pairs={{0,4},{2,6},{4,0},{6,2},{8,12},{10,14},{12,8},{14,10},{16,20},{18,... | collective-permute-start | bytes 110600 | tf_op jit(solution)/shard_map/ppermute | solution.py:266
  54.0 2.1 %collective-permute-start.15 = (f32[72,128]{1,0:T(8,128)S(1)}, f32[72,128]{1,0:T(8,128)S(1)}, u32[]{:S(2)}, u32[]{:S(2)}) collective-permute-start(f32[72,128]{1,0:T(8,128)S(1)} %get-tuple-element.71), channel_id=1, source_target_pairs={{0,12},{2,14},{4,8},{6,10},{8,4},{10,6},{12,0},{14,2},{16,28},{18,... | collective-permute-start | bytes 110600 | tf_op jit(solution)/shard_map/ppermute | solution.py:266
  56.5 1.4 %collective-permute-done.14.refs_2_ = f32[72,128]{1,0:T(8,128)S(1)} collective-permute-done((f32[72,128]{1,0:T(8,128)S(1)}, f32[72,128]{1,0:T(8,128)S(1)}, u32[]{:S(2)}, u32[]{:S(2)}) %collective-permute-start.14) | collective-permute-done | bytes 36896 | tf_op jit(solution)/shard_map/ppermute | solution.py:266
  57.9 0.9 %collective-permute-done.15.refs_3_ = f32[72,128]{1,0:T(8,128)S(1)} collective-permute-done((f32[72,128]{1,0:T(8,128)S(1)}, f32[72,128]{1,0:T(8,128)S(1)}, u32[]{:S(2)}, u32[]{:S(2)}) %collective-permute-start.15) | collective-permute-done | bytes 36896 | tf_op jit(solution)/shard_map/ppermute | solution.py:266
  (30 shorter events, 6.6 us)
Async XLA Ops:
  0.6 3.3 %copy-start = (f32[2048,64]{0,1:T(8,128)S(1)}, f32[2048,64]{0,1:T(8,128)}, u32[]{:S(2)}) copy-start(f32[2048,64]{0,1:T(8,128)} %param.7) | copy-start | bytes 1572868
  0.6 3.3 %copy-start.1 = (f32[512,512]{1,0:T(8,128)S(1)}, f32[512,512]{1,0:T(8,128)}, u32[]{:S(2)}) copy-start(f32[512,512]{1,0:T(8,128)} %x_ref.1) | copy-start | bytes 3145732
  10.5 6.5 %collective-permute-start = (f32[64,512]{1,0:T(8,128)S(1)}, f32[64,512]{1,0:T(8,128)S(1)}, u32[]{:S(2)}, u32[]{:S(2)}) collective-permute-start(f32[64,512]{1,0:T(8,128)S(1)} %get-tuple-element.40.refs_0_), channel_id=1, source_target_pairs={{0,1},{1,0},{2,3},{3,2},{4,5},{5,4},{6,7},{7,6},{8,9},{9,8},{10,11... | collective-permute-start | bytes 393224 | tf_op jit(solution)/shard_map/ppermute | solution.py:276
  13.5 3.5 %copy-start.2 = (f32[512,64]{0,1:T(8,128)S(1)}, f32[512,64]{0,1:T(8,128)}, u32[]{:S(2)}) copy-start(f32[512,64]{0,1:T(8,128)} %param.5) | copy-start | bytes 393220
  18.3 1.5 %collective-permute-start.1 = (f32[64,1024]{1,0:T(8,128)S(1)}, f32[64,1024]{1,0:T(8,128)S(1)}, u32[]{:S(2)}, u32[]{:S(2)}) collective-permute-start(f32[64,1024]{1,0:T(8,128)S(1)} %get-tuple-element.49), channel_id=1, source_target_pairs={{0,2},{2,0},{4,6},{6,4},{8,10},{10,8},{12,14},{14,12},{16,18},{18,... | collective-permute-start | bytes 786440 | tf_op jit(solution)/shard_map/ppermute | solution.py:266
  19.9 19.5 %collective-permute-start.6 = (f32[256,512]{1,0:T(8,128)S(1)}, f32[256,512]{1,0:T(8,128)S(1)}, u32[]{:S(2)}, u32[]{:S(2)}) collective-permute-start(f32[256,512]{1,0:T(8,128)S(1)} %get-tuple-element.54.refs_0_), channel_id=1, source_target_pairs={{0,1},{1,0},{2,3},{3,2},{4,5},{5,4},{6,7},{7,6},{8,9},{9,8},{10,11... | collective-permute-start | bytes 1572872 | tf_op jit(solution)/shard_map/ppermute | solution.py:276
  21.7 4.3 %collective-permute-start.2 = (f32[64,256]{1,0:T(8,128)S(1)}, f32[64,256]{1,0:T(8,128)S(1)}, u32[]{:S(2)}, u32[]{:S(2)}) collective-permute-start(f32[64,256]{1,0:T(8,128)S(1)} %get-tuple-element.51), channel_id=1, source_target_pairs={{0,4},{2,6},{4,0},{6,2},{8,12},{10,14},{12,8},{14,10},{16,20},{18,... | collective-permute-start | bytes 196616 | tf_op jit(solution)/shard_map/ppermute | solution.py:266
  23.2 4.8 %collective-permute-start.3 = (f32[64,256]{1,0:T(8,128)S(1)}, f32[64,256]{1,0:T(8,128)S(1)}, u32[]{:S(2)}, u32[]{:S(2)}) collective-permute-start(f32[64,256]{1,0:T(8,128)S(1)} %get-tuple-element.52), channel_id=1, source_target_pairs={{0,8},{2,10},{4,12},{6,14},{8,0},{10,2},{12,4},{14,6},{16,24},{18,... | collective-permute-start | bytes 196616 | tf_op jit(solution)/shard_map/ppermute | solution.py:266
  24.8 5.2 %collective-permute-start.4 = (f32[64,256]{1,0:T(8,128)S(1)}, f32[64,256]{1,0:T(8,128)S(1)}, u32[]{:S(2)}, u32[]{:S(2)}) collective-permute-start(f32[64,256]{1,0:T(8,128)S(1)} %get-tuple-element.53), channel_id=1, source_target_pairs={{0,12},{2,14},{4,8},{6,10},{8,4},{10,6},{12,0},{14,2},{16,28},{18,... | collective-permute-start | bytes 196616 | tf_op jit(solution)/shard_map/ppermute | solution.py:266
  30.0 5.8 %collective-permute-start.5 = (f32[64,256]{1,0:T(8,128)S(1)}, f32[64,256]{1,0:T(8,128)S(1)}, u32[]{:S(2)}, u32[]{:S(2)}) collective-permute-start(f32[64,256]{1,0:T(8,128)S(1)} %sum.2.refs_0_), channel_id=1, source_target_pairs={{0,16},{2,18},{4,20},{6,22},{8,24},{10,26},{12,28},{14,30},{16,0},... | collective-permute-start | bytes 196616 | tf_op jit(solution)/shard_map/ppermute | solution.py:266
  35.8 6.2 %collective-permute-start.9 = (f32[64,256]{1,0:T(8,128)S(1)}, f32[64,256]{1,0:T(8,128)S(1)}, u32[]{:S(2)}, u32[]{:S(2)}) collective-permute-start(f32[64,256]{1,0:T(8,128)S(1)} %sum.3.refs_0_.whole_ref), channel_id=1, source_target_pairs={{0,12},{2,14},{4,8},{6,10},{8,4},{10,6},{12,0},{14,2},{16,28},{18,... | collective-permute-start | bytes 196616 | tf_op jit(solution)/shard_map/ppermute | solution.py:266
  36.1 5.9 %collective-permute-start.8 = (f32[64,256]{1,0:T(8,128)S(1)}, f32[64,256]{1,0:T(8,128)S(1)}, u32[]{:S(2)}, u32[]{:S(2)}) collective-permute-start(f32[64,256]{1,0:T(8,128)S(1)} %sum.3.refs_0_.whole_ref), channel_id=1, source_target_pairs={{0,8},{2,10},{4,12},{6,14},{8,0},{10,2},{12,4},{14,6},{16,24},{18,... | collective-permute-start | bytes 196616 | tf_op jit(solution)/shard_map/ppermute | solution.py:266
  38.0 4.3 %collective-permute-start.7 = (f32[64,256]{1,0:T(8,128)S(1)}, f32[64,256]{1,0:T(8,128)S(1)}, u32[]{:S(2)}, u32[]{:S(2)}) collective-permute-start(f32[64,256]{1,0:T(8,128)S(1)} %sum.3.refs_0_.whole_ref), channel_id=1, source_target_pairs={{0,4},{2,6},{4,0},{6,2},{8,12},{10,14},{12,8},{14,10},{16,20},{18,... | collective-permute-start | bytes 196616 | tf_op jit(solution)/shard_map/ppermute | solution.py:266
  42.3 1.6 %collective-permute-start.10 = (f32[64,1024]{1,0:T(8,128)S(1)}, f32[64,1024]{1,0:T(8,128)S(1)}, u32[]{:S(2)}, u32[]{:S(2)}) collective-permute-start(f32[64,1024]{1,0:T(8,128)S(1)} %pack.1), channel_id=1, source_target_pairs={{0,2},{2,0},{4,6},{6,4},{8,10},{10,8},{12,14},{14,12},{16,18},{18,... | collective-permute-start | bytes 786440 | tf_op jit(solution)/shard_map/ppermute | solution.py:266
  44.4 6.0 %collective-permute-start.11 = (f32[72,512]{1,0:T(8,128)S(1)}, f32[72,512]{1,0:T(8,128)S(1)}, u32[]{:S(2)}, u32[]{:S(2)}) collective-permute-start(f32[72,512]{1,0:T(8,128)S(1)} %product_second.1.refs_0_), channel_id=1, source_target_pairs={{0,1},{1,0},{2,3},{3,2},{4,5},{5,4},{6,7},{7,6},{8,9},{9,8},{10,11... | collective-permute-start | bytes 442376 | tf_op jit(solution)/shard_map/ppermute | solution.py:276
  51.1 1.4 %collective-permute-start.12 = (f32[72,512]{1,0:T(8,128)S(1)}, f32[72,512]{1,0:T(8,128)S(1)}, u32[]{:S(2)}, u32[]{:S(2)}) collective-permute-start(f32[72,512]{1,0:T(8,128)S(1)} %get-tuple-element.66), channel_id=1, source_target_pairs={{0,2},{2,0},{4,6},{6,4},{8,10},{10,8},{12,14},{14,12},{16,18},{18,... | collective-permute-start | bytes 442376 | tf_op jit(solution)/shard_map/ppermute | solution.py:266
  52.6 4.0 %collective-permute-start.13 = (f32[72,128]{1,0:T(8,128)S(1)}, f32[72,128]{1,0:T(8,128)S(1)}, u32[]{:S(2)}, u32[]{:S(2)}) collective-permute-start(f32[72,128]{1,0:T(8,128)S(1)} %get-tuple-element.69), channel_id=1, source_target_pairs={{0,4},{2,6},{4,0},{6,2},{8,12},{10,14},{12,8},{14,10},{16,20},{18,... | collective-permute-start | bytes 110600 | tf_op jit(solution)/shard_map/ppermute | solution.py:266
  54.0 4.0 %collective-permute-start.14 = (f32[72,128]{1,0:T(8,128)S(1)}, f32[72,128]{1,0:T(8,128)S(1)}, u32[]{:S(2)}, u32[]{:S(2)}) collective-permute-start(f32[72,128]{1,0:T(8,128)S(1)} %get-tuple-element.70), channel_id=1, source_target_pairs={{0,8},{2,10},{4,12},{6,14},{8,0},{10,2},{12,4},{14,6},{16,24},{18,... | collective-permute-start | bytes 110600 | tf_op jit(solution)/shard_map/ppermute | solution.py:266
  54.0 4.9 %collective-permute-start.15 = (f32[72,128]{1,0:T(8,128)S(1)}, f32[72,128]{1,0:T(8,128)S(1)}, u32[]{:S(2)}, u32[]{:S(2)}) collective-permute-start(f32[72,128]{1,0:T(8,128)S(1)} %get-tuple-element.71), channel_id=1, source_target_pairs={{0,12},{2,14},{4,8},{6,10},{8,4},{10,6},{12,0},{14,2},{16,28},{18,... | collective-permute-start | bytes 110600 | tf_op jit(solution)/shard_map/ppermute | solution.py:266

commit v4 on v3

--- a/solution.py
+++ b/solution.py
@@ -31,17 +31,18 @@
     return jax.ShapeDtypeStruct(shape, dtype)
 
 
-def call(kernel, name, ins, outs, scratch=(), room=8 * mega, flops=0, space=pltpu.VMEM):
+def call(kernel, name, ins, outs, scratch=(), room=8 * mega, flops=0, far=()):
     return pl.pallas_call(
         kernel,
         name=name,
-        in_specs=[pl.BlockSpec(memory_space=space)] * len(ins),
+        in_specs=[pl.BlockSpec(memory_space=pltpu.VMEM)] * len(ins)
+        + [pl.BlockSpec(memory_space=pltpu.HBM)] * len(far),
         out_specs=[pl.BlockSpec(memory_space=pltpu.VMEM)] * len(outs),
         out_shape=list(outs),
         scratch_shapes=list(scratch),
         compiler_params=pltpu.CompilerParams(vmem_limit_bytes=room),
         cost_estimate=pl.CostEstimate(flops=flops, bytes_accessed=0, transcendentals=0),
-    )(*ins)
+    )(*ins, *far)
 
 
 def points_in(x):
@@ -51,17 +52,35 @@
     return (-2.0 * wide).astype(bf16), (-2.0 * rest).astype(bf16), square
 
 
-def entries(high, low, square, xh, xl, xsq):
-    cross = dot(high, xh) + dot(low, xh) + dot(high, xl)
+def crossed(high, low, xh, xl):
+    return dot(high, xh) + dot(low, xh) + dot(high, xl)
+
+
+def entries(cross, square, xsq):
     dist = jnp.maximum(cross + (square + xsq), 0.0) + softening
     return jnp.exp(dist * lax.rsqrt(dist) * (-1.0 / kernel_scale))
 
 
-def load_kernel(c_hbm, ch_ref, cl_ref, sq_ref, pair_ref, c_ref, sems):
-    rows, share = c_ref.shape[0], pair_ref.shape[0] // 2
-    index, half = place()[0], lax.axis_size("dp") // 2
+def staged(count, cross, finish):
+    held = cross(0)
+    for i in range(count):
+        coming = cross(i + 1) if i + 1 < count else None
+        finish(i, held)
+        held = coming
+
+
+def rows_in(x, where, high_ref, low_ref, square_ref):
+    high, low = split(x)
+    wide, rest = high.astype(f32), low.astype(f32)
+    high_ref[where, :] = high
+    low_ref[where, :] = low
+    square_ref[where, :] = jnp.sum(wide * wide + 2.0 * (wide * rest), axis=1, keepdims=True)
+    return high, low
+
+
+def load_kernel(c_hbm, ch_ref, cl_ref, sq_ref, c_ref, sems):
     loads = sems.shape[0]
-    load = rows // loads
+    load = c_ref.shape[0] // loads
     copies = [
         pltpu.make_async_copy(c_hbm.at[pl.ds(i * load, load)], c_ref.at[pl.ds(i * load, load)], sems.at[i])
         for i in range(loads)
@@ -71,37 +90,67 @@
     for i, copy in enumerate(copies):
         copy.wait()
         where = slice(i * load, (i + 1) * load)
-        high, low = split(c_ref[where, :])
-        wide, rest = high.astype(f32), low.astype(f32)
-        ch_ref[where, :] = high
-        cl_ref[where, :] = low
-        sq_ref[where, :] = jnp.sum(wide * wide + 2.0 * (wide * rest), axis=1, keepdims=True)
-    for t, at in enumerate((index, lax.rem(index + half, 2 * half))):
-        pair_ref[t * share : (t + 1) * share, :] = c_ref[pl.ds(pl.multiple_of(at * share, share), share), :]
-
-
-def data_kernel(block, x_ref, w_ref, ch_ref, cl_ref, sq_ref, kh_ref, kl_ref, pred_ref, xh_ref, xl_ref):
-    rows, outs = ch_ref.shape[0], pred_ref.shape[0]
+        rows_in(c_ref[where, :], where, ch_ref, cl_ref, sq_ref)
+
+
+def first_data_kernel(block, x_ref, ch_ref, cl_ref, sq_ref, c_hbm, *refs):
+    kh_ref, kl_ref, xh_ref, xl_ref, xsq_ref, rest_ref, pair_ref, sems = refs
+    half, share = rest_ref.shape[0], pair_ref.shape[0] // 2
+    index, count = place()[0], lax.axis_size("dp")
+    copies = [pltpu.make_async_copy(c_hbm.at[pl.ds(half, half)], rest_ref, sems.at[0])]
+    for t, at in enumerate((index, lax.rem(index + count // 2, count))):
+        where = pl.ds(pl.multiple_of(at * share, share), share)
+        copies.append(
+            pltpu.make_async_copy(c_hbm.at[where], pair_ref.at[pl.ds(t * share, share)], sems.at[1 + t])
+        )
+    for copy in copies:
+        copy.start()
     xh, xl, xsq = points_in(x_ref[...])
     xh_ref[...] = xh
     xl_ref[...] = xl
-    pred = None
-    for i in range(rows // block):
+    xsq_ref[...] = xsq
+
+    def cross(i):
         where = slice(i * block, (i + 1) * block)
-        tile = entries(ch_ref[where, :], cl_ref[where, :], sq_ref[where, :], xh_ref[...], xl_ref[...], xsq)
-        kh, kl = split(tile)
+        return crossed(ch_ref[where, :], cl_ref[where, :], xh_ref[...], xl_ref[...])
+
+    def finish(i, value):
+        where = slice(i * block, (i + 1) * block)
+        kh, kl = split(entries(value, sq_ref[where, :], xsq))
         kh_ref[where, :] = kh
         kl_ref[where, :] = kl
-        weights = jnp.concatenate(split(w_ref[:, where]), axis=0)
-        part = dot(weights, kh) + dot(weights, kl)
-        pred = part if pred is None else pred + part
+
+    staged(half // block, cross, finish)
+    for copy in copies:
+        copy.wait()
+
+
+def second_data_kernel(block, w_ref, rest_ref, xh_ref, xl_ref, xsq_ref, first_h, first_l, *refs):
+    ch_ref, cl_ref, sq_ref, kh_ref, kl_ref, pred_ref = refs
+    half, outs = rest_ref.shape[0], pred_ref.shape[0]
+
+    def cross(i):
+        where = slice(i * block, (i + 1) * block)
+        high, low = rows_in(rest_ref[where, :], where, ch_ref, cl_ref, sq_ref)
+        return crossed(high, low, xh_ref[...], xl_ref[...])
+
+    def finish(i, value):
+        where = slice(i * block, (i + 1) * block)
+        kh, kl = split(entries(value, sq_ref[where, :], xsq_ref[...]))
+        kh_ref[where, :] = kh
+        kl_ref[where, :] = kl
+
+    staged(half // block, cross, finish)
+    weights = jnp.concatenate(split(w_ref[...]), axis=0)
+    pred = dot(weights[:, :half], first_h[...]) + dot(weights[:, :half], first_l[...])
+    pred = pred + (dot(weights[:, half:], kh_ref[...]) + dot(weights[:, half:], kl_ref[...]))
     pred_ref[...] = pred[:outs, :] + pred[outs:, :]
 
 
 def centre_kernel(block, *refs):
-    x_refs = refs[:-8]
-    ch_ref, cl_ref, sq_ref, kh_ref, kl_ref, sum_ref, xh_ref, xl_ref = refs[-8:]
-    rows = ch_ref.shape[0]
+    x_refs, centres = refs[:-11], (refs[-11:-8], refs[-8:-5])
+    kh_ref, kl_ref, sum_ref, xh_ref, xl_ref = refs[-5:]
+    half = centres[0][0].shape[0]
     at = 0
     for x_ref in x_refs:
         span = slice(at, at + x_ref.shape[0])
@@ -109,57 +158,67 @@
         xh, xl, xsq = points_in(x_ref[...])
         xh_ref[...] = xh
         xl_ref[...] = xl
-        total = None
-        for i in range(rows // block):
+        sums = []
+
+        def cross(i):
+            high, low, _ = centres[i * block // half]
+            where = slice(i * block % half, i * block % half + block)
+            return crossed(high[where, :], low[where, :], xh_ref[...], xl_ref[...])
+
+        def finish(i, value):
+            square = centres[i * block // half][2]
+            tile = entries(value, square[i * block % half : i * block % half + block, :], xsq)
             where = slice(i * block, (i + 1) * block)
-            tile = entries(ch_ref[where, :], cl_ref[where, :], sq_ref[where, :], xh_ref[...], xl_ref[...], xsq)
             kh, kl = split(tile)
             kh_ref[where, span] = kh
             kl_ref[where, span] = kl
-            part = jnp.sum(tile.reshape(-1, 8, tile.shape[1]), axis=0)
-            total = part if total is None else total + part
-        sum_ref[:, span] = total
-
-
-def share_rows(mids, share, flip, tops=(0, 1)):
+            sums.append(jnp.sum(tile.reshape(-1, 8, tile.shape[1]), axis=0))
+
+        staged(2 * half // block, cross, finish)
+        sum_ref[:, span] = sum(sums[1:], sums[0])
+
+
+def share_blocks(mids, flip, tops=(0, 1)):
     _, core, mid, _ = place()
-    for m in range(mids):
-        for top in tops:
-            block = top * 2 * mids + 2 * (mid ^ m) + (core ^ flip)
-            yield pl.ds(pl.multiple_of(block * share, share), share)
-
-
-def take(ref, where):
-    return jnp.concatenate([ref[rows, :] for rows in where], axis=0)
-
-
-def back(where, parts, right):
-    where = list(where)
+    return [(top, 2 * (mid ^ m) + (core ^ flip)) for m in range(mids) for top in tops]
+
+
+def take(ref, where, share):
+    rows = []
+    for top, block in where:
+        source = ref[top] if isinstance(ref, tuple) else ref
+        at = block if isinstance(ref, tuple) else top * (source.shape[0] // share // 2) + block
+        rows.append(source[pl.ds(pl.multiple_of(at * share, share), share), :])
+    return jnp.concatenate(rows, axis=0)
+
+
+def back(where, share, parts, right):
     product, at = 0.0, 0
     for high, low in parts:
+        high, low = take(high, where, share), take(low, where, share)
         values = right[at : at + high.shape[1]]
         at += high.shape[1]
-        product = product + (dot(take(high, where), values) + dot(take(low, where), values))
+        product = product + (dot(high, values) + dot(low, values))
     product = product.T
     outs = right.shape[1] // 2
     return product[:outs] + product[outs:]
 
 
 def grad_kernel(mids, share, *refs):
-    t_ref, high_ref, low_ref, out_ref, res_ref, right_ref = refs[-6:]
+    t_ref, kernels, (out_ref, res_ref, right_ref) = refs[-8], refs[-7:-3], refs[-3:]
     total = refs[0][...]
-    for ref in refs[1:-6]:
+    for ref in refs[1:-8]:
         total = total + ref[...]
     residual = total - t_ref[...]
     res_ref[...] = residual
     right = jnp.concatenate(split(residual.T), axis=1)
     right_ref[...] = right
-    out_ref[...] = back(share_rows(mids, share, 1), [(high_ref, low_ref)], right)
-
-
-def grad_keep_kernel(mids, share, right_ref, high_ref, low_ref, out_ref):
-    right = right_ref[...]
-    out_ref[...] = back(share_rows(mids, share, 0), [(high_ref, low_ref)], right)
+    out_ref[...] = back(share_blocks(mids, 1), share, [(kernels[:2], kernels[2:])], right)
+
+
+def grad_keep_kernel(mids, share, right_ref, *refs):
+    out_ref = refs[4]
+    out_ref[...] = back(share_blocks(mids, 0), share, [(refs[:2], refs[2:4])], right_ref[...])
 
 
 def image_kernel(mids, share, shards, *refs):
@@ -178,13 +237,13 @@
         right_ref[j * size : (j + 1) * size, :] = jnp.concatenate(split(part.T), axis=1)
         if j == 0:
             own_ref[...] = part[:, :share]
-    where = share_rows(mids, share, 1, [place()[3]])
-    out_ref[:outs, :] = back(where, [kernels[:2], kernels[2:]], right_ref[...])
+    where = share_blocks(mids, 1, [place()[3]])
+    out_ref[:outs, :] = back(where, share, [kernels[:2], kernels[2:]], right_ref[...])
 
 
 def image_keep_kernel(mids, share, right_ref, *refs):
-    where = share_rows(mids, share, 0, [place()[3]])
-    refs[-1][...] = back(where, [refs[:2], refs[2:4]], right_ref[...])
+    where = share_blocks(mids, 0, [place()[3]])
+    refs[-1][...] = back(where, share, [refs[:2], refs[2:4]], right_ref[...])
 
 
 def shard_at(j, shards, share):
@@ -192,12 +251,12 @@
 
 
 def product(mids, share, flip, pieces, kernels):
-    where = list(share_rows(mids, share, flip))
+    where = share_blocks(mids, flip)
     high, low = split(jnp.concatenate([ref[...] for ref in pieces], axis=1))
     left = jnp.concatenate([high, low], axis=0)
     outs = high.shape[0]
     for kh, kl in (kernels[:2], kernels[2:]):
-        result = dot(left, take(kh, where)) + dot(left, take(kl, where))
+        result = dot(left, take(kh, where, share)) + dot(left, take(kl, where, share))
         yield result[:outs] + result[outs:]
 
 
@@ -291,31 +350,50 @@
     weights = coefficients.T
     block = min(256, rows)
 
-    loads = min(8, count)
-    kept = 4 * rows * width + 512 * rows + 8 * share * width
-    ch, cl, square, pair = call(
-        load_kernel, "load", [centres],
+    part = rows // 2
+    loads = min(4, count)
+    kept = 2 * part * width * 2 + 512 * part
+    loaded = call(
+        load_kernel, "load", [], [like(part, width, dtype=bf16), like(part, width, dtype=bf16), like(part, 1)],
+        [pltpu.VMEM((part, width), f32), pltpu.SemaphoreType.DMA((loads,))],
+        room=53 * mega - kept - 4 * points * width, far=[centres],
+    )
+    kept = 2 * kept + 8 * points * width + 4 * part * (points + width) + 8 * share * width
+    kh0, kl0, xh, xl, xsq, rest, pair = call(
+        functools.partial(first_data_kernel, block // 2), "data_first", [samples] + list(loaded),
         [
-            like(rows, width, dtype=bf16),
-            like(rows, width, dtype=bf16),
-            like(rows, 1),
+            like(part, points, dtype=bf16),
+            like(part, points, dtype=bf16),
+            like(width, points, dtype=bf16),
+            like(width, points, dtype=bf16),
+            like(1, points),
+            like(part, width),
             like(2 * share, width),
         ],
-        [pltpu.VMEM((rows, width), f32), pltpu.SemaphoreType.DMA((loads,))],
-        room=103 * mega // 2 - kept, space=pltpu.HBM,
-    )
-    kh, kl, pred = call(
-        functools.partial(data_kernel, block), "data", [samples, weights, ch, cl, square],
-        [like(rows, points, dtype=bf16), like(rows, points, dtype=bf16), like(outs, points)],
-        [pltpu.VMEM((width, points), bf16), pltpu.VMEM((width, points), bf16)],
-    )
+        [pltpu.SemaphoreType.DMA((3,))],
+        room=107 * mega // 2 - kept, far=[centres],
+    )
+    ch, cl, square, kh1, kl1, pred = call(
+        functools.partial(second_data_kernel, block // 2), "data_second",
+        [weights, rest, xh, xl, xsq, kh0, kl0],
+        [
+            like(part, width, dtype=bf16),
+            like(part, width, dtype=bf16),
+            like(part, 1),
+            like(part, points, dtype=bf16),
+            like(part, points, dtype=bf16),
+            like(outs, points),
+        ],
+    )
+    halves = list(loaded) + [ch, cl, square]
+    kernel = [kh0, kh1, kl0, kl1]
     got = [send_far(pred, 0, shift) for shift in range(1, shards)]
 
     def centre_tile(blocks, name):
         size = blocks[0].shape[0]
         columns = size * len(blocks)
         return call(
-            functools.partial(centre_kernel, block), name, blocks + [ch, cl, square],
+            functools.partial(centre_kernel, block // 2), name, blocks + halves,
             [like(rows, columns, dtype=bf16), like(rows, columns, dtype=bf16), like(8, columns)],
             [pltpu.VMEM((width, size), bf16), pltpu.VMEM((width, size), bf16)],
             flops=6 * rows * columns * width,
@@ -326,13 +404,13 @@
 
     give, residual, right = call(
         functools.partial(grad_kernel, mids, share), "grad_give",
-        [pred] + got + [targets.T, kh, kl],
+        [pred] + got + [targets.T] + kernel,
         [like(outs, half * share), like(outs, points), like(points, 2 * outs, dtype=bf16)],
     )
     received = send_xor(give, 1)
     (keep,) = call(
         functools.partial(grad_keep_kernel, mids, share), "grad_keep",
-        [right, kh, kl], [like(outs, half * share)],
+        [right] + kernel, [like(outs, half * share)],
     )
 
     def join(keep, received, extra, height):
@@ -359,14 +437,14 @@
     packed = call(
         pack_kernel, "pack", [after(whole, far_sums)] + gathered[1:], [like(outs, 2 * share * mids)]
     )[0]
-    crossed = [send_xor(packed, 1)]
+    swapped = [send_xor(packed, 1)]
     firsts = call(
         functools.partial(first_kernel, mids, share), "product_first",
         gathered + kernels, [like(outs, 2 * share), like(outs, wide)],
     )
     (image,) = call(
         functools.partial(second_kernel, mids, share, shards), "product_second",
-        crossed + kernels + list(firsts) + [own_sums, far_sums],
+        swapped + kernels + list(firsts) + [own_sums, far_sums],
         [like(outs + 8, 2 * share * shards)],
     )
     images = [image] + [send_far(image, 0, shift) for shift in range(1, shards)]

time: 59.7 us -> 58.3 us (0.977)
  Pallas kernels: 20 us -> 18 us
  waiting for transfers between devices: 19.9 us -> 20.6 us
    pallas_call x16 -> x17, Pallas kernels: 20 us -> 18 us  [call(): pl.pallas_call(kernel, name=name, in_specs=[pl.BlockSpec(memory_space=plt...]
  transfers between devices with their start and end apart: 16 -> 16, of which waited for: 13 -> 13; matrix products, arithmetic and copies ran while one was open for 0% -> 0% of each run, Pallas kernels for 12% -> 11%
where the time goes in v4:
time: 58.3 us; the launch traced here: 58.1 us
  waiting for transfers between devices  20.6 us (35%)
  starting transfers between devices  18.7 us (32%)
  Pallas kernels  18 us (31%)
  between operations  0.81 us (1%)
    pallas_call x17, Pallas kernels, call(): pl.pallas_call(kernel, name=name, in_specs=[pl.BlockSpec(memory_space=plt...  18 us
    ppermute x13, waiting for transfers between devices, send_xor(): return lax.ppermute(array, 'dp', [(i, i ^ mask) for i in range(count)])  14 us
    ppermute x13, starting transfers between devices, send_xor(): return lax.ppermute(array, 'dp', [(i, i ^ mask) for i in range(count)])  13.4 us
    ppermute x3, waiting for transfers between devices, send_far(): return lax.ppermute(array, ('dp', 'centre'), pairs)  6.62 us
    ppermute x3, starting transfers between devices, send_far(): return lax.ppermute(array, ('dp', 'centre'), pairs)  5.33 us
  transfers between devices with their start and end apart: 16, of which 13 were waited for; matrix products, arithmetic and copies ran while one was open for 0% of the time, Pallas kernels for 11%

profile of v4, /device:TPU:0, one launch (start us, length us, event | category | flops | bytes accessed | tf_op | source)
XLA Modules:
  0.0 58.1 jit_solution(9558432930720592815)
XLA Ops:
  0.6 2.2 %load.1 = (bf16[1024,512]{1,0:T(8,128)(2,1)S(1)}, bf16[1024,512]{1,0:T(8,128)(2,1)S(1)}, f32[1024,1]{1,0:T(8,128)S(1)}) custom-call(f32[2048,512]{1,0:T(8,128)} %c_hbm.3), custom_call_target="tpu_custom_call" | custom-call | tf_op jit(solution)/shard_map/load/pallas_call | solution.py:35
  2.8 3.2 %data_first.1 = (bf16[1024,512]{1,0:T(8,128)(2,1)S(1)}, bf16[1024,512]{1,0:T(8,128)(2,1)S(1)}, bf16[512,512]{1,0:T(8,128)(2,1)S(1)}, bf16[512,512]{1,0:T(8,128)(...) custom-call(f32[512,512]{1,0:T(8,128)S(1)} %copy-done.1, ...), custom_call_target="tpu_custom_call" | custom-call | tf_op jit(solution)/shard_map/data_first/pallas_call | solution.py:35
  6.0 3.1 %data_second.1 = (bf16[1024,512]{1,0:T(8,128)(2,1)S(1)}, bf16[1024,512]{1,0:T(8,128)(2,1)S(1)}, f32[1024,1]{1,0:T(8,128)S(1)}, bf16[1024,512]{1,0:T(8,128)(2,1)S...) custom-call(f32[64,2048]{1,0:T(8,128)S(1)} %bitcast.4, f32[1024,512]{1,0:T(8,128)S(1)} %get-tuple-element.49.rest_ref, ...), custom_call_target="tpu_custom_call" | custom-call | tf_op jit(solution)/shard_map/data_second/pallas_call | solution.py:35
  9.1 3.0 %collective-permute-start = (f32[64,512]{1,0:T(8,128)S(1)}, f32[64,512]{1,0:T(8,128)S(1)}, u32[]{:S(2)}, u32[]{:S(2)}) collective-permute-start(f32[64,512]{1,0:T(8,128)S(1)} %get-tuple-element.55.refs_0_), channel_id=1, source_target_pairs={{0,1},{1,0},{2,3},{3,2},{4,5},{5,4},{6,7},{7,6},{8,9},{9,8},{10,11... | collective-permute-start | bytes 393224 | tf_op jit(solution)/shard_map/ppermute | solution.py:335
  12.1 2.2 %own_tile.1 = (bf16[2048,256]{1,0:T(8,128)(2,1)S(1)}, bf16[2048,256]{1,0:T(8,128)(2,1)S(1)}, f32[8,256]{1,0:T(8,128)S(1)}) custom-call(f32[256,512]{1,0:T(8,128)S(1)} %get-tuple-element.72.refs_0_, bf16[1024,512]{1,0:T(8,128)(2,1)S(1)} %get-tuple-element.46.ch_ref.refs_1_, bf16[1024,512]{1,0:T(8,128)(2,1)S(1)} %get-tuple-element.47.cl_ref.refs_2_, ...), custom_call_target="tpu_custom_call" | custom-call | flops 1610612736 | tf_op jit(solution)/shard_map/own_tile/pallas_call | solution.py:35
  14.3 1.3 %collective-permute-done.refs_1_ = f32[64,512]{1,0:T(8,128)S(1)} collective-permute-done((f32[64,512]{1,0:T(8,128)S(1)}, f32[64,512]{1,0:T(8,128)S(1)}, u32[]{:S(2)}, u32[]{:S(2)}) %collective-permute-start) | collective-permute-done | bytes 131104 | tf_op jit(solution)/shard_map/ppermute | solution.py:335
  15.6 1.3 %grad_give.1 = (f32[64,1024]{1,0:T(8,128)S(1)}, f32[64,512]{1,0:T(8,128)}, bf16[512,128]{1,0:T(8,128)(2,1)S(1)}) custom-call(f32[64,512]{1,0:T(8,128)S(1)} %get-tuple-element.55.refs_0_, f32[64,512]{1,0:T(8,128)S(1)} %collective-permute-done.refs_1_, f32[64,512]{1,0:T(8,128)S(1)} %bitcast.6, bf16[1024,512]{1,0:T(8,128)(2,1)S(1)} %get-tuple-element.53.first_h.refs_3_.refs_0_, ...), custom_call_target="tpu_custom_call" | custom-call | tf_op jit(solution)/shard_map/grad_give/pallas_call | solution.py:35
  18.5 1.7 %collective-permute-start.6 = (f32[256,512]{1,0:T(8,128)S(1)}, f32[256,512]{1,0:T(8,128)S(1)}, u32[]{:S(2)}, u32[]{:S(2)}) collective-permute-start(f32[256,512]{1,0:T(8,128)S(1)} %get-tuple-element.72.refs_0_), channel_id=1, source_target_pairs={{0,1},{1,0},{2,3},{3,2},{4,5},{5,4},{6,7},{7,6},{8,9},{9,8},{10,11... | collective-permute-start | bytes 1572872 | tf_op jit(solution)/shard_map/ppermute | solution.py:335
  20.2 1.6 %collective-permute-start.2 = (f32[64,256]{1,0:T(8,128)S(1)}, f32[64,256]{1,0:T(8,128)S(1)}, u32[]{:S(2)}, u32[]{:S(2)}) collective-permute-start(f32[64,256]{1,0:T(8,128)S(1)} %get-tuple-element.69), channel_id=1, source_target_pairs={{0,4},{2,6},{4,0},{6,2},{8,12},{10,14},{12,8},{14,10},{16,20},{18,... | collective-permute-start | bytes 196616 | tf_op jit(solution)/shard_map/ppermute | solution.py:325
  21.8 1.6 %collective-permute-start.3 = (f32[64,256]{1,0:T(8,128)S(1)}, f32[64,256]{1,0:T(8,128)S(1)}, u32[]{:S(2)}, u32[]{:S(2)}) collective-permute-start(f32[64,256]{1,0:T(8,128)S(1)} %get-tuple-element.70), channel_id=1, source_target_pairs={{0,8},{2,10},{4,12},{6,14},{8,0},{10,2},{12,4},{14,6},{16,24},{18,... | collective-permute-start | bytes 196616 | tf_op jit(solution)/shard_map/ppermute | solution.py:325
  24.6 2.1 %collective-permute-done.3.refs_2_ = f32[64,256]{1,0:T(8,128)S(1)} collective-permute-done((f32[64,256]{1,0:T(8,128)S(1)}, f32[64,256]{1,0:T(8,128)S(1)}, u32[]{:S(2)}, u32[]{:S(2)}) %collective-permute-start.3) | collective-permute-done | bytes 65568 | tf_op jit(solution)/shard_map/ppermute | solution.py:325
  26.6 1.9 %collective-permute-done.4.refs_3_ = f32[64,256]{1,0:T(8,128)S(1)} collective-permute-done((f32[64,256]{1,0:T(8,128)S(1)}, f32[64,256]{1,0:T(8,128)S(1)}, u32[]{:S(2)}, u32[]{:S(2)}) %collective-permute-start.4) | collective-permute-done | bytes 65568 | tf_op jit(solution)/shard_map/ppermute | solution.py:325
  28.6 2.6 %collective-permute-start.5 = (f32[64,256]{1,0:T(8,128)S(1)}, f32[64,256]{1,0:T(8,128)S(1)}, u32[]{:S(2)}, u32[]{:S(2)}) collective-permute-start(f32[64,256]{1,0:T(8,128)S(1)} %sum.2.refs_0_), channel_id=1, source_target_pairs={{0,16},{2,18},{4,20},{6,22},{8,24},{10,26},{12,28},{14,30},{16,0},... | collective-permute-start | bytes 196616 | tf_op jit(solution)/shard_map/ppermute | solution.py:325
  31.2 3.2 %collective-permute-done.5.refs_1_ = f32[64,256]{1,0:T(8,128)S(1)} collective-permute-done((f32[64,256]{1,0:T(8,128)S(1)}, f32[64,256]{1,0:T(8,128)S(1)}, u32[]{:S(2)}, u32[]{:S(2)}) %collective-permute-start.5) | collective-permute-done | bytes 65568 | tf_op jit(solution)/shard_map/ppermute | solution.py:325
  34.7 1.9 %collective-permute-start.8 = (f32[64,256]{1,0:T(8,128)S(1)}, f32[64,256]{1,0:T(8,128)S(1)}, u32[]{:S(2)}, u32[]{:S(2)}) collective-permute-start(f32[64,256]{1,0:T(8,128)S(1)} %sum.3.refs_0_.whole_ref), channel_id=1, source_target_pairs={{0,8},{2,10},{4,12},{6,14},{8,0},{10,2},{12,4},{14,6},{16,24},{18,... | collective-permute-start | bytes 196616 | tf_op jit(solution)/shard_map/ppermute | solution.py:325
  36.6 1.4 %collective-permute-start.7 = (f32[64,256]{1,0:T(8,128)S(1)}, f32[64,256]{1,0:T(8,128)S(1)}, u32[]{:S(2)}, u32[]{:S(2)}) collective-permute-start(f32[64,256]{1,0:T(8,128)S(1)} %sum.3.refs_0_.whole_ref), channel_id=1, source_target_pairs={{0,4},{2,6},{4,0},{6,2},{8,12},{10,14},{12,8},{14,10},{16,20},{18,... | collective-permute-start | bytes 196616 | tf_op jit(solution)/shard_map/ppermute | solution.py:325
  38.0 2.2 %far_tile.1 = (bf16[2048,256]{1,0:T(8,128)(2,1)S(1)}, bf16[2048,256]{1,0:T(8,128)(2,1)S(1)}, f32[8,256]{1,0:T(8,128)S(1)}) custom-call(f32[256,512]{1,0:T(8,128)S(1)} %collective-permute-done.6.refs_0_, bf16[1024,512]{1,0:T(8,128)(2,1)S(1)} %get-tuple-element.46.ch_ref.refs_1_, bf16[1024,512]{1,0:T(8,128)(2,1)S(1)} %get-tuple-element.47.cl_ref.refs_2_, ...), custom_call_target="tpu_custom_call" | custom-call | flops 1610612736 | tf_op jit(solution)/shard_map/far_tile/pallas_call | solution.py:35
  41.4 1.0 %collective-permute-done.10.refs_0_ = f32[64,1024]{1,0:T(8,128)S(1)} collective-permute-done((f32[64,1024]{1,0:T(8,128)S(1)}, f32[64,1024]{1,0:T(8,128)S(1)}, u32[]{:S(2)}, u32[]{:S(2)}) %collective-permute-start.10) | collective-permute-done | bytes 262176 | tf_op jit(solution)/shard_map/ppermute | solution.py:325
  43.5 5.4 %collective-permute-done.11.refs_1_ = f32[72,512]{1,0:T(8,128)S(1)} collective-permute-done((f32[72,512]{1,0:T(8,128)S(1)}, f32[72,512]{1,0:T(8,128)S(1)}, u32[]{:S(2)}, u32[]{:S(2)}) %collective-permute-start.11) | collective-permute-done | bytes 147488 | tf_op jit(solution)/shard_map/ppermute | solution.py:335
  50.2 0.8 %collective-permute-done.12.got_ref = f32[72,512]{1,0:T(8,128)S(1)} collective-permute-done((f32[72,512]{1,0:T(8,128)S(1)}, f32[72,512]{1,0:T(8,128)S(1)}, u32[]{:S(2)}, u32[]{:S(2)}) %collective-permute-start.12) | collective-permute-done | bytes 147488 | tf_op jit(solution)/shard_map/ppermute | solution.py:325
  51.1 1.4 %collective-permute-start.13 = (f32[72,128]{1,0:T(8,128)S(1)}, f32[72,128]{1,0:T(8,128)S(1)}, u32[]{:S(2)}, u32[]{:S(2)}) collective-permute-start(f32[72,128]{1,0:T(8,128)S(1)} %get-tuple-element.87), channel_id=1, source_target_pairs={{0,4},{2,6},{4,0},{6,2},{8,12},{10,14},{12,8},{14,10},{16,20},{18,... | collective-permute-start | bytes 110600 | tf_op jit(solution)/shard_map/ppermute | solution.py:325
  52.6 2.1 %collective-permute-start.15 = (f32[72,128]{1,0:T(8,128)S(1)}, f32[72,128]{1,0:T(8,128)S(1)}, u32[]{:S(2)}, u32[]{:S(2)}) collective-permute-start(f32[72,128]{1,0:T(8,128)S(1)} %get-tuple-element.89), channel_id=1, source_target_pairs={{0,12},{2,14},{4,8},{6,10},{8,4},{10,6},{12,0},{14,2},{16,28},{18,... | collective-permute-start | bytes 110600 | tf_op jit(solution)/shard_map/ppermute | solution.py:325
  55.1 1.4 %collective-permute-done.14.refs_2_ = f32[72,128]{1,0:T(8,128)S(1)} collective-permute-done((f32[72,128]{1,0:T(8,128)S(1)}, f32[72,128]{1,0:T(8,128)S(1)}, u32[]{:S(2)}, u32[]{:S(2)}) %collective-permute-start.14) | collective-permute-done | bytes 36896 | tf_op jit(solution)/shard_map/ppermute | solution.py:325
  56.5 0.9 %collective-permute-done.15.refs_3_ = f32[72,128]{1,0:T(8,128)S(1)} collective-permute-done((f32[72,128]{1,0:T(8,128)S(1)}, f32[72,128]{1,0:T(8,128)S(1)}, u32[]{:S(2)}, u32[]{:S(2)}) %collective-permute-start.15) | collective-permute-done | bytes 36896 | tf_op jit(solution)/shard_map/ppermute | solution.py:325
  (31 shorter events, 7.8 us)
Async XLA Ops:
  0.6 2.2 %copy-start.1 = (f32[512,512]{1,0:T(8,128)S(1)}, f32[512,512]{1,0:T(8,128)}, u32[]{:S(2)}) copy-start(f32[512,512]{1,0:T(8,128)} %x_ref.1) | copy-start | bytes 3145732
  2.8 3.2 %copy-start = (f32[2048,64]{0,1:T(8,128)S(1)}, f32[2048,64]{0,1:T(8,128)}, u32[]{:S(2)}) copy-start(f32[2048,64]{0,1:T(8,128)} %param.7) | copy-start | bytes 1572868
  9.1 6.5 %copy-start.2 = (f32[512,64]{0,1:T(8,128)S(1)}, f32[512,64]{0,1:T(8,128)}, u32[]{:S(2)}) copy-start(f32[512,64]{0,1:T(8,128)} %param.5) | copy-start | bytes 393220
  9.1 6.5 %collective-permute-start = (f32[64,512]{1,0:T(8,128)S(1)}, f32[64,512]{1,0:T(8,128)S(1)}, u32[]{:S(2)}, u32[]{:S(2)}) collective-permute-start(f32[64,512]{1,0:T(8,128)S(1)} %get-tuple-element.55.refs_0_), channel_id=1, source_target_pairs={{0,1},{1,0},{2,3},{3,2},{4,5},{5,4},{6,7},{7,6},{8,9},{9,8},{10,11... | collective-permute-start | bytes 393224 | tf_op jit(solution)/shard_map/ppermute | solution.py:335
  16.9 1.5 %collective-permute-start.1 = (f32[64,1024]{1,0:T(8,128)S(1)}, f32[64,1024]{1,0:T(8,128)S(1)}, u32[]{:S(2)}, u32[]{:S(2)}) collective-permute-start(f32[64,1024]{1,0:T(8,128)S(1)} %get-tuple-element.67), channel_id=1, source_target_pairs={{0,2},{2,0},{4,6},{6,4},{8,10},{10,8},{12,14},{14,12},{16,18},{18,... | collective-permute-start | bytes 786440 | tf_op jit(solution)/shard_map/ppermute | solution.py:325
  18.5 19.5 %collective-permute-start.6 = (f32[256,512]{1,0:T(8,128)S(1)}, f32[256,512]{1,0:T(8,128)S(1)}, u32[]{:S(2)}, u32[]{:S(2)}) collective-permute-start(f32[256,512]{1,0:T(8,128)S(1)} %get-tuple-element.72.refs_0_), channel_id=1, source_target_pairs={{0,1},{1,0},{2,3},{3,2},{4,5},{5,4},{6,7},{7,6},{8,9},{9,8},{10,11... | collective-permute-start | bytes 1572872 | tf_op jit(solution)/shard_map/ppermute | solution.py:335
  20.2 4.3 %collective-permute-start.2 = (f32[64,256]{1,0:T(8,128)S(1)}, f32[64,256]{1,0:T(8,128)S(1)}, u32[]{:S(2)}, u32[]{:S(2)}) collective-permute-start(f32[64,256]{1,0:T(8,128)S(1)} %get-tuple-element.69), channel_id=1, source_target_pairs={{0,4},{2,6},{4,0},{6,2},{8,12},{10,14},{12,8},{14,10},{16,20},{18,... | collective-permute-start | bytes 196616 | tf_op jit(solution)/shard_map/ppermute | solution.py:325
  21.8 4.8 %collective-permute-start.3 = (f32[64,256]{1,0:T(8,128)S(1)}, f32[64,256]{1,0:T(8,128)S(1)}, u32[]{:S(2)}, u32[]{:S(2)}) collective-permute-start(f32[64,256]{1,0:T(8,128)S(1)} %get-tuple-element.70), channel_id=1, source_target_pairs={{0,8},{2,10},{4,12},{6,14},{8,0},{10,2},{12,4},{14,6},{16,24},{18,... | collective-permute-start | bytes 196616 | tf_op jit(solution)/shard_map/ppermute | solution.py:325
  23.4 5.2 %collective-permute-start.4 = (f32[64,256]{1,0:T(8,128)S(1)}, f32[64,256]{1,0:T(8,128)S(1)}, u32[]{:S(2)}, u32[]{:S(2)}) collective-permute-start(f32[64,256]{1,0:T(8,128)S(1)} %get-tuple-element.71), channel_id=1, source_target_pairs={{0,12},{2,14},{4,8},{6,10},{8,4},{10,6},{12,0},{14,2},{16,28},{18,... | collective-permute-start | bytes 196616 | tf_op jit(solution)/shard_map/ppermute | solution.py:325
  28.6 5.8 %collective-permute-start.5 = (f32[64,256]{1,0:T(8,128)S(1)}, f32[64,256]{1,0:T(8,128)S(1)}, u32[]{:S(2)}, u32[]{:S(2)}) collective-permute-start(f32[64,256]{1,0:T(8,128)S(1)} %sum.2.refs_0_), channel_id=1, source_target_pairs={{0,16},{2,18},{4,20},{6,22},{8,24},{10,26},{12,28},{14,30},{16,0},... | collective-permute-start | bytes 196616 | tf_op jit(solution)/shard_map/ppermute | solution.py:325
  34.4 5.8 %collective-permute-start.9 = (f32[64,256]{1,0:T(8,128)S(1)}, f32[64,256]{1,0:T(8,128)S(1)}, u32[]{:S(2)}, u32[]{:S(2)}) collective-permute-start(f32[64,256]{1,0:T(8,128)S(1)} %sum.3.refs_0_.whole_ref), channel_id=1, source_target_pairs={{0,12},{2,14},{4,8},{6,10},{8,4},{10,6},{12,0},{14,2},{16,28},{18,... | collective-permute-start | bytes 196616 | tf_op jit(solution)/shard_map/ppermute | solution.py:325
  34.7 5.5 %collective-permute-start.8 = (f32[64,256]{1,0:T(8,128)S(1)}, f32[64,256]{1,0:T(8,128)S(1)}, u32[]{:S(2)}, u32[]{:S(2)}) collective-permute-start(f32[64,256]{1,0:T(8,128)S(1)} %sum.3.refs_0_.whole_ref), channel_id=1, source_target_pairs={{0,8},{2,10},{4,12},{6,14},{8,0},{10,2},{12,4},{14,6},{16,24},{18,... | collective-permute-start | bytes 196616 | tf_op jit(solution)/shard_map/ppermute | solution.py:325
  36.6 4.3 %collective-permute-start.7 = (f32[64,256]{1,0:T(8,128)S(1)}, f32[64,256]{1,0:T(8,128)S(1)}, u32[]{:S(2)}, u32[]{:S(2)}) collective-permute-start(f32[64,256]{1,0:T(8,128)S(1)} %sum.3.refs_0_.whole_ref), channel_id=1, source_target_pairs={{0,4},{2,6},{4,0},{6,2},{8,12},{10,14},{12,8},{14,10},{16,20},{18,... | collective-permute-start | bytes 196616 | tf_op jit(solution)/shard_map/ppermute | solution.py:325
  40.9 1.6 %collective-permute-start.10 = (f32[64,1024]{1,0:T(8,128)S(1)}, f32[64,1024]{1,0:T(8,128)S(1)}, u32[]{:S(2)}, u32[]{:S(2)}) collective-permute-start(f32[64,1024]{1,0:T(8,128)S(1)} %pack.1), channel_id=1, source_target_pairs={{0,2},{2,0},{4,6},{6,4},{8,10},{10,8},{12,14},{14,12},{16,18},{18,... | collective-permute-start | bytes 786440 | tf_op jit(solution)/shard_map/ppermute | solution.py:325
  42.9 5.9 %collective-permute-start.11 = (f32[72,512]{1,0:T(8,128)S(1)}, f32[72,512]{1,0:T(8,128)S(1)}, u32[]{:S(2)}, u32[]{:S(2)}) collective-permute-start(f32[72,512]{1,0:T(8,128)S(1)} %product_second.1.refs_0_), channel_id=1, source_target_pairs={{0,1},{1,0},{2,3},{3,2},{4,5},{5,4},{6,7},{7,6},{8,9},{9,8},{10,11... | collective-permute-start | bytes 442376 | tf_op jit(solution)/shard_map/ppermute | solution.py:335
  49.6 1.4 %collective-permute-start.12 = (f32[72,512]{1,0:T(8,128)S(1)}, f32[72,512]{1,0:T(8,128)S(1)}, u32[]{:S(2)}, u32[]{:S(2)}) collective-permute-start(f32[72,512]{1,0:T(8,128)S(1)} %get-tuple-element.84), channel_id=1, source_target_pairs={{0,2},{2,0},{4,6},{6,4},{8,10},{10,8},{12,14},{14,12},{16,18},{18,... | collective-permute-start | bytes 442376 | tf_op jit(solution)/shard_map/ppermute | solution.py:325
  51.1 4.0 %collective-permute-start.13 = (f32[72,128]{1,0:T(8,128)S(1)}, f32[72,128]{1,0:T(8,128)S(1)}, u32[]{:S(2)}, u32[]{:S(2)}) collective-permute-start(f32[72,128]{1,0:T(8,128)S(1)} %get-tuple-element.87), channel_id=1, source_target_pairs={{0,4},{2,6},{4,0},{6,2},{8,12},{10,14},{12,8},{14,10},{16,20},{18,... | collective-permute-start | bytes 110600 | tf_op jit(solution)/shard_map/ppermute | solution.py:325
  52.6 4.0 %collective-permute-start.14 = (f32[72,128]{1,0:T(8,128)S(1)}, f32[72,128]{1,0:T(8,128)S(1)}, u32[]{:S(2)}, u32[]{:S(2)}) collective-permute-start(f32[72,128]{1,0:T(8,128)S(1)} %get-tuple-element.88), channel_id=1, source_target_pairs={{0,8},{2,10},{4,12},{6,14},{8,0},{10,2},{12,4},{14,6},{16,24},{18,... | collective-permute-start | bytes 110600 | tf_op jit(solution)/shard_map/ppermute | solution.py:325
  52.6 4.9 %collective-permute-start.15 = (f32[72,128]{1,0:T(8,128)S(1)}, f32[72,128]{1,0:T(8,128)S(1)}, u32[]{:S(2)}, u32[]{:S(2)}) collective-permute-start(f32[72,128]{1,0:T(8,128)S(1)} %get-tuple-element.89), channel_id=1, source_target_pairs={{0,12},{2,14},{4,8},{6,10},{8,4},{10,6},{12,0},{14,2},{16,28},{18,... | collective-permute-start | bytes 110600 | tf_op jit(solution)/shard_map/ppermute | solution.py:325

commit v5 on v4

--- a/solution.py
+++ b/solution.py
@@ -20,6 +20,10 @@
 
 def dot(left, right):
     return jnp.dot(left, right, preferred_element_type=f32)
+
+
+def dot_rows(left, right):
+    return lax.dot_general(left, right, (((1,), (1,)), ((), ())), preferred_element_type=f32)
 
 
 def place():
@@ -78,7 +82,12 @@
     return high, low
 
 
-def load_kernel(c_hbm, ch_ref, cl_ref, sq_ref, c_ref, sems):
+def own_block(ref, share):
+    at = lax.rem(place()[0], ref.shape[0] // share) * share
+    return ref[pl.ds(pl.multiple_of(at, share), share), :]
+
+
+def load_kernel(c_hbm, ch_ref, cl_ref, sq_ref, first_ref, c_ref, sems):
     loads = sems.shape[0]
     load = c_ref.shape[0] // loads
     copies = [
@@ -91,20 +100,14 @@
         copy.wait()
         where = slice(i * load, (i + 1) * load)
         rows_in(c_ref[where, :], where, ch_ref, cl_ref, sq_ref)
+    first_ref[...] = own_block(c_ref, first_ref.shape[0])
 
 
 def first_data_kernel(block, x_ref, ch_ref, cl_ref, sq_ref, c_hbm, *refs):
-    kh_ref, kl_ref, xh_ref, xl_ref, xsq_ref, rest_ref, pair_ref, sems = refs
-    half, share = rest_ref.shape[0], pair_ref.shape[0] // 2
-    index, count = place()[0], lax.axis_size("dp")
-    copies = [pltpu.make_async_copy(c_hbm.at[pl.ds(half, half)], rest_ref, sems.at[0])]
-    for t, at in enumerate((index, lax.rem(index + count // 2, count))):
-        where = pl.ds(pl.multiple_of(at * share, share), share)
-        copies.append(
-            pltpu.make_async_copy(c_hbm.at[where], pair_ref.at[pl.ds(t * share, share)], sems.at[1 + t])
-        )
-    for copy in copies:
-        copy.start()
+    kh_ref, kl_ref, xh_ref, xl_ref, xsq_ref, rest_ref, sem = refs
+    half = rest_ref.shape[0]
+    copy = pltpu.make_async_copy(c_hbm.at[pl.ds(half, half)], rest_ref, sem)
+    copy.start()
     xh, xl, xsq = points_in(x_ref[...])
     xh_ref[...] = xh
     xl_ref[...] = xl
@@ -121,13 +124,14 @@
         kl_ref[where, :] = kl
 
     staged(half // block, cross, finish)
-    for copy in copies:
-        copy.wait()
-
-
-def second_data_kernel(block, w_ref, rest_ref, xh_ref, xl_ref, xsq_ref, first_h, first_l, *refs):
-    ch_ref, cl_ref, sq_ref, kh_ref, kl_ref, pred_ref = refs
-    half, outs = rest_ref.shape[0], pred_ref.shape[0]
+    copy.wait()
+
+
+def second_data_kernel(block, w_ref, rest_ref, pair0_ref, xh_ref, xl_ref, xsq_ref, first_h, first_l, *refs):
+    ch_ref, cl_ref, sq_ref, kh_ref, kl_ref, pred_ref, pair_ref = refs
+    half, outs, share = rest_ref.shape[0], pred_ref.shape[0], pair0_ref.shape[0]
+    pair_ref[:share, :] = pair0_ref[...]
+    pair_ref[share:, :] = own_block(rest_ref, share)
 
     def cross(i):
         where = slice(i * block, (i + 1) * block)
@@ -183,47 +187,44 @@
     return [(top, 2 * (mid ^ m) + (core ^ flip)) for m in range(mids) for top in tops]
 
 
-def take(ref, where, share):
-    rows = []
-    for top, block in where:
-        source = ref[top] if isinstance(ref, tuple) else ref
-        at = block if isinstance(ref, tuple) else top * (source.shape[0] // share // 2) + block
-        rows.append(source[pl.ds(pl.multiple_of(at * share, share), share), :])
-    return jnp.concatenate(rows, axis=0)
-
-
-def back(where, share, parts, right):
-    product, at = 0.0, 0
-    for high, low in parts:
-        high, low = take(high, where, share), take(low, where, share)
-        values = right[at : at + high.shape[1]]
-        at += high.shape[1]
-        product = product + (dot(high, values) + dot(low, values))
-    product = product.T
-    outs = right.shape[1] // 2
-    return product[:outs] + product[outs:]
+def take(ref, spot, share):
+    top, block = spot
+    source = ref[top] if isinstance(ref, tuple) else ref
+    at = block if isinstance(ref, tuple) else top * (source.shape[0] // share // 2) + block
+    return source[pl.ds(pl.multiple_of(at * share, share), share), :]
+
+
+def back(where, share, parts, left, out_ref):
+    outs = left.shape[0] // 2
+    for j, spot in enumerate(where):
+        product, at = 0.0, 0
+        for high, low in parts:
+            high, low = take(high, spot, share), take(low, spot, share)
+            values = left[:, at : at + high.shape[1]]
+            at += high.shape[1]
+            product = product + (dot_rows(values, high) + dot_rows(values, low))
+        out_ref[:outs, j * share : (j + 1) * share] = product[:outs] + product[outs:]
 
 
 def grad_kernel(mids, share, *refs):
-    t_ref, kernels, (out_ref, res_ref, right_ref) = refs[-8], refs[-7:-3], refs[-3:]
+    t_ref, kernels, (out_ref, res_ref, left_ref) = refs[-8], refs[-7:-3], refs[-3:]
     total = refs[0][...]
     for ref in refs[1:-8]:
         total = total + ref[...]
     residual = total - t_ref[...]
     res_ref[...] = residual
-    right = jnp.concatenate(split(residual.T), axis=1)
-    right_ref[...] = right
-    out_ref[...] = back(share_blocks(mids, 1), share, [(kernels[:2], kernels[2:])], right)
-
-
-def grad_keep_kernel(mids, share, right_ref, *refs):
-    out_ref = refs[4]
-    out_ref[...] = back(share_blocks(mids, 0), share, [(refs[:2], refs[2:4])], right_ref[...])
+    left = jnp.concatenate(split(residual), axis=0)
+    left_ref[...] = left
+    back(share_blocks(mids, 1), share, [(kernels[:2], kernels[2:])], left, out_ref)
+
+
+def grad_keep_kernel(mids, share, left_ref, *refs):
+    back(share_blocks(mids, 0), share, [(refs[:2], refs[2:4])], left_ref[...], refs[4])
 
 
 def image_kernel(mids, share, shards, *refs):
     kernels = refs[shards : shards + 4]
-    out_ref, right_ref, own_ref, max_ref, image_ref = refs[shards + 4 :]
+    out_ref, left_ref, own_ref, max_ref, image_ref = refs[shards + 4 :]
     outs, size = own_ref.shape[0], 2 * share
     total = refs[0][...]
     for ref in refs[1:shards]:
@@ -234,20 +235,24 @@
     image_ref[...] = total[:outs]
     for j in range(shards):
         part = image_ref[:, pl.ds(shard_at(j, shards, size), size)]
-        right_ref[j * size : (j + 1) * size, :] = jnp.concatenate(split(part.T), axis=1)
+        left_ref[:, j * size : (j + 1) * size] = jnp.concatenate(split(part), axis=0)
         if j == 0:
-            own_ref[...] = part[:, :share]
+            own_ref[...] = jnp.where(place()[3] == 1, part[:, share:], part[:, :share])
     where = share_blocks(mids, 1, [place()[3]])
-    out_ref[:outs, :] = back(where, share, [kernels[:2], kernels[2:]], right_ref[...])
-
-
-def image_keep_kernel(mids, share, right_ref, *refs):
+    back(where, share, [kernels[:2], kernels[2:]], left_ref[...], out_ref)
+
+
+def image_keep_kernel(mids, share, left_ref, *refs):
     where = share_blocks(mids, 0, [place()[3]])
-    refs[-1][...] = back(where, share, [refs[:2], refs[2:4]], right_ref[...])
+    back(where, share, [refs[:2], refs[2:4]], left_ref[...], refs[-1])
 
 
 def shard_at(j, shards, share):
     return pl.multiple_of(lax.rem(lax.axis_index("centre") + j, shards) * share, share)
+
+
+def rows_of(ref, where, share):
+    return jnp.concatenate([take(ref, spot, share) for spot in where], axis=0)
 
 
 def product(mids, share, flip, pieces, kernels):
@@ -256,7 +261,7 @@
     left = jnp.concatenate([high, low], axis=0)
     outs = high.shape[0]
     for kh, kl in (kernels[:2], kernels[2:]):
-        result = dot(left, take(kh, where, share)) + dot(left, take(kl, where, share))
+        result = dot(left, rows_of(kh, where, share)) + dot(left, rows_of(kl, where, share))
         yield result[:outs] + result[outs:]
 
 
@@ -352,15 +357,21 @@
 
     part = rows // 2
     loads = min(4, count)
-    kept = 2 * part * width * 2 + 512 * part
-    loaded = call(
-        load_kernel, "load", [], [like(part, width, dtype=bf16), like(part, width, dtype=bf16), like(part, 1)],
+    kept = 4 * part * width + 512 * part + 4 * share * width
+    *loaded, first = call(
+        load_kernel, "load", [],
+        [
+            like(part, width, dtype=bf16),
+            like(part, width, dtype=bf16),
+            like(part, 1),
+            like(share, width),
+        ],
         [pltpu.VMEM((part, width), f32), pltpu.SemaphoreType.DMA((loads,))],
         room=53 * mega - kept - 4 * points * width, far=[centres],
     )
-    kept = 2 * kept + 8 * points * width + 4 * part * (points + width) + 8 * share * width
-    kh0, kl0, xh, xl, xsq, rest, pair = call(
-        functools.partial(first_data_kernel, block // 2), "data_first", [samples] + list(loaded),
+    kept = 2 * kept + 8 * points * width + 4 * part * (points + width)
+    kh0, kl0, xh, xl, xsq, rest = call(
+        functools.partial(first_data_kernel, block // 2), "data_first", [samples] + loaded,
         [
             like(part, points, dtype=bf16),
             like(part, points, dtype=bf16),
@@ -368,14 +379,13 @@
             like(width, points, dtype=bf16),
             like(1, points),
             like(part, width),
-            like(2 * share, width),
         ],
-        [pltpu.SemaphoreType.DMA((3,))],
+        [pltpu.SemaphoreType.DMA],
         room=107 * mega // 2 - kept, far=[centres],
     )
-    ch, cl, square, kh1, kl1, pred = call(
+    ch, cl, square, kh1, kl1, pred, pair = call(
         functools.partial(second_data_kernel, block // 2), "data_second",
-        [weights, rest, xh, xl, xsq, kh0, kl0],
+        [weights, rest, first, xh, xl, xsq, kh0, kl0],
         [
             like(part, width, dtype=bf16),
             like(part, width, dtype=bf16),
@@ -383,11 +393,13 @@
             like(part, points, dtype=bf16),
             like(part, points, dtype=bf16),
             like(outs, points),
+            like(2 * share, width),
         ],
     )
-    halves = list(loaded) + [ch, cl, square]
+    halves = loaded + [ch, cl, square]
     kernel = [kh0, kh1, kl0, kl1]
     got = [send_far(pred, 0, shift) for shift in range(1, shards)]
+    far = [send_far(pair, 0, -shift) for shift in range(1, shards)]
 
     def centre_tile(blocks, name):
         size = blocks[0].shape[0]
@@ -402,15 +414,15 @@
     own_high, own_low, own_sums = centre_tile([after(pair, pred)], "own_tile")
     got[0] = after(got[0], own_high)
 
-    give, residual, right = call(
+    give, residual, left = call(
         functools.partial(grad_kernel, mids, share), "grad_give",
         [pred] + got + [targets.T] + kernel,
-        [like(outs, half * share), like(outs, points), like(points, 2 * outs, dtype=bf16)],
+        [like(outs, half * share), like(outs, points), like(2 * outs, points, dtype=bf16)],
     )
     received = send_xor(give, 1)
     (keep,) = call(
         functools.partial(grad_keep_kernel, mids, share), "grad_keep",
-        [right] + kernel, [like(outs, half * share)],
+        [left] + kernel, [like(outs, half * share)],
     )
 
     def join(keep, received, extra, height):
@@ -426,9 +438,7 @@
         sent = [send_xor(pieces[m], 2 * m) for m in range(mids - 1, 0, -1)]
         return [pieces[0]] + sent[::-1]
 
-    pieces = spread(join(keep, received, [], outs))
-    far = [send_far(after(pair, received, keep), 0, -shift) for shift in range(1, shards)]
-    part = total(pieces)
+    part = total(spread(join(keep, received, [], outs)))
     whole = total([part, send_xor(part, half)])
     gathered = spread([whole] * mids)
     far_high, far_low, far_sums = centre_tile([after(f, whole) for f in far], "far_tile")
@@ -448,12 +458,12 @@
         [like(outs + 8, 2 * share * shards)],
     )
     images = [image] + [send_far(image, 0, shift) for shift in range(1, shards)]
-    give, right, own, largest = call(
+    give, left, own, largest = call(
         functools.partial(image_kernel, mids, share, shards), "image_give",
         images + kernels,
         [
             like(outs + 8, mids * share),
-            like(2 * share * shards, 2 * outs, dtype=bf16),
+            like(2 * outs, 2 * share * shards, dtype=bf16),
             like(outs, share),
             like(8, share),
         ],
@@ -462,7 +472,7 @@
     received = send_xor(give, 1)
     (keep,) = call(
         functools.partial(image_keep_kernel, mids, share), "image_keep",
-        [right] + kernels, [like(outs, mids * share)],
+        [left] + kernels, [like(outs, mids * share)],
     )
     pieces = spread(join(keep, received, [largest], outs + 8))
     (new_coefficients,) = call(

time: 58.3 us -> 56.3 us (0.966)
  Pallas kernels: 18 us -> 16.2 us
    pallas_call x17, Pallas kernels: 18 us -> 16.2 us  [call(): pl.pallas_call(kernel, name=name, in_specs=[pl.BlockSpec(memory_space=plt...]
    ppermute x3, starting transfers between devices: 5.33 us -> 4.64 us  [send_far(): return lax.ppermute(array, ('dp', 'centre'), pairs)]
  transfers between devices with their start and end apart: 16 -> 16, of which waited for: 13 -> 13; matrix products, arithmetic and copies ran while one was open for 0% -> 0% of each run, Pallas kernels for 11% -> 12%
where the time goes in v5:
time: 56.3 us; the launch traced here: 56.1 us
  waiting for transfers between devices  20.8 us (37%)
  starting transfers between devices  18.3 us (33%)
  Pallas kernels  16.2 us (29%)
  between operations  0.81 us (1%)
    pallas_call x17, Pallas kernels, call(): pl.pallas_call(kernel, name=name, in_specs=[pl.BlockSpec(memory_space=plt...  16.2 us
    ppermute x13, waiting for transfers between devices, send_xor(): return lax.ppermute(array, 'dp', [(i, i ^ mask) for i in range(count)])  14.4 us
    ppermute x13, starting transfers between devices, send_xor(): return lax.ppermute(array, 'dp', [(i, i ^ mask) for i in range(count)])  13.7 us
    ppermute x3, waiting for transfers between devices, send_far(): return lax.ppermute(array, ('dp', 'centre'), pairs)  6.41 us
    ppermute x3, starting transfers between devices, send_far(): return lax.ppermute(array, ('dp', 'centre'), pairs)  4.64 us
  transfers between devices with their start and end apart: 16, of which 13 were waited for; matrix products, arithmetic and copies ran while one was open for 0% of the time, Pallas kernels for 12%

profile of v5, /device:TPU:0, one launch (start us, length us, event | category | flops | bytes accessed | tf_op | source)
XLA Modules:
  0.0 56.1 jit_solution(10564380772438682290)
XLA Ops:
  0.6 2.2 %load.1 = (bf16[1024,512]{1,0:T(8,128)(2,1)S(1)}, bf16[1024,512]{1,0:T(8,128)(2,1)S(1)}, f32[1024,1]{1,0:T(8,128)S(1)}, f32[128,512]{1,0:T(8,128)S(1)}) custom-call(f32[2048,512]{1,0:T(8,128)} %c_hbm.3), custom_call_target="tpu_custom_call" | custom-call | tf_op jit(solution)/shard_map/load/pallas_call | solution.py:39
  2.8 2.3 %data_first.1 = (bf16[1024,512]{1,0:T(8,128)(2,1)S(1)}, bf16[1024,512]{1,0:T(8,128)(2,1)S(1)}, bf16[512,512]{1,0:T(8,128)(2,1)S(1)}, bf16[512,512]{1,0:T(8,128)(...) custom-call(f32[512,512]{1,0:T(8,128)S(1)} %copy-done.1, ...), custom_call_target="tpu_custom_call" | custom-call | tf_op jit(solution)/shard_map/data_first/pallas_call | solution.py:39
  5.2 3.1 %data_second.1 = (bf16[1024,512]{1,0:T(8,128)(2,1)S(1)}, bf16[1024,512]{1,0:T(8,128)(2,1)S(1)}, f32[1024,1]{1,0:T(8,128)S(1)}, bf16[1024,512]{1,0:T(8,128)(2,1)S...) custom-call(f32[64,2048]{1,0:T(8,128)S(1)} %bitcast.4, ...), custom_call_target="tpu_custom_call" | custom-call | tf_op jit(solution)/shard_map/data_second/pallas_call | solution.py:39
  8.3 3.0 %collective-permute-start = (f32[64,512]{1,0:T(8,128)S(1)}, f32[64,512]{1,0:T(8,128)S(1)}, u32[]{:S(2)}, u32[]{:S(2)}) collective-permute-start(f32[64,512]{1,0:T(8,128)S(1)} %get-tuple-element.56.refs_0_), channel_id=1, source_target_pairs={{0,1},{1,0},{2,3},{3,2},{4,5},{5,4},{6,7},{7,6},{8,9},{9,8},{10,11... | collective-permute-start | bytes 393224 | tf_op jit(solution)/shard_map/ppermute | solution.py:340
  11.3 2.2 %own_tile.1 = (bf16[2048,256]{1,0:T(8,128)(2,1)S(1)}, bf16[2048,256]{1,0:T(8,128)(2,1)S(1)}, f32[8,256]{1,0:T(8,128)S(1)}) custom-call(f32[256,512]{1,0:T(8,128)S(1)} %get-tuple-element.58.refs_0_, bf16[1024,512]{1,0:T(8,128)(2,1)S(1)} %get-tuple-element.46.ch_ref.refs_1_, bf16[1024,512]{1,0:T(8,128)(2,1)S(1)} %get-tuple-element.47.cl_ref.refs_2_, ...), custom_call_target="tpu_custom_call" | custom-call | flops 1610612736 | tf_op jit(solution)/shard_map/own_tile/pallas_call | solution.py:39
  13.6 2.0 %collective-permute-done.refs_1_ = f32[64,512]{1,0:T(8,128)S(1)} collective-permute-done((f32[64,512]{1,0:T(8,128)S(1)}, f32[64,512]{1,0:T(8,128)S(1)}, u32[]{:S(2)}, u32[]{:S(2)}) %collective-permute-start) | collective-permute-done | bytes 131104 | tf_op jit(solution)/shard_map/ppermute | solution.py:340
  18.0 2.2 %collective-permute-start.2 = (f32[64,256]{1,0:T(8,128)S(1)}, f32[64,256]{1,0:T(8,128)S(1)}, u32[]{:S(2)}, u32[]{:S(2)}) collective-permute-start(f32[64,256]{1,0:T(8,128)S(1)} %get-tuple-element.70), channel_id=1, source_target_pairs={{0,4},{2,6},{4,0},{6,2},{8,12},{10,14},{12,8},{14,10},{16,20},{18,... | collective-permute-start | bytes 196616 | tf_op jit(solution)/shard_map/ppermute | solution.py:330
  20.1 1.6 %collective-permute-start.3 = (f32[64,256]{1,0:T(8,128)S(1)}, f32[64,256]{1,0:T(8,128)S(1)}, u32[]{:S(2)}, u32[]{:S(2)}) collective-permute-start(f32[64,256]{1,0:T(8,128)S(1)} %get-tuple-element.71), channel_id=1, source_target_pairs={{0,8},{2,10},{4,12},{6,14},{8,0},{10,2},{12,4},{14,6},{16,24},{18,... | collective-permute-start | bytes 196616 | tf_op jit(solution)/shard_map/ppermute | solution.py:330
  21.7 0.8 %collective-permute-done.2.refs_1_ = f32[64,256]{1,0:T(8,128)S(1)} collective-permute-done((f32[64,256]{1,0:T(8,128)S(1)}, f32[64,256]{1,0:T(8,128)S(1)}, u32[]{:S(2)}, u32[]{:S(2)}) %collective-permute-start.2) | collective-permute-done | bytes 65568 | tf_op jit(solution)/shard_map/ppermute | solution.py:330
  22.5 2.5 %collective-permute-done.3.refs_2_ = f32[64,256]{1,0:T(8,128)S(1)} collective-permute-done((f32[64,256]{1,0:T(8,128)S(1)}, f32[64,256]{1,0:T(8,128)S(1)}, u32[]{:S(2)}, u32[]{:S(2)}) %collective-permute-start.3) | collective-permute-done | bytes 65568 | tf_op jit(solution)/shard_map/ppermute | solution.py:330
  25.0 1.9 %collective-permute-done.4.refs_3_ = f32[64,256]{1,0:T(8,128)S(1)} collective-permute-done((f32[64,256]{1,0:T(8,128)S(1)}, f32[64,256]{1,0:T(8,128)S(1)}, u32[]{:S(2)}, u32[]{:S(2)}) %collective-permute-start.4) | collective-permute-done | bytes 65568 | tf_op jit(solution)/shard_map/ppermute | solution.py:330
  26.9 2.7 %collective-permute-start.5 = (f32[64,256]{1,0:T(8,128)S(1)}, f32[64,256]{1,0:T(8,128)S(1)}, u32[]{:S(2)}, u32[]{:S(2)}) collective-permute-start(f32[64,256]{1,0:T(8,128)S(1)} %sum.2.refs_0_), channel_id=1, source_target_pairs={{0,16},{2,18},{4,20},{6,22},{8,24},{10,26},{12,28},{14,30},{16,0},... | collective-permute-start | bytes 196616 | tf_op jit(solution)/shard_map/ppermute | solution.py:330
  29.5 3.2 %collective-permute-done.5.refs_1_ = f32[64,256]{1,0:T(8,128)S(1)} collective-permute-done((f32[64,256]{1,0:T(8,128)S(1)}, f32[64,256]{1,0:T(8,128)S(1)}, u32[]{:S(2)}, u32[]{:S(2)}) %collective-permute-start.5) | collective-permute-done | bytes 65568 | tf_op jit(solution)/shard_map/ppermute | solution.py:330
  33.3 1.6 %collective-permute-start.8 = (f32[64,256]{1,0:T(8,128)S(1)}, f32[64,256]{1,0:T(8,128)S(1)}, u32[]{:S(2)}, u32[]{:S(2)}) collective-permute-start(f32[64,256]{1,0:T(8,128)S(1)} %sum.3.refs_0_.whole_ref), channel_id=1, source_target_pairs={{0,8},{2,10},{4,12},{6,14},{8,0},{10,2},{12,4},{14,6},{16,24},{18,... | collective-permute-start | bytes 196616 | tf_op jit(solution)/shard_map/ppermute | solution.py:330
  34.9 1.4 %collective-permute-start.7 = (f32[64,256]{1,0:T(8,128)S(1)}, f32[64,256]{1,0:T(8,128)S(1)}, u32[]{:S(2)}, u32[]{:S(2)}) collective-permute-start(f32[64,256]{1,0:T(8,128)S(1)} %sum.3.refs_0_.whole_ref), channel_id=1, source_target_pairs={{0,4},{2,6},{4,0},{6,2},{8,12},{10,14},{12,8},{14,10},{16,20},{18,... | collective-permute-start | bytes 196616 | tf_op jit(solution)/shard_map/ppermute | solution.py:330
  36.3 2.2 %far_tile.1 = (bf16[2048,256]{1,0:T(8,128)(2,1)S(1)}, bf16[2048,256]{1,0:T(8,128)(2,1)S(1)}, f32[8,256]{1,0:T(8,128)S(1)}) custom-call(f32[256,512]{1,0:T(8,128)S(1)} %collective-permute-done.6.refs_0_, bf16[1024,512]{1,0:T(8,128)(2,1)S(1)} %get-tuple-element.46.ch_ref.refs_1_, bf16[1024,512]{1,0:T(8,128)(2,1)S(1)} %get-tuple-element.47.cl_ref.refs_2_, ...), custom_call_target="tpu_custom_call" | custom-call | flops 1610612736 | tf_op jit(solution)/shard_map/far_tile/pallas_call | solution.py:39
  39.7 1.0 %collective-permute-done.10.refs_0_ = f32[64,1024]{1,0:T(8,128)S(1)} collective-permute-done((f32[64,1024]{1,0:T(8,128)S(1)}, f32[64,1024]{1,0:T(8,128)S(1)}, u32[]{:S(2)}, u32[]{:S(2)}) %collective-permute-start.10) | collective-permute-done | bytes 262176 | tf_op jit(solution)/shard_map/ppermute | solution.py:330
  41.2 1.6 %collective-permute-start.11 = (f32[72,512]{1,0:T(8,128)S(1)}, f32[72,512]{1,0:T(8,128)S(1)}, u32[]{:S(2)}, u32[]{:S(2)}) collective-permute-start(f32[72,512]{1,0:T(8,128)S(1)} %product_second.1.refs_0_), channel_id=1, source_target_pairs={{0,1},{1,0},{2,3},{3,2},{4,5},{5,4},{6,7},{7,6},{8,9},{9,8},{10,11... | collective-permute-start | bytes 442376 | tf_op jit(solution)/shard_map/ppermute | solution.py:340
  42.8 4.4 %collective-permute-done.11.refs_1_ = f32[72,512]{1,0:T(8,128)S(1)} collective-permute-done((f32[72,512]{1,0:T(8,128)S(1)}, f32[72,512]{1,0:T(8,128)S(1)}, u32[]{:S(2)}, u32[]{:S(2)}) %collective-permute-start.11) | collective-permute-done | bytes 147488 | tf_op jit(solution)/shard_map/ppermute | solution.py:340
  48.2 0.9 %collective-permute-done.12.got_ref = f32[72,512]{1,0:T(8,128)S(1)} collective-permute-done((f32[72,512]{1,0:T(8,128)S(1)}, f32[72,512]{1,0:T(8,128)S(1)}, u32[]{:S(2)}, u32[]{:S(2)}) %collective-permute-start.12) | collective-permute-done | bytes 147488 | tf_op jit(solution)/shard_map/ppermute | solution.py:330
  49.2 1.4 %collective-permute-start.13 = (f32[72,128]{1,0:T(8,128)S(1)}, f32[72,128]{1,0:T(8,128)S(1)}, u32[]{:S(2)}, u32[]{:S(2)}) collective-permute-start(f32[72,128]{1,0:T(8,128)S(1)} %get-tuple-element.87), channel_id=1, source_target_pairs={{0,4},{2,6},{4,0},{6,2},{8,12},{10,14},{12,8},{14,10},{16,20},{18,... | collective-permute-start | bytes 110600 | tf_op jit(solution)/shard_map/ppermute | solution.py:330
  50.6 2.1 %collective-permute-start.15 = (f32[72,128]{1,0:T(8,128)S(1)}, f32[72,128]{1,0:T(8,128)S(1)}, u32[]{:S(2)}, u32[]{:S(2)}) collective-permute-start(f32[72,128]{1,0:T(8,128)S(1)} %get-tuple-element.89), channel_id=1, source_target_pairs={{0,12},{2,14},{4,8},{6,10},{8,4},{10,6},{12,0},{14,2},{16,28},{18,... | collective-permute-start | bytes 110600 | tf_op jit(solution)/shard_map/ppermute | solution.py:330
  53.1 1.4 %collective-permute-done.14.refs_2_ = f32[72,128]{1,0:T(8,128)S(1)} collective-permute-done((f32[72,128]{1,0:T(8,128)S(1)}, f32[72,128]{1,0:T(8,128)S(1)}, u32[]{:S(2)}, u32[]{:S(2)}) %collective-permute-start.14) | collective-permute-done | bytes 36896 | tf_op jit(solution)/shard_map/ppermute | solution.py:330
  54.6 0.9 %collective-permute-done.15.refs_3_ = f32[72,128]{1,0:T(8,128)S(1)} collective-permute-done((f32[72,128]{1,0:T(8,128)S(1)}, f32[72,128]{1,0:T(8,128)S(1)}, u32[]{:S(2)}, u32[]{:S(2)}) %collective-permute-start.15) | collective-permute-done | bytes 36896 | tf_op jit(solution)/shard_map/ppermute | solution.py:330
  (31 shorter events, 6.9 us)
Async XLA Ops:
  0.6 2.2 %copy-start.1 = (f32[512,512]{1,0:T(8,128)S(1)}, f32[512,512]{1,0:T(8,128)}, u32[]{:S(2)}) copy-start(f32[512,512]{1,0:T(8,128)} %x_ref.1) | copy-start | bytes 3145732
  2.8 2.4 %copy-start = (f32[2048,64]{0,1:T(8,128)S(1)}, f32[2048,64]{0,1:T(8,128)}, u32[]{:S(2)}) copy-start(f32[2048,64]{0,1:T(8,128)} %param.7) | copy-start | bytes 1572868
  8.3 7.3 %copy-start.2 = (f32[512,64]{0,1:T(8,128)S(1)}, f32[512,64]{0,1:T(8,128)}, u32[]{:S(2)}) copy-start(f32[512,64]{0,1:T(8,128)} %param.5) | copy-start | bytes 393220
  8.3 7.3 %collective-permute-start = (f32[64,512]{1,0:T(8,128)S(1)}, f32[64,512]{1,0:T(8,128)S(1)}, u32[]{:S(2)}, u32[]{:S(2)}) collective-permute-start(f32[64,512]{1,0:T(8,128)S(1)} %get-tuple-element.56.refs_0_), channel_id=1, source_target_pairs={{0,1},{1,0},{2,3},{3,2},{4,5},{5,4},{6,7},{7,6},{8,9},{9,8},{10,11... | collective-permute-start | bytes 393224 | tf_op jit(solution)/shard_map/ppermute | solution.py:340
  11.3 25.0 %collective-permute-start.6 = (f32[256,512]{1,0:T(8,128)S(1)}, f32[256,512]{1,0:T(8,128)S(1)}, u32[]{:S(2)}, u32[]{:S(2)}) collective-permute-start(f32[256,512]{1,0:T(8,128)S(1)} %get-tuple-element.58.refs_0_), channel_id=1, source_target_pairs={{0,1},{1,0},{2,3},{3,2},{4,5},{5,4},{6,7},{7,6},{8,9},{9,8},{10,11... | collective-permute-start | bytes 1572872 | tf_op jit(solution)/shard_map/ppermute | solution.py:340
  16.3 1.6 %collective-permute-start.1 = (f32[64,1024]{1,0:T(8,128)S(1)}, f32[64,1024]{1,0:T(8,128)S(1)}, u32[]{:S(2)}, u32[]{:S(2)}) collective-permute-start(f32[64,1024]{1,0:T(8,128)S(1)} %get-tuple-element.68), channel_id=1, source_target_pairs={{0,2},{2,0},{4,6},{6,4},{8,10},{10,8},{12,14},{14,12},{16,18},{18,... | collective-permute-start | bytes 786440 | tf_op jit(solution)/shard_map/ppermute | solution.py:330
  18.0 4.5 %collective-permute-start.2 = (f32[64,256]{1,0:T(8,128)S(1)}, f32[64,256]{1,0:T(8,128)S(1)}, u32[]{:S(2)}, u32[]{:S(2)}) collective-permute-start(f32[64,256]{1,0:T(8,128)S(1)} %get-tuple-element.70), channel_id=1, source_target_pairs={{0,4},{2,6},{4,0},{6,2},{8,12},{10,14},{12,8},{14,10},{16,20},{18,... | collective-permute-start | bytes 196616 | tf_op jit(solution)/shard_map/ppermute | solution.py:330
  20.1 4.8 %collective-permute-start.3 = (f32[64,256]{1,0:T(8,128)S(1)}, f32[64,256]{1,0:T(8,128)S(1)}, u32[]{:S(2)}, u32[]{:S(2)}) collective-permute-start(f32[64,256]{1,0:T(8,128)S(1)} %get-tuple-element.71), channel_id=1, source_target_pairs={{0,8},{2,10},{4,12},{6,14},{8,0},{10,2},{12,4},{14,6},{16,24},{18,... | collective-permute-start | bytes 196616 | tf_op jit(solution)/shard_map/ppermute | solution.py:330
  21.7 5.2 %collective-permute-start.4 = (f32[64,256]{1,0:T(8,128)S(1)}, f32[64,256]{1,0:T(8,128)S(1)}, u32[]{:S(2)}, u32[]{:S(2)}) collective-permute-start(f32[64,256]{1,0:T(8,128)S(1)} %get-tuple-element.72), channel_id=1, source_target_pairs={{0,12},{2,14},{4,8},{6,10},{8,4},{10,6},{12,0},{14,2},{16,28},{18,... | collective-permute-start | bytes 196616 | tf_op jit(solution)/shard_map/ppermute | solution.py:330
  26.9 5.8 %collective-permute-start.5 = (f32[64,256]{1,0:T(8,128)S(1)}, f32[64,256]{1,0:T(8,128)S(1)}, u32[]{:S(2)}, u32[]{:S(2)}) collective-permute-start(f32[64,256]{1,0:T(8,128)S(1)} %sum.2.refs_0_), channel_id=1, source_target_pairs={{0,16},{2,18},{4,20},{6,22},{8,24},{10,26},{12,28},{14,30},{16,0},... | collective-permute-start | bytes 196616 | tf_op jit(solution)/shard_map/ppermute | solution.py:330
  32.7 5.8 %collective-permute-start.9 = (f32[64,256]{1,0:T(8,128)S(1)}, f32[64,256]{1,0:T(8,128)S(1)}, u32[]{:S(2)}, u32[]{:S(2)}) collective-permute-start(f32[64,256]{1,0:T(8,128)S(1)} %sum.3.refs_0_.whole_ref), channel_id=1, source_target_pairs={{0,12},{2,14},{4,8},{6,10},{8,4},{10,6},{12,0},{14,2},{16,28},{18,... | collective-permute-start | bytes 196616 | tf_op jit(solution)/shard_map/ppermute | solution.py:330
  33.3 5.2 %collective-permute-start.8 = (f32[64,256]{1,0:T(8,128)S(1)}, f32[64,256]{1,0:T(8,128)S(1)}, u32[]{:S(2)}, u32[]{:S(2)}) collective-permute-start(f32[64,256]{1,0:T(8,128)S(1)} %sum.3.refs_0_.whole_ref), channel_id=1, source_target_pairs={{0,8},{2,10},{4,12},{6,14},{8,0},{10,2},{12,4},{14,6},{16,24},{18,... | collective-permute-start | bytes 196616 | tf_op jit(solution)/shard_map/ppermute | solution.py:330
  34.9 4.3 %collective-permute-start.7 = (f32[64,256]{1,0:T(8,128)S(1)}, f32[64,256]{1,0:T(8,128)S(1)}, u32[]{:S(2)}, u32[]{:S(2)}) collective-permute-start(f32[64,256]{1,0:T(8,128)S(1)} %sum.3.refs_0_.whole_ref), channel_id=1, source_target_pairs={{0,4},{2,6},{4,0},{6,2},{8,12},{10,14},{12,8},{14,10},{16,20},{18,... | collective-permute-start | bytes 196616 | tf_op jit(solution)/shard_map/ppermute | solution.py:330
  39.1 1.6 %collective-permute-start.10 = (f32[64,1024]{1,0:T(8,128)S(1)}, f32[64,1024]{1,0:T(8,128)S(1)}, u32[]{:S(2)}, u32[]{:S(2)}) collective-permute-start(f32[64,1024]{1,0:T(8,128)S(1)} %pack.1), channel_id=1, source_target_pairs={{0,2},{2,0},{4,6},{6,4},{8,10},{10,8},{12,14},{14,12},{16,18},{18,... | collective-permute-start | bytes 786440 | tf_op jit(solution)/shard_map/ppermute | solution.py:330
  41.2 5.9 %collective-permute-start.11 = (f32[72,512]{1,0:T(8,128)S(1)}, f32[72,512]{1,0:T(8,128)S(1)}, u32[]{:S(2)}, u32[]{:S(2)}) collective-permute-start(f32[72,512]{1,0:T(8,128)S(1)} %product_second.1.refs_0_), channel_id=1, source_target_pairs={{0,1},{1,0},{2,3},{3,2},{4,5},{5,4},{6,7},{7,6},{8,9},{9,8},{10,11... | collective-permute-start | bytes 442376 | tf_op jit(solution)/shard_map/ppermute | solution.py:340
  47.7 1.4 %collective-permute-start.12 = (f32[72,512]{1,0:T(8,128)S(1)}, f32[72,512]{1,0:T(8,128)S(1)}, u32[]{:S(2)}, u32[]{:S(2)}) collective-permute-start(f32[72,512]{1,0:T(8,128)S(1)} %get-tuple-element.84), channel_id=1, source_target_pairs={{0,2},{2,0},{4,6},{6,4},{8,10},{10,8},{12,14},{14,12},{16,18},{18,... | collective-permute-start | bytes 442376 | tf_op jit(solution)/shard_map/ppermute | solution.py:330
  49.2 4.0 %collective-permute-start.13 = (f32[72,128]{1,0:T(8,128)S(1)}, f32[72,128]{1,0:T(8,128)S(1)}, u32[]{:S(2)}, u32[]{:S(2)}) collective-permute-start(f32[72,128]{1,0:T(8,128)S(1)} %get-tuple-element.87), channel_id=1, source_target_pairs={{0,4},{2,6},{4,0},{6,2},{8,12},{10,14},{12,8},{14,10},{16,20},{18,... | collective-permute-start | bytes 110600 | tf_op jit(solution)/shard_map/ppermute | solution.py:330
  50.6 4.0 %collective-permute-start.14 = (f32[72,128]{1,0:T(8,128)S(1)}, f32[72,128]{1,0:T(8,128)S(1)}, u32[]{:S(2)}, u32[]{:S(2)}) collective-permute-start(f32[72,128]{1,0:T(8,128)S(1)} %get-tuple-element.88), channel_id=1, source_target_pairs={{0,8},{2,10},{4,12},{6,14},{8,0},{10,2},{12,4},{14,6},{16,24},{18,... | collective-permute-start | bytes 110600 | tf_op jit(solution)/shard_map/ppermute | solution.py:330
  50.6 4.9 %collective-permute-start.15 = (f32[72,128]{1,0:T(8,128)S(1)}, f32[72,128]{1,0:T(8,128)S(1)}, u32[]{:S(2)}, u32[]{:S(2)}) collective-permute-start(f32[72,128]{1,0:T(8,128)S(1)} %get-tuple-element.89), channel_id=1, source_target_pairs={{0,12},{2,14},{4,8},{6,10},{8,4},{10,6},{12,0},{14,2},{16,28},{18,... | collective-permute-start | bytes 110600 | tf_op jit(solution)/shard_map/ppermute | solution.py:330

commit v6 on v5

--- a/solution.py
+++ b/solution.py
@@ -49,11 +49,15 @@
     )(*ins, *far)
 
 
+def pieces_of(x):
+    high = x.astype(bf16)
+    wide = high.astype(f32)
+    return high, (x - wide).astype(bf16), ((x - wide) + x) * wide
+
+
 def points_in(x):
-    high, low = split(x.T)
-    wide, rest = high.astype(f32), low.astype(f32)
-    square = jnp.sum(wide * wide + 2.0 * (wide * rest), axis=0, keepdims=True)
-    return (-2.0 * wide).astype(bf16), (-2.0 * rest).astype(bf16), square
+    high, low, terms = pieces_of(-2.0 * x.T)
+    return high, low, jnp.sum(terms, axis=0, keepdims=True) * 0.25
 
 
 def crossed(high, low, xh, xl):
@@ -74,11 +78,10 @@
 
 
 def rows_in(x, where, high_ref, low_ref, square_ref):
-    high, low = split(x)
-    wide, rest = high.astype(f32), low.astype(f32)
+    high, low, terms = pieces_of(x)
     high_ref[where, :] = high
     low_ref[where, :] = low
-    square_ref[where, :] = jnp.sum(wide * wide + 2.0 * (wide * rest), axis=1, keepdims=True)
+    square_ref[where, :] = jnp.sum(terms, axis=1, keepdims=True)
     return high, low
 
 
@@ -87,7 +90,7 @@
     return ref[pl.ds(pl.multiple_of(at, share), share), :]
 
 
-def load_kernel(c_hbm, ch_ref, cl_ref, sq_ref, first_ref, c_ref, sems):
+def load_kernel(c_hbm, ch_ref, cl_ref, sq_ref, first_ref, shift_ref, c_ref, sems):
     loads = sems.shape[0]
     load = c_ref.shape[0] // loads
     copies = [
@@ -99,16 +102,18 @@
     for i, copy in enumerate(copies):
         copy.wait()
         where = slice(i * load, (i + 1) * load)
-        rows_in(c_ref[where, :], where, ch_ref, cl_ref, sq_ref)
+        if i == 0:
+            shift_ref[...] = jnp.sum(c_ref[where, :], axis=0, keepdims=True) * (1.0 / load)
+        rows_in(c_ref[where, :] - shift_ref[...], where, ch_ref, cl_ref, sq_ref)
     first_ref[...] = own_block(c_ref, first_ref.shape[0])
 
 
-def first_data_kernel(block, x_ref, ch_ref, cl_ref, sq_ref, c_hbm, *refs):
+def first_data_kernel(block, x_ref, shift_ref, ch_ref, cl_ref, sq_ref, c_hbm, *refs):
     kh_ref, kl_ref, xh_ref, xl_ref, xsq_ref, rest_ref, sem = refs
     half = rest_ref.shape[0]
     copy = pltpu.make_async_copy(c_hbm.at[pl.ds(half, half)], rest_ref, sem)
     copy.start()
-    xh, xl, xsq = points_in(x_ref[...])
+    xh, xl, xsq = points_in(x_ref[...] - shift_ref[...])
     xh_ref[...] = xh
     xl_ref[...] = xl
     xsq_ref[...] = xsq
@@ -127,7 +132,7 @@
     copy.wait()
 
 
-def second_data_kernel(block, w_ref, rest_ref, pair0_ref, xh_ref, xl_ref, xsq_ref, first_h, first_l, *refs):
+def second_data_kernel(block, w_ref, rest_ref, pair0_ref, shift_ref, xh_ref, xl_ref, xsq_ref, first_h, first_l, *refs):
     ch_ref, cl_ref, sq_ref, kh_ref, kl_ref, pred_ref, pair_ref = refs
     half, outs, share = rest_ref.shape[0], pred_ref.shape[0], pair0_ref.shape[0]
     pair_ref[:share, :] = pair0_ref[...]
@@ -135,7 +140,7 @@
 
     def cross(i):
         where = slice(i * block, (i + 1) * block)
-        high, low = rows_in(rest_ref[where, :], where, ch_ref, cl_ref, sq_ref)
+        high, low = rows_in(rest_ref[where, :] - shift_ref[...], where, ch_ref, cl_ref, sq_ref)
         return crossed(high, low, xh_ref[...], xl_ref[...])
 
     def finish(i, value):
@@ -152,14 +157,14 @@
 
 
 def centre_kernel(block, *refs):
-    x_refs, centres = refs[:-11], (refs[-11:-8], refs[-8:-5])
+    x_refs, shift_ref, centres = refs[:-12], refs[-12], (refs[-11:-8], refs[-8:-5])
     kh_ref, kl_ref, sum_ref, xh_ref, xl_ref = refs[-5:]
     half = centres[0][0].shape[0]
     at = 0
     for x_ref in x_refs:
         span = slice(at, at + x_ref.shape[0])
         at = span.stop
-        xh, xl, xsq = points_in(x_ref[...])
+        xh, xl, xsq = points_in(x_ref[...] - shift_ref[...])
         xh_ref[...] = xh
         xl_ref[...] = xl
         sums = []
@@ -358,20 +363,21 @@
     part = rows // 2
     loads = min(4, count)
     kept = 4 * part * width + 512 * part + 4 * share * width
-    *loaded, first = call(
+    *loaded, first, shift = call(
         load_kernel, "load", [],
         [
             like(part, width, dtype=bf16),
             like(part, width, dtype=bf16),
             like(part, 1),
             like(share, width),
+            like(1, width),
         ],
         [pltpu.VMEM((part, width), f32), pltpu.SemaphoreType.DMA((loads,))],
         room=53 * mega - kept - 4 * points * width, far=[centres],
     )
     kept = 2 * kept + 8 * points * width + 4 * part * (points + width)
     kh0, kl0, xh, xl, xsq, rest = call(
-        functools.partial(first_data_kernel, block // 2), "data_first", [samples] + loaded,
+        functools.partial(first_data_kernel, block // 2), "data_first", [samples, shift] + loaded,
         [
             like(part, points, dtype=bf16),
             like(part, points, dtype=bf16),
@@ -385,7 +391,7 @@
     )
     ch, cl, square, kh1, kl1, pred, pair = call(
         functools.partial(second_data_kernel, block // 2), "data_second",
-        [weights, rest, first, xh, xl, xsq, kh0, kl0],
+        [weights, rest, first, shift, xh, xl, xsq, kh0, kl0],
         [
             like(part, width, dtype=bf16),
             like(part, width, dtype=bf16),
@@ -405,7 +411,7 @@
         size = blocks[0].shape[0]
         columns = size * len(blocks)
         return call(
-            functools.partial(centre_kernel, block // 2), name, blocks + halves,
+            functools.partial(centre_kernel, block // 2), name, blocks + [shift] + halves,
             [like(rows, columns, dtype=bf16), like(rows, columns, dtype=bf16), like(8, columns)],
             [pltpu.VMEM((width, size), bf16), pltpu.VMEM((width, size), bf16)],
             flops=6 * rows * columns * width,

time: 56.3 us -> 56.3 us (level)
  no operation moved by 1% of the time
where the time goes in v6:
time: 56.3 us; the launch traced here: 56.2 us
  waiting for transfers between devices  20.7 us (37%)
  starting transfers between devices  18.3 us (33%)
  Pallas kernels  16.3 us (29%)
  between operations  0.81 us (1%)
    pallas_call x17, Pallas kernels, call(): pl.pallas_call(kernel, name=name, in_specs=[pl.BlockSpec(memory_space=plt...  16.3 us
    ppermute x13, waiting for transfers between devices, send_xor(): return lax.ppermute(array, 'dp', [(i, i ^ mask) for i in range(count)])  14.4 us
    ppermute x13, starting transfers between devices, send_xor(): return lax.ppermute(array, 'dp', [(i, i ^ mask) for i in range(count)])  13.7 us
    ppermute x3, waiting for transfers between devices, send_far(): return lax.ppermute(array, ('dp', 'centre'), pairs)  6.37 us
    ppermute x3, starting transfers between devices, send_far(): return lax.ppermute(array, ('dp', 'centre'), pairs)  4.64 us
  transfers between devices with their start and end apart: 16, of which 13 were waited for; matrix products, arithmetic and copies ran while one was open for 0% of the time, Pallas kernels for 12%

profile of v6, /device:TPU:0, one launch (start us, length us, event | category | flops | bytes accessed | tf_op | source)
XLA Modules:
  0.0 56.2 jit_solution(456256115237801630)
XLA Ops:
  0.6 2.1 %load.1 = (bf16[1024,512]{1,0:T(8,128)(2,1)S(1)}, bf16[1024,512]{1,0:T(8,128)(2,1)S(1)}, f32[1024,1]{1,0:T(8,128)S(1)}, f32[128,512]{1,0:T(8,128)S(1)}, f32[1,512]{1,0:T(1,128)S(1)}) custom-call(f32[2048,512]{1,0:T(8,128)} %c_hbm.3), custom_call_target="tpu_custom_call" | custom-call | tf_op jit(solution)/shard_map/load/pallas_call | solution.py:39
  2.7 2.4 %data_first.1 = (bf16[1024,512]{1,0:T(8,128)(2,1)S(1)}, bf16[1024,512]{1,0:T(8,128)(2,1)S(1)}, bf16[512,512]{1,0:T(8,128)(2,1)S(1)}, bf16[512,512]{1,0:T(8,128)(...) custom-call(f32[512,512]{1,0:T(8,128)S(1)} %copy-done.1, f32[1,512]{1,0:T(1,128)S(1)} %get-tuple-element.47.shift_ref.refs_1_, ...), custom_call_target="tpu_custom_call" | custom-call | tf_op jit(solution)/shard_map/data_first/pallas_call | solution.py:39
  5.1 3.2 %data_second.1 = (bf16[1024,512]{1,0:T(8,128)(2,1)S(1)}, bf16[1024,512]{1,0:T(8,128)(2,1)S(1)}, f32[1024,1]{1,0:T(8,128)S(1)}, bf16[1024,512]{1,0:T(8,128)(2,1)S...) custom-call(f32[64,2048]{1,0:T(8,128)S(1)} %bitcast.4, ...), custom_call_target="tpu_custom_call" | custom-call | tf_op jit(solution)/shard_map/data_second/pallas_call | solution.py:39
  8.3 3.0 %collective-permute-start = (f32[64,512]{1,0:T(8,128)S(1)}, f32[64,512]{1,0:T(8,128)S(1)}, u32[]{:S(2)}, u32[]{:S(2)}) collective-permute-start(f32[64,512]{1,0:T(8,128)S(1)} %get-tuple-element.58.refs_0_), channel_id=1, source_target_pairs={{0,1},{1,0},{2,3},{3,2},{4,5},{5,4},{6,7},{7,6},{8,9},{9,8},{10,11... | collective-permute-start | bytes 393224 | tf_op jit(solution)/shard_map/ppermute | solution.py:345
  11.4 2.3 %own_tile.1 = (bf16[2048,256]{1,0:T(8,128)(2,1)S(1)}, bf16[2048,256]{1,0:T(8,128)(2,1)S(1)}, f32[8,256]{1,0:T(8,128)S(1)}) custom-call(f32[256,512]{1,0:T(8,128)S(1)} %get-tuple-element.60.refs_0_, f32[1,512]{1,0:T(1,128)S(1)} %get-tuple-element.47.shift_ref.refs_1_, bf16[1024,512]{1,0:T(8,128)(2,1)S(1)} %get-tuple-element.48.ch_ref.refs_2_, ...), custom_call_target="tpu_custom_call" | custom-call | flops 1610612736 | tf_op jit(solution)/shard_map/own_tile/pallas_call | solution.py:39
  13.7 2.0 %collective-permute-done.refs_1_ = f32[64,512]{1,0:T(8,128)S(1)} collective-permute-done((f32[64,512]{1,0:T(8,128)S(1)}, f32[64,512]{1,0:T(8,128)S(1)}, u32[]{:S(2)}, u32[]{:S(2)}) %collective-permute-start) | collective-permute-done | bytes 131104 | tf_op jit(solution)/shard_map/ppermute | solution.py:345
  18.0 2.2 %collective-permute-start.2 = (f32[64,256]{1,0:T(8,128)S(1)}, f32[64,256]{1,0:T(8,128)S(1)}, u32[]{:S(2)}, u32[]{:S(2)}) collective-permute-start(f32[64,256]{1,0:T(8,128)S(1)} %get-tuple-element.72), channel_id=1, source_target_pairs={{0,4},{2,6},{4,0},{6,2},{8,12},{10,14},{12,8},{14,10},{16,20},{18,... | collective-permute-start | bytes 196616 | tf_op jit(solution)/shard_map/ppermute | solution.py:335
  20.2 1.6 %collective-permute-start.3 = (f32[64,256]{1,0:T(8,128)S(1)}, f32[64,256]{1,0:T(8,128)S(1)}, u32[]{:S(2)}, u32[]{:S(2)}) collective-permute-start(f32[64,256]{1,0:T(8,128)S(1)} %get-tuple-element.73), channel_id=1, source_target_pairs={{0,8},{2,10},{4,12},{6,14},{8,0},{10,2},{12,4},{14,6},{16,24},{18,... | collective-permute-start | bytes 196616 | tf_op jit(solution)/shard_map/ppermute | solution.py:335
  21.7 0.8 %collective-permute-done.2.refs_1_ = f32[64,256]{1,0:T(8,128)S(1)} collective-permute-done((f32[64,256]{1,0:T(8,128)S(1)}, f32[64,256]{1,0:T(8,128)S(1)}, u32[]{:S(2)}, u32[]{:S(2)}) %collective-permute-start.2) | collective-permute-done | bytes 65568 | tf_op jit(solution)/shard_map/ppermute | solution.py:335
  22.5 2.4 %collective-permute-done.3.refs_2_ = f32[64,256]{1,0:T(8,128)S(1)} collective-permute-done((f32[64,256]{1,0:T(8,128)S(1)}, f32[64,256]{1,0:T(8,128)S(1)}, u32[]{:S(2)}, u32[]{:S(2)}) %collective-permute-start.3) | collective-permute-done | bytes 65568 | tf_op jit(solution)/shard_map/ppermute | solution.py:335
  25.0 1.9 %collective-permute-done.4.refs_3_ = f32[64,256]{1,0:T(8,128)S(1)} collective-permute-done((f32[64,256]{1,0:T(8,128)S(1)}, f32[64,256]{1,0:T(8,128)S(1)}, u32[]{:S(2)}, u32[]{:S(2)}) %collective-permute-start.4) | collective-permute-done | bytes 65568 | tf_op jit(solution)/shard_map/ppermute | solution.py:335
  26.9 2.7 %collective-permute-start.5 = (f32[64,256]{1,0:T(8,128)S(1)}, f32[64,256]{1,0:T(8,128)S(1)}, u32[]{:S(2)}, u32[]{:S(2)}) collective-permute-start(f32[64,256]{1,0:T(8,128)S(1)} %sum.2.refs_0_), channel_id=1, source_target_pairs={{0,16},{2,18},{4,20},{6,22},{8,24},{10,26},{12,28},{14,30},{16,0},... | collective-permute-start | bytes 196616 | tf_op jit(solution)/shard_map/ppermute | solution.py:335
  29.6 3.2 %collective-permute-done.5.refs_1_ = f32[64,256]{1,0:T(8,128)S(1)} collective-permute-done((f32[64,256]{1,0:T(8,128)S(1)}, f32[64,256]{1,0:T(8,128)S(1)}, u32[]{:S(2)}, u32[]{:S(2)}) %collective-permute-start.5) | collective-permute-done | bytes 65568 | tf_op jit(solution)/shard_map/ppermute | solution.py:335
  33.3 1.6 %collective-permute-start.8 = (f32[64,256]{1,0:T(8,128)S(1)}, f32[64,256]{1,0:T(8,128)S(1)}, u32[]{:S(2)}, u32[]{:S(2)}) collective-permute-start(f32[64,256]{1,0:T(8,128)S(1)} %sum.3.refs_0_.whole_ref), channel_id=1, source_target_pairs={{0,8},{2,10},{4,12},{6,14},{8,0},{10,2},{12,4},{14,6},{16,24},{18,... | collective-permute-start | bytes 196616 | tf_op jit(solution)/shard_map/ppermute | solution.py:335
  34.9 1.4 %collective-permute-start.7 = (f32[64,256]{1,0:T(8,128)S(1)}, f32[64,256]{1,0:T(8,128)S(1)}, u32[]{:S(2)}, u32[]{:S(2)}) collective-permute-start(f32[64,256]{1,0:T(8,128)S(1)} %sum.3.refs_0_.whole_ref), channel_id=1, source_target_pairs={{0,4},{2,6},{4,0},{6,2},{8,12},{10,14},{12,8},{14,10},{16,20},{18,... | collective-permute-start | bytes 196616 | tf_op jit(solution)/shard_map/ppermute | solution.py:335
  36.3 2.3 %far_tile.1 = (bf16[2048,256]{1,0:T(8,128)(2,1)S(1)}, bf16[2048,256]{1,0:T(8,128)(2,1)S(1)}, f32[8,256]{1,0:T(8,128)S(1)}) custom-call(f32[256,512]{1,0:T(8,128)S(1)} %collective-permute-done.6.refs_0_, f32[1,512]{1,0:T(1,128)S(1)} %get-tuple-element.47.shift_ref.refs_1_, bf16[1024,512]{1,0:T(8,128)(2,1)S(1)} %get-tuple-element.48.ch_ref.refs_2_, ...), custom_call_target="tpu_custom_call" | custom-call | flops 1610612736 | tf_op jit(solution)/shard_map/far_tile/pallas_call | solution.py:39
  39.8 1.0 %collective-permute-done.10.refs_0_ = f32[64,1024]{1,0:T(8,128)S(1)} collective-permute-done((f32[64,1024]{1,0:T(8,128)S(1)}, f32[64,1024]{1,0:T(8,128)S(1)}, u32[]{:S(2)}, u32[]{:S(2)}) %collective-permute-start.10) | collective-permute-done | bytes 262176 | tf_op jit(solution)/shard_map/ppermute | solution.py:335
  41.3 1.6 %collective-permute-start.11 = (f32[72,512]{1,0:T(8,128)S(1)}, f32[72,512]{1,0:T(8,128)S(1)}, u32[]{:S(2)}, u32[]{:S(2)}) collective-permute-start(f32[72,512]{1,0:T(8,128)S(1)} %product_second.1.refs_0_), channel_id=1, source_target_pairs={{0,1},{1,0},{2,3},{3,2},{4,5},{5,4},{6,7},{7,6},{8,9},{9,8},{10,11... | collective-permute-start | bytes 442376 | tf_op jit(solution)/shard_map/ppermute | solution.py:345
  42.8 4.4 %collective-permute-done.11.refs_1_ = f32[72,512]{1,0:T(8,128)S(1)} collective-permute-done((f32[72,512]{1,0:T(8,128)S(1)}, f32[72,512]{1,0:T(8,128)S(1)}, u32[]{:S(2)}, u32[]{:S(2)}) %collective-permute-start.11) | collective-permute-done | bytes 147488 | tf_op jit(solution)/shard_map/ppermute | solution.py:345
  48.2 0.9 %collective-permute-done.12.got_ref = f32[72,512]{1,0:T(8,128)S(1)} collective-permute-done((f32[72,512]{1,0:T(8,128)S(1)}, f32[72,512]{1,0:T(8,128)S(1)}, u32[]{:S(2)}, u32[]{:S(2)}) %collective-permute-start.12) | collective-permute-done | bytes 147488 | tf_op jit(solution)/shard_map/ppermute | solution.py:335
  49.2 1.4 %collective-permute-start.13 = (f32[72,128]{1,0:T(8,128)S(1)}, f32[72,128]{1,0:T(8,128)S(1)}, u32[]{:S(2)}, u32[]{:S(2)}) collective-permute-start(f32[72,128]{1,0:T(8,128)S(1)} %get-tuple-element.89), channel_id=1, source_target_pairs={{0,4},{2,6},{4,0},{6,2},{8,12},{10,14},{12,8},{14,10},{16,20},{18,... | collective-permute-start | bytes 110600 | tf_op jit(solution)/shard_map/ppermute | solution.py:335
  50.6 2.1 %collective-permute-start.15 = (f32[72,128]{1,0:T(8,128)S(1)}, f32[72,128]{1,0:T(8,128)S(1)}, u32[]{:S(2)}, u32[]{:S(2)}) collective-permute-start(f32[72,128]{1,0:T(8,128)S(1)} %get-tuple-element.91), channel_id=1, source_target_pairs={{0,12},{2,14},{4,8},{6,10},{8,4},{10,6},{12,0},{14,2},{16,28},{18,... | collective-permute-start | bytes 110600 | tf_op jit(solution)/shard_map/ppermute | solution.py:335
  53.2 1.4 %collective-permute-done.14.refs_2_ = f32[72,128]{1,0:T(8,128)S(1)} collective-permute-done((f32[72,128]{1,0:T(8,128)S(1)}, f32[72,128]{1,0:T(8,128)S(1)}, u32[]{:S(2)}, u32[]{:S(2)}) %collective-permute-start.14) | collective-permute-done | bytes 36896 | tf_op jit(solution)/shard_map/ppermute | solution.py:335
  54.6 0.9 %collective-permute-done.15.refs_3_ = f32[72,128]{1,0:T(8,128)S(1)} collective-permute-done((f32[72,128]{1,0:T(8,128)S(1)}, f32[72,128]{1,0:T(8,128)S(1)}, u32[]{:S(2)}, u32[]{:S(2)}) %collective-permute-start.15) | collective-permute-done | bytes 36896 | tf_op jit(solution)/shard_map/ppermute | solution.py:335
  (31 shorter events, 6.9 us)
Async XLA Ops:
  0.6 2.1 %copy-start.1 = (f32[512,512]{1,0:T(8,128)S(1)}, f32[512,512]{1,0:T(8,128)}, u32[]{:S(2)}) copy-start(f32[512,512]{1,0:T(8,128)} %x_ref.1) | copy-start | bytes 3145732
  2.7 2.4 %copy-start = (f32[2048,64]{0,1:T(8,128)S(1)}, f32[2048,64]{0,1:T(8,128)}, u32[]{:S(2)}) copy-start(f32[2048,64]{0,1:T(8,128)} %param.7) | copy-start | bytes 1572868
  8.3 7.3 %copy-start.2 = (f32[512,64]{0,1:T(8,128)S(1)}, f32[512,64]{0,1:T(8,128)}, u32[]{:S(2)}) copy-start(f32[512,64]{0,1:T(8,128)} %param.5) | copy-start | bytes 393220
  8.3 7.3 %collective-permute-start = (f32[64,512]{1,0:T(8,128)S(1)}, f32[64,512]{1,0:T(8,128)S(1)}, u32[]{:S(2)}, u32[]{:S(2)}) collective-permute-start(f32[64,512]{1,0:T(8,128)S(1)} %get-tuple-element.58.refs_0_), channel_id=1, source_target_pairs={{0,1},{1,0},{2,3},{3,2},{4,5},{5,4},{6,7},{7,6},{8,9},{9,8},{10,11... | collective-permute-start | bytes 393224 | tf_op jit(solution)/shard_map/ppermute | solution.py:345
  11.3 25.0 %collective-permute-start.6 = (f32[256,512]{1,0:T(8,128)S(1)}, f32[256,512]{1,0:T(8,128)S(1)}, u32[]{:S(2)}, u32[]{:S(2)}) collective-permute-start(f32[256,512]{1,0:T(8,128)S(1)} %get-tuple-element.60.refs_0_), channel_id=1, source_target_pairs={{0,1},{1,0},{2,3},{3,2},{4,5},{5,4},{6,7},{7,6},{8,9},{9,8},{10,11... | collective-permute-start | bytes 1572872 | tf_op jit(solution)/shard_map/ppermute | solution.py:345
  16.4 1.6 %collective-permute-start.1 = (f32[64,1024]{1,0:T(8,128)S(1)}, f32[64,1024]{1,0:T(8,128)S(1)}, u32[]{:S(2)}, u32[]{:S(2)}) collective-permute-start(f32[64,1024]{1,0:T(8,128)S(1)} %get-tuple-element.70), channel_id=1, source_target_pairs={{0,2},{2,0},{4,6},{6,4},{8,10},{10,8},{12,14},{14,12},{16,18},{18,... | collective-permute-start | bytes 786440 | tf_op jit(solution)/shard_map/ppermute | solution.py:335
  18.0 4.5 %collective-permute-start.2 = (f32[64,256]{1,0:T(8,128)S(1)}, f32[64,256]{1,0:T(8,128)S(1)}, u32[]{:S(2)}, u32[]{:S(2)}) collective-permute-start(f32[64,256]{1,0:T(8,128)S(1)} %get-tuple-element.72), channel_id=1, source_target_pairs={{0,4},{2,6},{4,0},{6,2},{8,12},{10,14},{12,8},{14,10},{16,20},{18,... | collective-permute-start | bytes 196616 | tf_op jit(solution)/shard_map/ppermute | solution.py:335
  20.2 4.8 %collective-permute-start.3 = (f32[64,256]{1,0:T(8,128)S(1)}, f32[64,256]{1,0:T(8,128)S(1)}, u32[]{:S(2)}, u32[]{:S(2)}) collective-permute-start(f32[64,256]{1,0:T(8,128)S(1)} %get-tuple-element.73), channel_id=1, source_target_pairs={{0,8},{2,10},{4,12},{6,14},{8,0},{10,2},{12,4},{14,6},{16,24},{18,... | collective-permute-start | bytes 196616 | tf_op jit(solution)/shard_map/ppermute | solution.py:335
  21.7 5.2 %collective-permute-start.4 = (f32[64,256]{1,0:T(8,128)S(1)}, f32[64,256]{1,0:T(8,128)S(1)}, u32[]{:S(2)}, u32[]{:S(2)}) collective-permute-start(f32[64,256]{1,0:T(8,128)S(1)} %get-tuple-element.74), channel_id=1, source_target_pairs={{0,12},{2,14},{4,8},{6,10},{8,4},{10,6},{12,0},{14,2},{16,28},{18,... | collective-permute-start | bytes 196616 | tf_op jit(solution)/shard_map/ppermute | solution.py:335
  26.9 5.8 %collective-permute-start.5 = (f32[64,256]{1,0:T(8,128)S(1)}, f32[64,256]{1,0:T(8,128)S(1)}, u32[]{:S(2)}, u32[]{:S(2)}) collective-permute-start(f32[64,256]{1,0:T(8,128)S(1)} %sum.2.refs_0_), channel_id=1, source_target_pairs={{0,16},{2,18},{4,20},{6,22},{8,24},{10,26},{12,28},{14,30},{16,0},... | collective-permute-start | bytes 196616 | tf_op jit(solution)/shard_map/ppermute | solution.py:335
  32.7 5.8 %collective-permute-start.9 = (f32[64,256]{1,0:T(8,128)S(1)}, f32[64,256]{1,0:T(8,128)S(1)}, u32[]{:S(2)}, u32[]{:S(2)}) collective-permute-start(f32[64,256]{1,0:T(8,128)S(1)} %sum.3.refs_0_.whole_ref), channel_id=1, source_target_pairs={{0,12},{2,14},{4,8},{6,10},{8,4},{10,6},{12,0},{14,2},{16,28},{18,... | collective-permute-start | bytes 196616 | tf_op jit(solution)/shard_map/ppermute | solution.py:335
  33.3 5.3 %collective-permute-start.8 = (f32[64,256]{1,0:T(8,128)S(1)}, f32[64,256]{1,0:T(8,128)S(1)}, u32[]{:S(2)}, u32[]{:S(2)}) collective-permute-start(f32[64,256]{1,0:T(8,128)S(1)} %sum.3.refs_0_.whole_ref), channel_id=1, source_target_pairs={{0,8},{2,10},{4,12},{6,14},{8,0},{10,2},{12,4},{14,6},{16,24},{18,... | collective-permute-start | bytes 196616 | tf_op jit(solution)/shard_map/ppermute | solution.py:335
  34.9 4.3 %collective-permute-start.7 = (f32[64,256]{1,0:T(8,128)S(1)}, f32[64,256]{1,0:T(8,128)S(1)}, u32[]{:S(2)}, u32[]{:S(2)}) collective-permute-start(f32[64,256]{1,0:T(8,128)S(1)} %sum.3.refs_0_.whole_ref), channel_id=1, source_target_pairs={{0,4},{2,6},{4,0},{6,2},{8,12},{10,14},{12,8},{14,10},{16,20},{18,... | collective-permute-start | bytes 196616 | tf_op jit(solution)/shard_map/ppermute | solution.py:335
  39.2 1.6 %collective-permute-start.10 = (f32[64,1024]{1,0:T(8,128)S(1)}, f32[64,1024]{1,0:T(8,128)S(1)}, u32[]{:S(2)}, u32[]{:S(2)}) collective-permute-start(f32[64,1024]{1,0:T(8,128)S(1)} %pack.1), channel_id=1, source_target_pairs={{0,2},{2,0},{4,6},{6,4},{8,10},{10,8},{12,14},{14,12},{16,18},{18,... | collective-permute-start | bytes 786440 | tf_op jit(solution)/shard_map/ppermute | solution.py:335
  41.3 6.0 %collective-permute-start.11 = (f32[72,512]{1,0:T(8,128)S(1)}, f32[72,512]{1,0:T(8,128)S(1)}, u32[]{:S(2)}, u32[]{:S(2)}) collective-permute-start(f32[72,512]{1,0:T(8,128)S(1)} %product_second.1.refs_0_), channel_id=1, source_target_pairs={{0,1},{1,0},{2,3},{3,2},{4,5},{5,4},{6,7},{7,6},{8,9},{9,8},{10,11... | collective-permute-start | bytes 442376 | tf_op jit(solution)/shard_map/ppermute | solution.py:345
  47.7 1.4 %collective-permute-start.12 = (f32[72,512]{1,0:T(8,128)S(1)}, f32[72,512]{1,0:T(8,128)S(1)}, u32[]{:S(2)}, u32[]{:S(2)}) collective-permute-start(f32[72,512]{1,0:T(8,128)S(1)} %get-tuple-element.86), channel_id=1, source_target_pairs={{0,2},{2,0},{4,6},{6,4},{8,10},{10,8},{12,14},{14,12},{16,18},{18,... | collective-permute-start | bytes 442376 | tf_op jit(solution)/shard_map/ppermute | solution.py:335
  49.2 4.0 %collective-permute-start.13 = (f32[72,128]{1,0:T(8,128)S(1)}, f32[72,128]{1,0:T(8,128)S(1)}, u32[]{:S(2)}, u32[]{:S(2)}) collective-permute-start(f32[72,128]{1,0:T(8,128)S(1)} %get-tuple-element.89), channel_id=1, source_target_pairs={{0,4},{2,6},{4,0},{6,2},{8,12},{10,14},{12,8},{14,10},{16,20},{18,... | collective-permute-start | bytes 110600 | tf_op jit(solution)/shard_map/ppermute | solution.py:335
  50.6 4.0 %collective-permute-start.14 = (f32[72,128]{1,0:T(8,128)S(1)}, f32[72,128]{1,0:T(8,128)S(1)}, u32[]{:S(2)}, u32[]{:S(2)}) collective-permute-start(f32[72,128]{1,0:T(8,128)S(1)} %get-tuple-element.90), channel_id=1, source_target_pairs={{0,8},{2,10},{4,12},{6,14},{8,0},{10,2},{12,4},{14,6},{16,24},{18,... | collective-permute-start | bytes 110600 | tf_op jit(solution)/shard_map/ppermute | solution.py:335
  50.6 4.9 %collective-permute-start.15 = (f32[72,128]{1,0:T(8,128)S(1)}, f32[72,128]{1,0:T(8,128)S(1)}, u32[]{:S(2)}, u32[]{:S(2)}) collective-permute-start(f32[72,128]{1,0:T(8,128)S(1)} %get-tuple-element.91), channel_id=1, source_target_pairs={{0,12},{2,14},{4,8},{6,10},{8,4},{10,6},{12,0},{14,2},{16,28},{18,... | collective-permute-start | bytes 110600 | tf_op jit(solution)/shard_map/ppermute | solution.py:335

commit v7 on v6

--- a/solution.py
+++ b/solution.py
@@ -228,16 +228,19 @@
 
 
 def image_kernel(mids, share, shards, *refs):
-    kernels = refs[shards : shards + 4]
-    out_ref, left_ref, own_ref, max_ref, image_ref = refs[shards + 4 :]
+    sums, kernels = refs[shards : 2 * shards], refs[2 * shards : 2 * shards + 4]
+    out_ref, left_ref, own_ref, max_ref, image_ref = refs[2 * shards + 4 :]
     outs, size = own_ref.shape[0], 2 * share
     total = refs[0][...]
     for ref in refs[1:shards]:
         total = total + ref[...]
-    largest = jnp.max(total[outs : outs + 1], keepdims=True)
+    row_sums = sums[0][...]
+    for ref in sums[1:]:
+        row_sums = row_sums + ref[...]
+    largest = jnp.max(row_sums[:1], keepdims=True)
     max_ref[...] = jnp.broadcast_to(largest, max_ref.shape)
     out_ref[outs:, :] = jnp.broadcast_to(largest, (8, out_ref.shape[1]))
-    image_ref[...] = total[:outs]
+    image_ref[...] = total
     for j in range(shards):
         part = image_ref[:, pl.ds(shard_at(j, shards, size), size)]
         left_ref[:, j * size : (j + 1) * size] = jnp.concatenate(split(part), axis=0)
@@ -278,20 +281,20 @@
 
 
 def second_kernel(mids, share, shards, *refs):
-    own_ref, far_ref, osum, fsum, out_ref = refs[-5:]
-    outs, size = own_ref.shape[0], 2 * share
-    own, far = product(mids, share, 1, refs[:-9], refs[-9:-5])
+    own_ref, far_ref, out_ref = refs[-3:]
+    size = 2 * share
+    own, far = product(mids, share, 1, refs[:-7], refs[-7:-3])
     own, far = own + own_ref[...], far + far_ref[...]
     for j in range(shards):
-        source, sums, at = (own, osum, 0) if j == 0 else (far, fsum, size * (j - 1))
-        where = pl.ds(shard_at(j, shards, size), size)
-        out_ref[:outs, where] = source[:, at : at + size]
-        row_sums = jnp.sum(sums[:, at : at + size], axis=0, keepdims=True)
-        out_ref[outs:, where] = jnp.broadcast_to(row_sums, (8, size))
-
-
-def pack_kernel(*refs):
-    refs[-1][...] = jnp.concatenate([ref[...] for ref in refs[:-1]], axis=1)
+        source, at = (own, 0) if j == 0 else (far, size * (j - 1))
+        out_ref[:, pl.ds(shard_at(j, shards, size), size)] = source[:, at : at + size]
+
+
+def row_sums_kernel(shards, size, own_ref, far_ref, out_ref):
+    for j in range(shards):
+        source, at = (own_ref, 0) if j == 0 else (far_ref, size * (j - 1))
+        sums = jnp.sum(source[:, at : at + size], axis=0, keepdims=True)
+        out_ref[:, pl.ds(shard_at(j, shards, size), size)] = jnp.broadcast_to(sums, (8, size))
 
 
 def join_kernel(mids, keep_ref, got_ref, *refs):
@@ -450,23 +453,24 @@
     far_high, far_low, far_sums = centre_tile([after(f, whole) for f in far], "far_tile")
     kernels = [own_high, own_low, far_high, far_low]
     wide = 2 * share * (shards - 1)
-    packed = call(
-        pack_kernel, "pack", [after(whole, far_sums)] + gathered[1:], [like(outs, 2 * share * mids)]
-    )[0]
-    swapped = [send_xor(packed, 1)]
+    (sums,) = call(
+        functools.partial(row_sums_kernel, shards, 2 * share), "row_sums",
+        [own_sums, far_sums], [like(8, 2 * share * shards)],
+    )
+    sums = [sums] + [send_far(sums, 0, shift) for shift in range(1, shards)]
+    swapped = [send_xor(whole, 1)] + [send_xor(after(piece, far_sums), 1) for piece in gathered[1:]]
     firsts = call(
         functools.partial(first_kernel, mids, share), "product_first",
         gathered + kernels, [like(outs, 2 * share), like(outs, wide)],
     )
     (image,) = call(
         functools.partial(second_kernel, mids, share, shards), "product_second",
-        swapped + kernels + list(firsts) + [own_sums, far_sums],
-        [like(outs + 8, 2 * share * shards)],
+        swapped + kernels + list(firsts), [like(outs, 2 * share * shards)],
     )
     images = [image] + [send_far(image, 0, shift) for shift in range(1, shards)]
     give, left, own, largest = call(
         functools.partial(image_kernel, mids, share, shards), "image_give",
-        images + kernels,
+        images + sums + kernels,
         [
             like(outs + 8, mids * share),
             like(2 * outs, 2 * share * shards, dtype=bf16),

time: 56.3 us -> 56.3 us (level)
  starting transfers between devices: 18.3 us -> 19.9 us
  waiting for transfers between devices: 20.7 us -> 19.2 us
    ppermute x13 -> x16, waiting for transfers between devices: 14.4 us -> 13.2 us  [send_xor(): return lax.ppermute(array, 'dp', [(i, i ^ mask) for i in range(count)])]
    ppermute x13 -> x16, starting transfers between devices: 13.7 us -> 14.7 us  [send_xor(): return lax.ppermute(array, 'dp', [(i, i ^ mask) for i in range(count)])]
    ppermute x3 -> x4, starting transfers between devices: 4.64 us -> 5.24 us  [send_far(): return lax.ppermute(array, ('dp', 'centre'), pairs)]
    ppermute x3 -> x4, waiting for transfers between devices: 6.37 us -> 5.97 us  [send_far(): return lax.ppermute(array, ('dp', 'centre'), pairs)]
  transfers between devices with their start and end apart: 16 -> 20, of which waited for: 13 -> 13; matrix products, arithmetic and copies ran while one was open for 0% -> 0% of each run, Pallas kernels for 12% -> 12%
where the time goes in v7:
time: 56.3 us; the launch traced here: 56.2 us
  starting transfers between devices  19.9 us (35%)
  waiting for transfers between devices  19.2 us (34%)
  Pallas kernels  16.3 us (29%)
  between operations  0.81 us (1%)
    pallas_call x17, Pallas kernels, call(): pl.pallas_call(kernel, name=name, in_specs=[pl.BlockSpec(memory_space=plt...  16.3 us
    ppermute x16, starting transfers between devices, send_xor(): return lax.ppermute(array, 'dp', [(i, i ^ mask) for i in range(count)])  14.7 us
    ppermute x16, waiting for transfers between devices, send_xor(): return lax.ppermute(array, 'dp', [(i, i ^ mask) for i in range(count)])  13.2 us
    ppermute x4, waiting for transfers between devices, send_far(): return lax.ppermute(array, ('dp', 'centre'), pairs)  5.97 us
    ppermute x4, starting transfers between devices, send_far(): return lax.ppermute(array, ('dp', 'centre'), pairs)  5.24 us
  transfers between devices with their start and end apart: 20, of which 13 were waited for; matrix products, arithmetic and copies ran while one was open for 0% of the time, Pallas kernels for 12%

profile of v7, /device:TPU:0, one launch (start us, length us, event | category | flops | bytes accessed | tf_op | source)
XLA Modules:
  0.0 56.2 jit_solution(4383669785333299181)
XLA Ops:
  0.6 2.1 %load.1 = (bf16[1024,512]{1,0:T(8,128)(2,1)S(1)}, bf16[1024,512]{1,0:T(8,128)(2,1)S(1)}, f32[1024,1]{1,0:T(8,128)S(1)}, f32[128,512]{1,0:T(8,128)S(1)}, f32[1,512]{1,0:T(1,128)S(1)}) custom-call(f32[2048,512]{1,0:T(8,128)} %c_hbm.3), custom_call_target="tpu_custom_call" | custom-call | tf_op jit(solution)/shard_map/load/pallas_call | solution.py:39
  2.7 2.4 %data_first.1 = (bf16[1024,512]{1,0:T(8,128)(2,1)S(1)}, bf16[1024,512]{1,0:T(8,128)(2,1)S(1)}, bf16[512,512]{1,0:T(8,128)(2,1)S(1)}, bf16[512,512]{1,0:T(8,128)(...) custom-call(f32[512,512]{1,0:T(8,128)S(1)} %copy-done.1, f32[1,512]{1,0:T(1,128)S(1)} %get-tuple-element.49.shift_ref.refs_1_, ...), custom_call_target="tpu_custom_call" | custom-call | tf_op jit(solution)/shard_map/data_first/pallas_call | solution.py:39
  5.1 3.2 %data_second.1 = (bf16[1024,512]{1,0:T(8,128)(2,1)S(1)}, bf16[1024,512]{1,0:T(8,128)(2,1)S(1)}, f32[1024,1]{1,0:T(8,128)S(1)}, bf16[1024,512]{1,0:T(8,128)(2,1)S...) custom-call(f32[64,2048]{1,0:T(8,128)S(1)} %bitcast.4, ...), custom_call_target="tpu_custom_call" | custom-call | tf_op jit(solution)/shard_map/data_second/pallas_call | solution.py:39
  8.3 3.0 %collective-permute-start = (f32[64,512]{1,0:T(8,128)S(1)}, f32[64,512]{1,0:T(8,128)S(1)}, u32[]{:S(2)}, u32[]{:S(2)}) collective-permute-start(f32[64,512]{1,0:T(8,128)S(1)} %get-tuple-element.60.refs_0_), channel_id=1, source_target_pairs={{0,1},{1,0},{2,3},{3,2},{4,5},{5,4},{6,7},{7,6},{8,9},{9,8},{10,11... | collective-permute-start | bytes 393224 | tf_op jit(solution)/shard_map/ppermute | solution.py:348
  11.4 2.3 %own_tile.1 = (bf16[2048,256]{1,0:T(8,128)(2,1)S(1)}, bf16[2048,256]{1,0:T(8,128)(2,1)S(1)}, f32[8,256]{1,0:T(8,128)S(1)}) custom-call(f32[256,512]{1,0:T(8,128)S(1)} %get-tuple-element.62.refs_0_, f32[1,512]{1,0:T(1,128)S(1)} %get-tuple-element.49.shift_ref.refs_1_, bf16[1024,512]{1,0:T(8,128)(2,1)S(1)} %get-tuple-element.50.ch_ref.refs_2_, ...), custom_call_target="tpu_custom_call" | custom-call | flops 1610612736 | tf_op jit(solution)/shard_map/own_tile/pallas_call | solution.py:39
  13.7 2.0 %collective-permute-done.refs_1_ = f32[64,512]{1,0:T(8,128)S(1)} collective-permute-done((f32[64,512]{1,0:T(8,128)S(1)}, f32[64,512]{1,0:T(8,128)S(1)}, u32[]{:S(2)}, u32[]{:S(2)}) %collective-permute-start) | collective-permute-done | bytes 131104 | tf_op jit(solution)/shard_map/ppermute | solution.py:348
  17.2 0.8 %collective-permute-done.1.got_ref = f32[64,1024]{1,0:T(8,128)S(1)} collective-permute-done((f32[64,1024]{1,0:T(8,128)S(1)}, f32[64,1024]{1,0:T(8,128)S(1)}, u32[]{:S(2)}, u32[]{:S(2)}) %collective-permute-start.1) | collective-permute-done | bytes 262176 | tf_op jit(solution)/shard_map/ppermute | solution.py:338
  18.0 2.2 %collective-permute-start.2 = (f32[64,256]{1,0:T(8,128)S(1)}, f32[64,256]{1,0:T(8,128)S(1)}, u32[]{:S(2)}, u32[]{:S(2)}) collective-permute-start(f32[64,256]{1,0:T(8,128)S(1)} %get-tuple-element.74), channel_id=1, source_target_pairs={{0,4},{2,6},{4,0},{6,2},{8,12},{10,14},{12,8},{14,10},{16,20},{18,... | collective-permute-start | bytes 196616 | tf_op jit(solution)/shard_map/ppermute | solution.py:338
  20.2 1.6 %collective-permute-start.3 = (f32[64,256]{1,0:T(8,128)S(1)}, f32[64,256]{1,0:T(8,128)S(1)}, u32[]{:S(2)}, u32[]{:S(2)}) collective-permute-start(f32[64,256]{1,0:T(8,128)S(1)} %get-tuple-element.75), channel_id=1, source_target_pairs={{0,8},{2,10},{4,12},{6,14},{8,0},{10,2},{12,4},{14,6},{16,24},{18,... | collective-permute-start | bytes 196616 | tf_op jit(solution)/shard_map/ppermute | solution.py:338
  21.7 0.8 %collective-permute-done.2.refs_1_ = f32[64,256]{1,0:T(8,128)S(1)} collective-permute-done((f32[64,256]{1,0:T(8,128)S(1)}, f32[64,256]{1,0:T(8,128)S(1)}, u32[]{:S(2)}, u32[]{:S(2)}) %collective-permute-start.2) | collective-permute-done | bytes 65568 | tf_op jit(solution)/shard_map/ppermute | solution.py:338
  22.5 2.4 %collective-permute-done.3.refs_2_ = f32[64,256]{1,0:T(8,128)S(1)} collective-permute-done((f32[64,256]{1,0:T(8,128)S(1)}, f32[64,256]{1,0:T(8,128)S(1)}, u32[]{:S(2)}, u32[]{:S(2)}) %collective-permute-start.3) | collective-permute-done | bytes 65568 | tf_op jit(solution)/shard_map/ppermute | solution.py:338
  25.0 1.9 %collective-permute-done.4.refs_3_ = f32[64,256]{1,0:T(8,128)S(1)} collective-permute-done((f32[64,256]{1,0:T(8,128)S(1)}, f32[64,256]{1,0:T(8,128)S(1)}, u32[]{:S(2)}, u32[]{:S(2)}) %collective-permute-start.4) | collective-permute-done | bytes 65568 | tf_op jit(solution)/shard_map/ppermute | solution.py:338
  26.9 2.7 %collective-permute-start.5 = (f32[64,256]{1,0:T(8,128)S(1)}, f32[64,256]{1,0:T(8,128)S(1)}, u32[]{:S(2)}, u32[]{:S(2)}) collective-permute-start(f32[64,256]{1,0:T(8,128)S(1)} %sum.2.refs_0_), channel_id=1, source_target_pairs={{0,16},{2,18},{4,20},{6,22},{8,24},{10,26},{12,28},{14,30},{16,0},... | collective-permute-start | bytes 196616 | tf_op jit(solution)/shard_map/ppermute | solution.py:338
  29.6 3.2 %collective-permute-done.5.refs_1_ = f32[64,256]{1,0:T(8,128)S(1)} collective-permute-done((f32[64,256]{1,0:T(8,128)S(1)}, f32[64,256]{1,0:T(8,128)S(1)}, u32[]{:S(2)}, u32[]{:S(2)}) %collective-permute-start.5) | collective-permute-done | bytes 65568 | tf_op jit(solution)/shard_map/ppermute | solution.py:338
  33.3 1.6 %collective-permute-start.10 = (f32[64,256]{1,0:T(8,128)S(1)}, f32[64,256]{1,0:T(8,128)S(1)}, u32[]{:S(2)}, u32[]{:S(2)}) collective-permute-start(f32[64,256]{1,0:T(8,128)S(1)} %sum.3.refs_0_.whole_ref), channel_id=1, source_target_pairs={{0,8},{2,10},{4,12},{6,14},{8,0},{10,2},{12,4},{14,6},{16,24},{18,... | collective-permute-start | bytes 196616 | tf_op jit(solution)/shard_map/ppermute | solution.py:338
  34.9 1.4 %collective-permute-start.7 = (f32[64,256]{1,0:T(8,128)S(1)}, f32[64,256]{1,0:T(8,128)S(1)}, u32[]{:S(2)}, u32[]{:S(2)}) collective-permute-start(f32[64,256]{1,0:T(8,128)S(1)} %sum.3.refs_0_.whole_ref), channel_id=1, source_target_pairs={{0,4},{2,6},{4,0},{6,2},{8,12},{10,14},{12,8},{14,10},{16,20},{18,... | collective-permute-start | bytes 196616 | tf_op jit(solution)/shard_map/ppermute | solution.py:338
  36.3 2.3 %far_tile.1 = (bf16[2048,256]{1,0:T(8,128)(2,1)S(1)}, bf16[2048,256]{1,0:T(8,128)(2,1)S(1)}, f32[8,256]{1,0:T(8,128)S(1)}) custom-call(f32[256,512]{1,0:T(8,128)S(1)} %collective-permute-done.8.refs_0_, f32[1,512]{1,0:T(1,128)S(1)} %get-tuple-element.49.shift_ref.refs_1_, bf16[1024,512]{1,0:T(8,128)(2,1)S(1)} %get-tuple-element.50.ch_ref.refs_2_, ...), custom_call_target="tpu_custom_call" | custom-call | flops 1610612736 | tf_op jit(solution)/shard_map/far_tile/pallas_call | solution.py:39
  41.1 1.6 %collective-permute-start.14 = (f32[64,512]{1,0:T(8,128)S(1)}, f32[64,512]{1,0:T(8,128)S(1)}, u32[]{:S(2)}, u32[]{:S(2)}) collective-permute-start(f32[64,512]{1,0:T(8,128)S(1)} %product_second.1.refs_0_), channel_id=1, source_target_pairs={{0,1},{1,0},{2,3},{3,2},{4,5},{5,4},{6,7},{7,6},{8,9},{9,8},{10,11... | collective-permute-start | bytes 393224 | tf_op jit(solution)/shard_map/ppermute | solution.py:348
  43.2 4.0 %collective-permute-done.15.refs_3_ = f32[8,512]{1,0:T(8,128)S(1)} collective-permute-done((f32[8,512]{1,0:T(8,128)S(1)}, f32[8,512]{1,0:T(8,128)S(1)}, u32[]{:S(2)}, u32[]{:S(2)}) %collective-permute-start.15) | collective-permute-done | bytes 16416 | tf_op jit(solution)/shard_map/ppermute | solution.py:348
  48.3 0.9 %collective-permute-done.16.got_ref = f32[72,512]{1,0:T(8,128)S(1)} collective-permute-done((f32[72,512]{1,0:T(8,128)S(1)}, f32[72,512]{1,0:T(8,128)S(1)}, u32[]{:S(2)}, u32[]{:S(2)}) %collective-permute-start.16) | collective-permute-done | bytes 147488 | tf_op jit(solution)/shard_map/ppermute | solution.py:338
  49.2 1.1 %collective-permute-start.17 = (f32[72,128]{1,0:T(8,128)S(1)}, f32[72,128]{1,0:T(8,128)S(1)}, u32[]{:S(2)}, u32[]{:S(2)}) collective-permute-start(f32[72,128]{1,0:T(8,128)S(1)} %get-tuple-element.93), channel_id=1, source_target_pairs={{0,4},{2,6},{4,0},{6,2},{8,12},{10,14},{12,8},{14,10},{16,20},{18,... | collective-permute-start | bytes 110600 | tf_op jit(solution)/shard_map/ppermute | solution.py:338
  50.6 2.1 %collective-permute-start.19 = (f32[72,128]{1,0:T(8,128)S(1)}, f32[72,128]{1,0:T(8,128)S(1)}, u32[]{:S(2)}, u32[]{:S(2)}) collective-permute-start(f32[72,128]{1,0:T(8,128)S(1)} %get-tuple-element.95), channel_id=1, source_target_pairs={{0,12},{2,14},{4,8},{6,10},{8,4},{10,6},{12,0},{14,2},{16,28},{18,... | collective-permute-start | bytes 110600 | tf_op jit(solution)/shard_map/ppermute | solution.py:338
  53.2 1.0 %collective-permute-done.18.refs_2_ = f32[72,128]{1,0:T(8,128)S(1)} collective-permute-done((f32[72,128]{1,0:T(8,128)S(1)}, f32[72,128]{1,0:T(8,128)S(1)}, u32[]{:S(2)}, u32[]{:S(2)}) %collective-permute-start.18) | collective-permute-done | bytes 36896 | tf_op jit(solution)/shard_map/ppermute | solution.py:338
  54.2 1.3 %collective-permute-done.19.refs_3_ = f32[72,128]{1,0:T(8,128)S(1)} collective-permute-done((f32[72,128]{1,0:T(8,128)S(1)}, f32[72,128]{1,0:T(8,128)S(1)}, u32[]{:S(2)}, u32[]{:S(2)}) %collective-permute-start.19) | collective-permute-done | bytes 36896 | tf_op jit(solution)/shard_map/ppermute | solution.py:338
  (39 shorter events, 7.9 us)
Async XLA Ops:
  0.6 2.1 %copy-start.1 = (f32[512,512]{1,0:T(8,128)S(1)}, f32[512,512]{1,0:T(8,128)}, u32[]{:S(2)}) copy-start(f32[512,512]{1,0:T(8,128)} %x_ref.1) | copy-start | bytes 3145732
  2.7 2.4 %copy-start = (f32[2048,64]{0,1:T(8,128)S(1)}, f32[2048,64]{0,1:T(8,128)}, u32[]{:S(2)}) copy-start(f32[2048,64]{0,1:T(8,128)} %param.7) | copy-start | bytes 1572868
  8.3 7.3 %copy-start.2 = (f32[512,64]{0,1:T(8,128)S(1)}, f32[512,64]{0,1:T(8,128)}, u32[]{:S(2)}) copy-start(f32[512,64]{0,1:T(8,128)} %param.5) | copy-start | bytes 393220
  8.3 7.3 %collective-permute-start = (f32[64,512]{1,0:T(8,128)S(1)}, f32[64,512]{1,0:T(8,128)S(1)}, u32[]{:S(2)}, u32[]{:S(2)}) collective-permute-start(f32[64,512]{1,0:T(8,128)S(1)} %get-tuple-element.60.refs_0_), channel_id=1, source_target_pairs={{0,1},{1,0},{2,3},{3,2},{4,5},{5,4},{6,7},{7,6},{8,9},{9,8},{10,11... | collective-permute-start | bytes 393224 | tf_op jit(solution)/shard_map/ppermute | solution.py:348
  11.3 25.0 %collective-permute-start.8 = (f32[256,512]{1,0:T(8,128)S(1)}, f32[256,512]{1,0:T(8,128)S(1)}, u32[]{:S(2)}, u32[]{:S(2)}) collective-permute-start(f32[256,512]{1,0:T(8,128)S(1)} %get-tuple-element.62.refs_0_), channel_id=1, source_target_pairs={{0,1},{1,0},{2,3},{3,2},{4,5},{5,4},{6,7},{7,6},{8,9},{9,8},{10,11... | collective-permute-start | bytes 1572872 | tf_op jit(solution)/shard_map/ppermute | solution.py:348
  16.4 1.6 %collective-permute-start.1 = (f32[64,1024]{1,0:T(8,128)S(1)}, f32[64,1024]{1,0:T(8,128)S(1)}, u32[]{:S(2)}, u32[]{:S(2)}) collective-permute-start(f32[64,1024]{1,0:T(8,128)S(1)} %get-tuple-element.72), channel_id=1, source_target_pairs={{0,2},{2,0},{4,6},{6,4},{8,10},{10,8},{12,14},{14,12},{16,18},{18,... | collective-permute-start | bytes 786440 | tf_op jit(solution)/shard_map/ppermute | solution.py:338
  18.0 4.5 %collective-permute-start.2 = (f32[64,256]{1,0:T(8,128)S(1)}, f32[64,256]{1,0:T(8,128)S(1)}, u32[]{:S(2)}, u32[]{:S(2)}) collective-permute-start(f32[64,256]{1,0:T(8,128)S(1)} %get-tuple-element.74), channel_id=1, source_target_pairs={{0,4},{2,6},{4,0},{6,2},{8,12},{10,14},{12,8},{14,10},{16,20},{18,... | collective-permute-start | bytes 196616 | tf_op jit(solution)/shard_map/ppermute | solution.py:338
  20.2 4.8 %collective-permute-start.3 = (f32[64,256]{1,0:T(8,128)S(1)}, f32[64,256]{1,0:T(8,128)S(1)}, u32[]{:S(2)}, u32[]{:S(2)}) collective-permute-start(f32[64,256]{1,0:T(8,128)S(1)} %get-tuple-element.75), channel_id=1, source_target_pairs={{0,8},{2,10},{4,12},{6,14},{8,0},{10,2},{12,4},{14,6},{16,24},{18,... | collective-permute-start | bytes 196616 | tf_op jit(solution)/shard_map/ppermute | solution.py:338
  21.7 5.2 %collective-permute-start.4 = (f32[64,256]{1,0:T(8,128)S(1)}, f32[64,256]{1,0:T(8,128)S(1)}, u32[]{:S(2)}, u32[]{:S(2)}) collective-permute-start(f32[64,256]{1,0:T(8,128)S(1)} %get-tuple-element.76), channel_id=1, source_target_pairs={{0,12},{2,14},{4,8},{6,10},{8,4},{10,6},{12,0},{14,2},{16,28},{18,... | collective-permute-start | bytes 196616 | tf_op jit(solution)/shard_map/ppermute | solution.py:338
  26.9 5.8 %collective-permute-start.5 = (f32[64,256]{1,0:T(8,128)S(1)}, f32[64,256]{1,0:T(8,128)S(1)}, u32[]{:S(2)}, u32[]{:S(2)}) collective-permute-start(f32[64,256]{1,0:T(8,128)S(1)} %sum.2.refs_0_), channel_id=1, source_target_pairs={{0,16},{2,18},{4,20},{6,22},{8,24},{10,26},{12,28},{14,30},{16,0},... | collective-permute-start | bytes 196616 | tf_op jit(solution)/shard_map/ppermute | solution.py:338
  32.7 5.8 %collective-permute-start.12 = (f32[64,256]{1,0:T(8,128)S(1)}, f32[64,256]{1,0:T(8,128)S(1)}, u32[]{:S(2)}, u32[]{:S(2)}) collective-permute-start(f32[64,256]{1,0:T(8,128)S(1)} %sum.3.refs_0_.whole_ref), channel_id=1, source_target_pairs={{0,12},{2,14},{4,8},{6,10},{8,4},{10,6},{12,0},{14,2},{16,28},{18,... | collective-permute-start | bytes 196616 | tf_op jit(solution)/shard_map/ppermute | solution.py:338
  33.3 5.9 %collective-permute-start.10 = (f32[64,256]{1,0:T(8,128)S(1)}, f32[64,256]{1,0:T(8,128)S(1)}, u32[]{:S(2)}, u32[]{:S(2)}) collective-permute-start(f32[64,256]{1,0:T(8,128)S(1)} %sum.3.refs_0_.whole_ref), channel_id=1, source_target_pairs={{0,8},{2,10},{4,12},{6,14},{8,0},{10,2},{12,4},{14,6},{16,24},{18,... | collective-permute-start | bytes 196616 | tf_op jit(solution)/shard_map/ppermute | solution.py:338
  34.9 4.4 %collective-permute-start.7 = (f32[64,256]{1,0:T(8,128)S(1)}, f32[64,256]{1,0:T(8,128)S(1)}, u32[]{:S(2)}, u32[]{:S(2)}) collective-permute-start(f32[64,256]{1,0:T(8,128)S(1)} %sum.3.refs_0_.whole_ref), channel_id=1, source_target_pairs={{0,4},{2,6},{4,0},{6,2},{8,12},{10,14},{12,8},{14,10},{16,20},{18,... | collective-permute-start | bytes 196616 | tf_op jit(solution)/shard_map/ppermute | solution.py:338
  36.3 3.9 %collective-permute-start.6 = (f32[64,256]{1,0:T(8,128)S(1)}, f32[64,256]{1,0:T(8,128)S(1)}, u32[]{:S(2)}, u32[]{:S(2)}) collective-permute-start(f32[64,256]{1,0:T(8,128)S(1)} %sum.3.refs_0_.whole_ref), channel_id=1, source_target_pairs={{0,2},{2,0},{4,6},{6,4},{8,10},{10,8},{12,14},{14,12},{16,18},{18,... | collective-permute-start | bytes 196616 | tf_op jit(solution)/shard_map/ppermute | solution.py:338
  38.6 1.6 %collective-permute-start.13 = (f32[64,256]{1,0:T(8,128)S(1)}, f32[64,256]{1,0:T(8,128)S(1)}, u32[]{:S(2)}, u32[]{:S(2)}) collective-permute-start(f32[64,256]{1,0:T(8,128)S(1)} %collective-permute-done.12.refs_3_), channel_id=1, source_target_pairs={{0,2},{2,0},{4,6},{6,4},{8,10},{10,8},{12,14},{14,12},{16,18},{18,... | collective-permute-start | bytes 196616 | tf_op jit(solution)/shard_map/ppermute | solution.py:338
  39.2 1.3 %collective-permute-start.11 = (f32[64,256]{1,0:T(8,128)S(1)}, f32[64,256]{1,0:T(8,128)S(1)}, u32[]{:S(2)}, u32[]{:S(2)}) collective-permute-start(f32[64,256]{1,0:T(8,128)S(1)} %collective-permute-done.10.refs_2_), channel_id=1, source_target_pairs={{0,2},{2,0},{4,6},{6,4},{8,10},{10,8},{12,14},{14,12},{16,18},{18,... | collective-permute-start | bytes 196616 | tf_op jit(solution)/shard_map/ppermute | solution.py:338
  39.3 1.3 %collective-permute-start.9 = (f32[64,256]{1,0:T(8,128)S(1)}, f32[64,256]{1,0:T(8,128)S(1)}, u32[]{:S(2)}, u32[]{:S(2)}) collective-permute-start(f32[64,256]{1,0:T(8,128)S(1)} %collective-permute-done.7.refs_1_), channel_id=1, source_target_pairs={{0,2},{2,0},{4,6},{6,4},{8,10},{10,8},{12,14},{14,12},{16,18},{18,... | collective-permute-start | bytes 196616 | tf_op jit(solution)/shard_map/ppermute | solution.py:338
  41.1 6.2 %collective-permute-start.14 = (f32[64,512]{1,0:T(8,128)S(1)}, f32[64,512]{1,0:T(8,128)S(1)}, u32[]{:S(2)}, u32[]{:S(2)}) collective-permute-start(f32[64,512]{1,0:T(8,128)S(1)} %product_second.1.refs_0_), channel_id=1, source_target_pairs={{0,1},{1,0},{2,3},{3,2},{4,5},{5,4},{6,7},{7,6},{8,9},{9,8},{10,11... | collective-permute-start | bytes 393224 | tf_op jit(solution)/shard_map/ppermute | solution.py:348
  42.6 4.6 %collective-permute-start.15 = (f32[8,512]{1,0:T(8,128)S(1)}, f32[8,512]{1,0:T(8,128)S(1)}, u32[]{:S(2)}, u32[]{:S(2)}) collective-permute-start(f32[8,512]{1,0:T(8,128)S(1)} %row_sums.1.refs_2_), channel_id=1, source_target_pairs={{0,1},{1,0},{2,3},{3,2},{4,5},{5,4},{6,7},{7,6},{8,9},{9,8},{10,11... | collective-permute-start | bytes 49160 | tf_op jit(solution)/shard_map/ppermute | solution.py:348
  47.7 1.4 %collective-permute-start.16 = (f32[72,512]{1,0:T(8,128)S(1)}, f32[72,512]{1,0:T(8,128)S(1)}, u32[]{:S(2)}, u32[]{:S(2)}) collective-permute-start(f32[72,512]{1,0:T(8,128)S(1)} %get-tuple-element.90), channel_id=1, source_target_pairs={{0,2},{2,0},{4,6},{6,4},{8,10},{10,8},{12,14},{14,12},{16,18},{18,... | collective-permute-start | bytes 442376 | tf_op jit(solution)/shard_map/ppermute | solution.py:338
  49.2 4.0 %collective-permute-start.17 = (f32[72,128]{1,0:T(8,128)S(1)}, f32[72,128]{1,0:T(8,128)S(1)}, u32[]{:S(2)}, u32[]{:S(2)}) collective-permute-start(f32[72,128]{1,0:T(8,128)S(1)} %get-tuple-element.93), channel_id=1, source_target_pairs={{0,4},{2,6},{4,0},{6,2},{8,12},{10,14},{12,8},{14,10},{16,20},{18,... | collective-permute-start | bytes 110600 | tf_op jit(solution)/shard_map/ppermute | solution.py:338
  50.3 4.0 %collective-permute-start.18 = (f32[72,128]{1,0:T(8,128)S(1)}, f32[72,128]{1,0:T(8,128)S(1)}, u32[]{:S(2)}, u32[]{:S(2)}) collective-permute-start(f32[72,128]{1,0:T(8,128)S(1)} %get-tuple-element.94), channel_id=1, source_target_pairs={{0,8},{2,10},{4,12},{6,14},{8,0},{10,2},{12,4},{14,6},{16,24},{18,... | collective-permute-start | bytes 110600 | tf_op jit(solution)/shard_map/ppermute | solution.py:338
  50.6 4.9 %collective-permute-start.19 = (f32[72,128]{1,0:T(8,128)S(1)}, f32[72,128]{1,0:T(8,128)S(1)}, u32[]{:S(2)}, u32[]{:S(2)}) collective-permute-start(f32[72,128]{1,0:T(8,128)S(1)} %get-tuple-element.95), channel_id=1, source_target_pairs={{0,12},{2,14},{4,8},{6,10},{8,4},{10,6},{12,0},{14,2},{16,28},{18,... | collective-permute-start | bytes 110600 | tf_op jit(solution)/shard_map/ppermute | solution.py:338
